TPU v7x, 128 devices: a whole 4x4x4 slice. The times are simulated.
128 devices in a mesh: wide: 16 (over z, x), narrow: 8 (over y, core).
Axes of the slice: x: 4, y: 4, z: 4, core: 2. Of those that a mesh axis runs over, the one named last changes fastest.
Arguments:
- load: float32 [3, 128, 128, 384], P(None, 'wide', 'narrow'), may hold values from -6 to 6
- density: float32 [128, 128, 384], P('wide', 'narrow'), may hold values from 0.55 to 1
Outputs:
- correction: float32 [3, 128, 128, 384], P(None, 'wide', 'narrow')
All inputs are finite; a program needn't handle non-finite values.
Results may differ from a plain program's by a relative error of at most 0.0001.
Values sent between devices are 32-bit elements; how exact they have to be, the bound alone decides.
No kernel may reach another device: no remote copies, remote signals or barrier semaphores. Data moves between devices by JAX's collectives and lax.ppermute only.
A program may use at most 128 MiB of HBM per device.

v0:
```python
import jax
import jax.numpy as jnp
from jax import lax
from jax.sharding import PartitionSpec as P

LEVELS = 4
SWEEPS = 2


damping = 0.5
mass_term = 0.02


def with_halo(block, sides, width):
    for axis, dim in sides:
        count = lax.axis_size(axis)
        forward = [(i, i + 1) for i in range(count - 1)]
        backward = [(target, source) for source, target in forward]
        low = lax.ppermute(
            lax.slice_in_dim(block, block.shape[dim] - width, None, axis=dim), axis, forward
        )
        high = lax.ppermute(lax.slice_in_dim(block, 0, width, axis=dim), axis, backward)
        block = jnp.concatenate([low, block, high], axis=dim)
    return block


def from_behind(value, axis, steps):
    count = lax.axis_size(axis)
    initial, last = (max(0, -steps), min(count, count - steps))
    return lax.ppermute(value, axis, [(source, source + steps) for source in range(initial, last)])


def pad_along_x(field):
    return jnp.pad(field, [(0, 0)] * (field.ndim - 1) + [(1, 1)])


def inner(padded, axis, step):
    count = padded.ndim
    index = [slice(None)] * (count - 3) + [slice(1, -1)] * 3
    extent = padded.shape[count - 3 + axis]
    index[count - 3 + axis] = slice(1 + step, extent - 1 + step)
    return padded[tuple(index)]


def coarsen_sum(field):
    shape = field.shape
    lead = shape[:-3]
    split = field.reshape(lead + (shape[-3] // 2, 2, shape[-2] // 2, 2, shape[-1] // 2, 2))
    return jnp.sum(split, axis=(-5, -3, -1))


def prolong(field):
    return jnp.repeat(jnp.repeat(jnp.repeat(field, 2, -3), 2, -2), 2, -1)


def moduli(dens):
    shear = dens * dens * dens
    bulk = shear * (0.5 + dens)
    return (shear, bulk)


def rims_moduli(pair):
    return pad_along_x(with_halo(pair, (("wide", 1), ("narrow", 2)), 1))


def rims_displacement(field):
    return pad_along_x(with_halo(field, (("wide", 1), ("narrow", 2)), 1))


def stress_upper(stress):
    top_z = from_behind(stress[:1], "wide", -1)
    top_y = from_behind(stress[:, :1], "narrow", -1)
    upper_z = jnp.concatenate([stress[1:], top_z], 0)
    upper_y = jnp.concatenate([stress[:, 1:], top_y], 1)
    upper_x = jnp.concatenate([stress[:, :, 1:], jnp.zeros_like(stress[:, :, :1])], 2)
    return (upper_z, upper_y, upper_x)


def level_coefficients(dens):
    shear, bulk = moduli(dens)
    pads = rims_moduli(jnp.stack([shear, bulk]))
    shear_pad = pads[0]
    bulk_pad = pads[1]
    plus = [0.5 * (shear + inner(shear_pad, d, 1)) for d in range(3)]
    minus = [0.5 * (shear + inner(shear_pad, d, -1)) for d in range(3)]
    total = mass_term + plus[0] + minus[0] + plus[1] + minus[1] + plus[2] + minus[2]
    diag = jnp.stack([total + bulk + inner(bulk_pad, c, 1) for c in range(3)])
    return (plus, minus, bulk, diag, bulk_pad)


def operate(field, coef):
    plus, minus, bulk, diag, bulk_pad = coef
    padded = rims_displacement(field)
    div = (
        field[0]
        - inner(padded[0], 0, -1)
        + (field[1] - inner(padded[1], 1, -1))
        + (field[2] - inner(padded[2], 2, -1))
    )
    stress = bulk * div
    upper = stress_upper(stress)
    grad = jnp.stack([stress - upper[c] for c in range(3)])
    lap = plus[0] * (field - inner(padded, 0, 1)) + minus[0] * (field - inner(padded, 0, -1))
    lap = lap + plus[1] * (field - inner(padded, 1, 1)) + minus[1] * (field - inner(padded, 1, -1))
    lap = lap + plus[2] * (field - inner(padded, 2, 1)) + minus[2] * (field - inner(padded, 2, -1))
    return mass_term * field + lap + grad


def smooth(rhs, coef, count):
    field = damping * rhs / coef[3]
    for sweep in range(count - 1):
        field = field + damping * (rhs - operate(field, coef)) / coef[3]
    return field


def shards(load, density):
    dens = [density]
    for level in range(1, LEVELS):
        dens.append(coarsen_sum(dens[-1]) * 0.125)
    rhs = load
    saved = []
    for level in range(LEVELS - 1):
        coef = level_coefficients(dens[level])
        field = smooth(rhs, coef, SWEEPS)
        resid = rhs - operate(field, coef)
        saved.append((field, rhs, coef))
        rhs = 0.5 * coarsen_sum(resid)
    coef = level_coefficients(dens[-1])
    field = smooth(rhs, coef, 2 * SWEEPS)
    for level in reversed(range(LEVELS - 1)):
        fine_field, fine_rhs, coef = saved[level]
        field = fine_field + prolong(field)
        for sweep in range(SWEEPS):
            field = field + damping * (fine_rhs - operate(field, coef)) / coef[3]
    return field


def solution(mesh):
    in_specs = (P(None, "wide", "narrow", None), P("wide", "narrow", None))
    out_specs = P(None, "wide", "narrow", None)
    return jax.shard_map(shards, mesh=mesh, in_specs=in_specs, out_specs=out_specs, check_vma=False)
```

profile of v0, /device:TPU:115, one launch (start us, length us, event | category | flops | bytes accessed | tf_op | source)
XLA Modules:
  0.0 534.2 jit_solution(1738574102054457721)
XLA Ops:
  6.3 14.3 %reshape.278 = f32[4,2,8,2,192,2]{5,4,3,2,1,0:T(8,128)} reshape(f32[8,16,384]{2,1,0:T(8,128)} %param.3) | data formatting | bytes 393216 | tf_op jit(solution)/shard_map/reshape | solution.py:48
  20.6 5.7 %reduce_sum.69 = f32[4,8,192]{2,1,0:T(8,128)S(1)} reduce(f32[4,2,8,2,192,2]{5,4,3,2,1,0:T(8,128)} %reshape.278, f32[]{:T(128)} %constant.6.clone.1), dimensions={1,3,5}, to_apply=%region_1.0 | reduce | flops 43008 | bytes 221188 | tf_op jit(solution)/shard_map/reduce_sum | solution.py:49
  40.0 5.1 collective-permute-start.4
  49.2 3.5 collective-permute-start.18
  62.1 5.5 %collective-permute-start.8 = (f32[1,16,384]{2,1,0:T(8,128)S(1)}, f32[1,16,384]{2,1,0:T(8,128)S(1)}, u32[]{:S(2)}, u32[]{:S(2)}) collective-permute-start(f32[1,16,384]{2,1,0:T(8,128)S(1)} %slice.1775), channel_id=1, source_target_pairs={{8,0},{16,8},{24,16},{32,24},{40,32},{48,40},{56,48},{64,56},{72,6... | collective-permute-start | bytes 73736 | tf_op jit(solution)/shard_map/ppermute | solution.py:30
  67.6 3.6 collective-permute-start.9
  74.4 5.5 %collective-permute-start.10 = (f32[3,1,16,384]{3,2,1,0:T(8,128)S(1)}, f32[3,1,16,384]{3,2,1,0:T(8,128)S(1)}, u32[]{:S(2)}, u32[]{:S(2)}) collective-permute-start(f32[3,1,16,384]{3,2,1,0:T(8,128)S(1)} %get-tuple-element.54), channel_id=1, source_target_pairs={{8,0},{16,8},{24,16},{32,24},{40,32},{48,40},{56,48},{64,56},{72,6... | collective-permute-start | bytes 221192 | tf_op jit(solution)/shard_map/ppermute | solution.py:22
  97.5 5.4 %collective-permute-start.14 = (f32[1,16,384]{2,1,0:T(8,128)S(1)}, f32[1,16,384]{2,1,0:T(8,128)S(1)}, u32[]{:S(2)}, u32[]{:S(2)}) collective-permute-start(f32[1,16,384]{2,1,0:T(8,128)S(1)} %slice.1793), channel_id=1, source_target_pairs={{8,0},{16,8},{24,16},{32,24},{40,32},{48,40},{56,48},{64,56},{72,6... | collective-permute-start | bytes 73736 | tf_op jit(solution)/shard_map/ppermute | solution.py:30
  109.6 39.3 %reshape.277 = f32[3,4,2,8,2,192,2]{6,5,4,3,2,1,0:T(8,128)} reshape(f32[3,8,16,384]{3,2,1,0:T(8,128)S(1)} %fusion.48) | data formatting | bytes 1179648 | tf_op jit(solution)/shard_map/reshape | solution.py:48
  148.8 13.6 %reduce_sum.68 = f32[3,4,8,192]{3,2,1,0:T(8,128)S(1)} reduce(f32[3,4,2,8,2,192,2]{6,5,4,3,2,1,0:T(8,128)} %reshape.277, f32[]{:T(128)} %constant.6.clone.1), dimensions={2,4,6}, to_apply=%region_0.0 | reduce | flops 129024 | bytes 663556 | tf_op jit(solution)/shard_map/reduce_sum | solution.py:49
  180.8 3.6 collective-permute-start.34
  193.4 5.7 %collective-permute-start.26 = (f32[3,1,8,192]{3,2,1,0:T(8,128)S(1)}, f32[3,1,8,192]{3,2,1,0:T(8,128)S(1)}, u32[]{:S(2)}, u32[]{:S(2)}) collective-permute-start(f32[3,1,8,192]{3,2,1,0:T(8,128)S(1)} %get-tuple-element.110), channel_id=1, source_target_pairs={{8,0},{16,8},{24,16},{32,24},{40,32},{48,40},{56,48},{64,56},{72,6... | collective-permute-start | bytes 55304 | tf_op jit(solution)/shard_map/ppermute | solution.py:22
  205.7 3.6 collective-permute-start.29
  210.6 4.5 collective-permute-start.30
  221.0 6.1 %reshape.279 = f32[3,2,2,4,2,96,2]{6,5,4,3,2,1,0:T(8,128)} reshape(f32[3,4,8,192]{3,2,1,0:T(8,128)S(1)} %fusion.160) | data formatting | bytes 147456 | tf_op jit(solution)/shard_map/reshape | solution.py:48
  243.0 5.6 %collective-permute-start.40 = (f32[1,4,96]{2,1,0:T(4,128)S(1)}, f32[1,4,96]{2,1,0:T(4,128)S(1)}, u32[]{:S(2)}, u32[]{:S(2)}) collective-permute-start(f32[1,4,96]{2,1,0:T(4,128)S(1)} %get-tuple-element.218), channel_id=1, source_target_pairs={{8,0},{16,8},{24,16},{32,24},{40,32},{48,40},{56,48},{64,56},{72,6... | collective-permute-start | bytes 4616 | tf_op jit(solution)/shard_map/ppermute | solution.py:30
  267.6 5.6 %collective-permute-start.49 = (f32[2,1,2,48]{3,2,1,0:T(2,128)S(1)}, f32[2,1,2,48]{3,2,1,0:T(2,128)S(1)}, u32[]{:S(2)}, u32[]{:S(2)}) collective-permute-start(f32[2,1,2,48]{3,2,1,0:T(2,128)S(1)} %pad_maximum_fusion.175), channel_id=1, source_target_pairs={{8,0},{16,8},{24,16},{32,24},{40,32},{48,40},{56,48},{64,56},{72,6... | collective-permute-start | bytes 2312 | tf_op jit(solution)/shard_map/ppermute | solution.py:22
  278.6 3.8 collective-permute-start.47
  284.4 3.6 collective-permute-start.50
  289.1 3.8 collective-permute-start.52
  297.2 4.2 collective-permute-start.54
  305.7 3.7 collective-permute-start.56
  328.0 5.7 %collective-permute-start.62 = (f32[1,2,48]{2,1,0:T(2,128)S(1)}, f32[1,2,48]{2,1,0:T(2,128)S(1)}, u32[]{:S(2)}, u32[]{:S(2)}) collective-permute-start(f32[1,2,48]{2,1,0:T(2,128)S(1)} %fusion.395), channel_id=1, source_target_pairs={{8,0},{16,8},{24,16},{32,24},{40,32},{48,40},{56,48},{64,56},{72,6... | collective-permute-start | bytes 1160 | tf_op jit(solution)/shard_map/ppermute | solution.py:30
  352.3 5.7 %collective-permute-start.68 = (f32[1,2,48]{2,1,0:T(2,128)S(1)}, f32[1,2,48]{2,1,0:T(2,128)S(1)}, u32[]{:S(2)}, u32[]{:S(2)}) collective-permute-start(f32[1,2,48]{2,1,0:T(2,128)S(1)} %fusion.392), channel_id=1, source_target_pairs={{8,0},{16,8},{24,16},{32,24},{40,32},{48,40},{56,48},{64,56},{72,6... | collective-permute-start | bytes 1160 | tf_op jit(solution)/shard_map/ppermute | solution.py:30
  376.9 5.7 %collective-permute-start.74 = (f32[1,4,96]{2,1,0:T(4,128)S(1)}, f32[1,4,96]{2,1,0:T(4,128)S(1)}, u32[]{:S(2)}, u32[]{:S(2)}) collective-permute-start(f32[1,4,96]{2,1,0:T(4,128)S(1)} %get-tuple-element.206), channel_id=1, source_target_pairs={{8,0},{16,8},{24,16},{32,24},{40,32},{48,40},{56,48},{64,56},{72,6... | collective-permute-start | bytes 4616 | tf_op jit(solution)/shard_map/ppermute | solution.py:30
  401.3 5.6 %collective-permute-start.80 = (f32[1,4,96]{2,1,0:T(4,128)S(1)}, f32[1,4,96]{2,1,0:T(4,128)S(1)}, u32[]{:S(2)}, u32[]{:S(2)}) collective-permute-start(f32[1,4,96]{2,1,0:T(4,128)S(1)} %get-tuple-element.201), channel_id=1, source_target_pairs={{8,0},{16,8},{24,16},{32,24},{40,32},{48,40},{56,48},{64,56},{72,6... | collective-permute-start | bytes 4616 | tf_op jit(solution)/shard_map/ppermute | solution.py:30
  431.1 5.7 %collective-permute-start.86 = (f32[1,8,192]{2,1,0:T(8,128)S(1)}, f32[1,8,192]{2,1,0:T(8,128)S(1)}, u32[]{:S(2)}, u32[]{:S(2)}) collective-permute-start(f32[1,8,192]{2,1,0:T(8,128)S(1)} %slice.1995), channel_id=1, source_target_pairs={{8,0},{16,8},{24,16},{32,24},{40,32},{48,40},{56,48},{64,56},{72,6... | collective-permute-start | bytes 18440 | tf_op jit(solution)/shard_map/ppermute | solution.py:30
  456.2 5.7 %collective-permute-start.92 = (f32[1,8,192]{2,1,0:T(8,128)S(1)}, f32[1,8,192]{2,1,0:T(8,128)S(1)}, u32[]{:S(2)}, u32[]{:S(2)}) collective-permute-start(f32[1,8,192]{2,1,0:T(8,128)S(1)} %slice.2013), channel_id=1, source_target_pairs={{8,0},{16,8},{24,16},{32,24},{40,32},{48,40},{56,48},{64,56},{72,6... | collective-permute-start | bytes 18440 | tf_op jit(solution)/shard_map/ppermute | solution.py:30
  470.3 4.1 broadcast_in_dim.32
  474.4 3.7 copy.667
  493.5 5.5 %collective-permute-start.98 = (f32[1,16,384]{2,1,0:T(8,128)S(1)}, f32[1,16,384]{2,1,0:T(8,128)S(1)}, u32[]{:S(2)}, u32[]{:S(2)}) collective-permute-start(f32[1,16,384]{2,1,0:T(8,128)S(1)} %slice.2031), channel_id=1, source_target_pairs={{8,0},{16,8},{24,16},{32,24},{40,32},{48,40},{56,48},{64,56},{72,6... | collective-permute-start | bytes 73736 | tf_op jit(solution)/shard_map/ppermute | solution.py:30
  521.2 5.3 collective-permute-start.104
  (503 shorter events, 323.2 us)
Async XLA Ops:
  1.0 25.4 %collective-permute-start.1 = (f32[2,1,16,384]{3,2,1,0:T(8,128)S(1)}, f32[2,1,16,384]{3,2,1,0:T(8,128)S(1)}, u32[]{:S(2)}, u32[]{:S(2)}) collective-permute-start(f32[2,1,16,384]{3,2,1,0:T(8,128)S(1)} %get-tuple-element.60), channel_id=1, source_target_pairs={{8,0},{16,8},{24,16},{32,24},{40,32},{48,40},{56,48},{64,56},{72,6... | collective-permute-start | bytes 147464 | tf_op jit(solution)/shard_map/ppermute | solution.py:22
  3.1 23.2 %collective-permute-start = (f32[2,1,16,384]{3,2,1,0:T(8,128)S(1)}, f32[2,1,16,384]{3,2,1,0:T(8,128)S(1)}, u32[]{:S(2)}, u32[]{:S(2)}) collective-permute-start(f32[2,1,16,384]{3,2,1,0:T(8,128)S(1)} %get-tuple-element.59), channel_id=1, source_target_pairs={{0,8},{8,16},{16,24},{24,32},{32,40},{40,48},{48,56},{56,64},{64,7... | collective-permute-start | bytes 147464 | tf_op jit(solution)/shard_map/ppermute | solution.py:19
  26.5 11.3 %collective-permute-start.3 = (f32[2,10,1,384]{3,0,2,1:T(2,128)S(1)}, f32[2,10,1,384]{3,0,2,1:T(2,128)S(1)}, u32[]{:S(2)}, u32[]{:S(2)}) collective-permute-start(f32[2,10,1,384]{3,0,2,1:T(2,128)S(1)} %copy.673), channel_id=1, source_target_pairs={{1,0},{2,1},{3,2},{4,3},{5,4},{6,5},{7,6},{9,8},{10,9},{11,10},{12... | collective-permute-start | bytes 92168 | tf_op jit(solution)/shard_map/ppermute | solution.py:22
  32.5 14.6 %collective-permute-start.17 = (f32[2,1,8,192]{3,2,1,0:T(8,128)S(1)}, f32[2,1,8,192]{3,2,1,0:T(8,128)S(1)}, u32[]{:S(2)}, u32[]{:S(2)}) collective-permute-start(f32[2,1,8,192]{3,2,1,0:T(8,128)S(1)} %get-tuple-element.116), channel_id=1, source_target_pairs={{8,0},{16,8},{24,16},{32,24},{40,32},{48,40},{56,48},{64,56},{72,6... | collective-permute-start | bytes 36872 | tf_op jit(solution)/shard_map/ppermute | solution.py:22
  35.2 11.8 %collective-permute-start.16 = (f32[2,1,8,192]{3,2,1,0:T(8,128)S(1)}, f32[2,1,8,192]{3,2,1,0:T(8,128)S(1)}, u32[]{:S(2)}, u32[]{:S(2)}) collective-permute-start(f32[2,1,8,192]{3,2,1,0:T(8,128)S(1)} %get-tuple-element.115), channel_id=1, source_target_pairs={{0,8},{8,16},{16,24},{24,32},{32,40},{40,48},{48,56},{56,64},{64,7... | collective-permute-start | bytes 36872 | tf_op jit(solution)/shard_map/ppermute | solution.py:19
  40.0 13.6 %collective-permute-start.4 = (f32[3,1,16,384]{3,2,1,0:T(8,128)S(1)}, f32[3,1,16,384]{3,2,1,0:T(8,128)S(1)}, u32[]{:S(2)}, u32[]{:S(2)}) collective-permute-start(f32[3,1,16,384]{3,2,1,0:T(8,128)S(1)} %get-tuple-element.56), channel_id=1, source_target_pairs={{8,0},{16,8},{24,16},{32,24},{40,32},{48,40},{56,48},{64,56},{72,6... | collective-permute-start | bytes 221192 | tf_op jit(solution)/shard_map/ppermute | solution.py:22
  62.1 11.4 %collective-permute-start.8 = (f32[1,16,384]{2,1,0:T(8,128)S(1)}, f32[1,16,384]{2,1,0:T(8,128)S(1)}, u32[]{:S(2)}, u32[]{:S(2)}) collective-permute-start(f32[1,16,384]{2,1,0:T(8,128)S(1)} %slice.1775), channel_id=1, source_target_pairs={{8,0},{16,8},{24,16},{32,24},{40,32},{48,40},{56,48},{64,56},{72,6... | collective-permute-start | bytes 73736 | tf_op jit(solution)/shard_map/ppermute | solution.py:30
  86.5 8.8 %collective-permute-start.12 = (f32[3,10,1,384]{3,2,1,0:T(1,128)}, f32[3,10,1,384]{3,2,1,0:T(1,128)}, u32[]{:S(2)}, u32[]{:S(2)}) collective-permute-start(f32[3,10,1,384]{3,2,1,0:T(1,128)} %get-tuple-element.44), channel_id=1, source_target_pairs={{1,0},{2,1},{3,2},{4,3},{5,4},{6,5},{7,6},{9,8},{10,9},{11,10},{12... | collective-permute-start | bytes 138248 | tf_op jit(solution)/shard_map/ppermute | solution.py:22
  97.5 10.5 %collective-permute-start.14 = (f32[1,16,384]{2,1,0:T(8,128)S(1)}, f32[1,16,384]{2,1,0:T(8,128)S(1)}, u32[]{:S(2)}, u32[]{:S(2)}) collective-permute-start(f32[1,16,384]{2,1,0:T(8,128)S(1)} %slice.1793), channel_id=1, source_target_pairs={{8,0},{16,8},{24,16},{32,24},{40,32},{48,40},{56,48},{64,56},{72,6... | collective-permute-start | bytes 73736 | tf_op jit(solution)/shard_map/ppermute | solution.py:30
  162.6 10.6 %collective-permute-start.20 = (f32[3,1,8,192]{3,2,1,0:T(8,128)S(1)}, f32[3,1,8,192]{3,2,1,0:T(8,128)S(1)}, u32[]{:S(2)}, u32[]{:S(2)}) collective-permute-start(f32[3,1,8,192]{3,2,1,0:T(8,128)S(1)} %get-tuple-element.112), channel_id=1, source_target_pairs={{8,0},{16,8},{24,16},{32,24},{40,32},{48,40},{56,48},{64,56},{72,6... | collective-permute-start | bytes 55304 | tf_op jit(solution)/shard_map/ppermute | solution.py:22
  164.5 8.7 %collective-permute-start.21 = (f32[3,1,8,192]{3,2,1,0:T(8,128)S(1)}, f32[3,1,8,192]{3,2,1,0:T(8,128)S(1)}, u32[]{:S(2)}, u32[]{:S(2)}) collective-permute-start(f32[3,1,8,192]{3,2,1,0:T(8,128)S(1)} %get-tuple-element.111), channel_id=1, source_target_pairs={{0,8},{8,16},{16,24},{24,32},{32,40},{40,48},{48,56},{56,64},{64,7... | collective-permute-start | bytes 55304 | tf_op jit(solution)/shard_map/ppermute | solution.py:19
  167.9 10.9 %collective-permute-start.33 = (f32[2,1,4,96]{3,2,1,0:T(4,128)S(1)}, f32[2,1,4,96]{3,2,1,0:T(4,128)S(1)}, u32[]{:S(2)}, u32[]{:S(2)}) collective-permute-start(f32[2,1,4,96]{3,2,1,0:T(4,128)S(1)} %get-tuple-element.184), channel_id=1, source_target_pairs={{8,0},{16,8},{24,16},{32,24},{40,32},{48,40},{56,48},{64,56},{72,6... | collective-permute-start | bytes 9224 | tf_op jit(solution)/shard_map/ppermute | solution.py:22
  169.8 9.0 %collective-permute-start.32 = (f32[2,1,4,96]{3,2,1,0:T(4,128)S(1)}, f32[2,1,4,96]{3,2,1,0:T(4,128)S(1)}, u32[]{:S(2)}, u32[]{:S(2)}) collective-permute-start(f32[2,1,4,96]{3,2,1,0:T(4,128)S(1)} %get-tuple-element.183), channel_id=1, source_target_pairs={{0,8},{8,16},{16,24},{24,32},{32,40},{40,48},{48,56},{56,64},{64,7... | collective-permute-start | bytes 9224 | tf_op jit(solution)/shard_map/ppermute | solution.py:19
  173.2 11.2 %collective-permute-start.22 = (f32[3,6,1,192]{3,2,1,0:T(1,128)S(1)}, f32[3,6,1,192]{3,2,1,0:T(1,128)S(1)}, u32[]{:S(2)}, u32[]{:S(2)}) collective-permute-start(f32[3,6,1,192]{3,2,1,0:T(1,128)S(1)} %get-tuple-element.96), channel_id=1, source_target_pairs={{1,0},{2,1},{3,2},{4,3},{5,4},{6,5},{7,6},{9,8},{10,9},{11,10},{12... | collective-permute-start | bytes 41480 | tf_op jit(solution)/shard_map/ppermute | solution.py:22
  175.4 9.0 %collective-permute-start.23 = (f32[3,6,1,192]{3,2,1,0:T(1,128)S(1)}, f32[3,6,1,192]{3,2,1,0:T(1,128)S(1)}, u32[]{:S(2)}, u32[]{:S(2)}) collective-permute-start(f32[3,6,1,192]{3,2,1,0:T(1,128)S(1)} %get-tuple-element.95), channel_id=1, source_target_pairs={{0,1},{1,2},{2,3},{3,4},{4,5},{5,6},{6,7},{8,9},{9,10},{10,11},{11... | collective-permute-start | bytes 41480 | tf_op jit(solution)/shard_map/ppermute | solution.py:19
  178.8 11.3 %collective-permute-start.35 = (f32[2,4,1,96]{3,2,1,0:T(1,128)S(1)}, f32[2,4,1,96]{3,2,1,0:T(1,128)S(1)}, u32[]{:S(2)}, u32[]{:S(2)}) collective-permute-start(f32[2,4,1,96]{3,2,1,0:T(1,128)S(1)} %get-tuple-element.166), channel_id=1, source_target_pairs={{1,0},{2,1},{3,2},{4,3},{5,4},{6,5},{7,6},{9,8},{10,9},{11,10},{12... | collective-permute-start | bytes 9224 | tf_op jit(solution)/shard_map/ppermute | solution.py:22
  180.8 9.4 %collective-permute-start.34 = (f32[2,4,1,96]{3,2,1,0:T(1,128)S(1)}, f32[2,4,1,96]{3,2,1,0:T(1,128)S(1)}, u32[]{:S(2)}, u32[]{:S(2)}) collective-permute-start(f32[2,4,1,96]{3,2,1,0:T(1,128)S(1)} %get-tuple-element.165), channel_id=1, source_target_pairs={{0,1},{1,2},{2,3},{3,4},{4,5},{5,6},{6,7},{8,9},{9,10},{10,11},{11... | collective-permute-start | bytes 9224 | tf_op jit(solution)/shard_map/ppermute | solution.py:19
  210.6 10.3 %collective-permute-start.30 = (f32[1,8,192]{2,1,0:T(8,128)S(1)}, f32[1,8,192]{2,1,0:T(8,128)S(1)}, u32[]{:S(2)}, u32[]{:S(2)}) collective-permute-start(f32[1,8,192]{2,1,0:T(8,128)S(1)} %slice.1840), channel_id=1, source_target_pairs={{8,0},{16,8},{24,16},{32,24},{40,32},{48,40},{56,48},{64,56},{72,6... | collective-permute-start | bytes 18440 | tf_op jit(solution)/shard_map/ppermute | solution.py:30
  243.0 11.4 %collective-permute-start.40 = (f32[1,4,96]{2,1,0:T(4,128)S(1)}, f32[1,4,96]{2,1,0:T(4,128)S(1)}, u32[]{:S(2)}, u32[]{:S(2)}) collective-permute-start(f32[1,4,96]{2,1,0:T(4,128)S(1)} %get-tuple-element.218), channel_id=1, source_target_pairs={{8,0},{16,8},{24,16},{32,24},{40,32},{48,40},{56,48},{64,56},{72,6... | collective-permute-start | bytes 4616 | tf_op jit(solution)/shard_map/ppermute | solution.py:30
  267.6 14.8 %collective-permute-start.49 = (f32[2,1,2,48]{3,2,1,0:T(2,128)S(1)}, f32[2,1,2,48]{3,2,1,0:T(2,128)S(1)}, u32[]{:S(2)}, u32[]{:S(2)}) collective-permute-start(f32[2,1,2,48]{3,2,1,0:T(2,128)S(1)} %pad_maximum_fusion.175), channel_id=1, source_target_pairs={{8,0},{16,8},{24,16},{32,24},{40,32},{48,40},{56,48},{64,56},{72,6... | collective-permute-start | bytes 2312 | tf_op jit(solution)/shard_map/ppermute | solution.py:22
  273.3 9.2 %collective-permute-start.48 = (f32[2,1,2,48]{3,2,1,0:T(2,128)S(1)}, f32[2,1,2,48]{3,2,1,0:T(2,128)S(1)}, u32[]{:S(2)}, u32[]{:S(2)}) collective-permute-start(f32[2,1,2,48]{3,2,1,0:T(2,128)S(1)} %pad_maximum_fusion.175), channel_id=1, source_target_pairs={{0,8},{8,16},{16,24},{24,32},{32,40},{40,48},{48,56},{56,64},{64,7... | collective-permute-start | bytes 2312 | tf_op jit(solution)/shard_map/ppermute | solution.py:19
  275.3 12.8 %collective-permute-start.46 = (f32[1,4,96]{2,1,0:T(4,128)S(1)}, f32[1,4,96]{2,1,0:T(4,128)S(1)}, u32[]{:S(2)}, u32[]{:S(2)}) collective-permute-start(f32[1,4,96]{2,1,0:T(4,128)S(1)} %get-tuple-element.213), channel_id=1, source_target_pairs={{8,0},{16,8},{24,16},{32,24},{40,32},{48,40},{56,48},{64,56},{72,6... | collective-permute-start | bytes 4616 | tf_op jit(solution)/shard_map/ppermute | solution.py:30
  278.6 9.4 %collective-permute-start.47 = (f32[2,1,96]{2,1,0:T(1,128)S(1)}, f32[2,1,96]{2,1,0:T(1,128)S(1)}, u32[]{:S(2)}, u32[]{:S(2)}) collective-permute-start(f32[2,1,96]{2,1,0:T(1,128)S(1)} %slice.1891), channel_id=1, source_target_pairs={{1,0},{2,1},{3,2},{4,3},{5,4},{6,5},{7,6},{9,8},{10,9},{11,10},{12... | collective-permute-start | bytes 2312 | tf_op jit(solution)/shard_map/ppermute | solution.py:30
  305.7 9.4 %collective-permute-start.56 = (f32[1,2,48]{2,1,0:T(2,128)S(1)}, f32[1,2,48]{2,1,0:T(2,128)S(1)}, u32[]{:S(2)}, u32[]{:S(2)}) collective-permute-start(f32[1,2,48]{2,1,0:T(2,128)S(1)} %fusion.398), channel_id=1, source_target_pairs={{8,0},{16,8},{24,16},{32,24},{40,32},{48,40},{56,48},{64,56},{72,6... | collective-permute-start | bytes 1160 | tf_op jit(solution)/shard_map/ppermute | solution.py:30
  328.0 11.4 %collective-permute-start.62 = (f32[1,2,48]{2,1,0:T(2,128)S(1)}, f32[1,2,48]{2,1,0:T(2,128)S(1)}, u32[]{:S(2)}, u32[]{:S(2)}) collective-permute-start(f32[1,2,48]{2,1,0:T(2,128)S(1)} %fusion.395), channel_id=1, source_target_pairs={{8,0},{16,8},{24,16},{32,24},{40,32},{48,40},{56,48},{64,56},{72,6... | collective-permute-start | bytes 1160 | tf_op jit(solution)/shard_map/ppermute | solution.py:30
  352.3 11.4 %collective-permute-start.68 = (f32[1,2,48]{2,1,0:T(2,128)S(1)}, f32[1,2,48]{2,1,0:T(2,128)S(1)}, u32[]{:S(2)}, u32[]{:S(2)}) collective-permute-start(f32[1,2,48]{2,1,0:T(2,128)S(1)} %fusion.392), channel_id=1, source_target_pairs={{8,0},{16,8},{24,16},{32,24},{40,32},{48,40},{56,48},{64,56},{72,6... | collective-permute-start | bytes 1160 | tf_op jit(solution)/shard_map/ppermute | solution.py:30
  376.9 11.4 %collective-permute-start.74 = (f32[1,4,96]{2,1,0:T(4,128)S(1)}, f32[1,4,96]{2,1,0:T(4,128)S(1)}, u32[]{:S(2)}, u32[]{:S(2)}) collective-permute-start(f32[1,4,96]{2,1,0:T(4,128)S(1)} %get-tuple-element.206), channel_id=1, source_target_pairs={{8,0},{16,8},{24,16},{32,24},{40,32},{48,40},{56,48},{64,56},{72,6... | collective-permute-start | bytes 4616 | tf_op jit(solution)/shard_map/ppermute | solution.py:30
  401.3 11.4 %collective-permute-start.80 = (f32[1,4,96]{2,1,0:T(4,128)S(1)}, f32[1,4,96]{2,1,0:T(4,128)S(1)}, u32[]{:S(2)}, u32[]{:S(2)}) collective-permute-start(f32[1,4,96]{2,1,0:T(4,128)S(1)} %get-tuple-element.201), channel_id=1, source_target_pairs={{8,0},{16,8},{24,16},{32,24},{40,32},{48,40},{56,48},{64,56},{72,6... | collective-permute-start | bytes 4616 | tf_op jit(solution)/shard_map/ppermute | solution.py:30
  431.1 11.4 %collective-permute-start.86 = (f32[1,8,192]{2,1,0:T(8,128)S(1)}, f32[1,8,192]{2,1,0:T(8,128)S(1)}, u32[]{:S(2)}, u32[]{:S(2)}) collective-permute-start(f32[1,8,192]{2,1,0:T(8,128)S(1)} %slice.1995), channel_id=1, source_target_pairs={{8,0},{16,8},{24,16},{32,24},{40,32},{48,40},{56,48},{64,56},{72,6... | collective-permute-start | bytes 18440 | tf_op jit(solution)/shard_map/ppermute | solution.py:30
  456.2 11.5 %collective-permute-start.92 = (f32[1,8,192]{2,1,0:T(8,128)S(1)}, f32[1,8,192]{2,1,0:T(8,128)S(1)}, u32[]{:S(2)}, u32[]{:S(2)}) collective-permute-start(f32[1,8,192]{2,1,0:T(8,128)S(1)} %slice.2013), channel_id=1, source_target_pairs={{8,0},{16,8},{24,16},{32,24},{40,32},{48,40},{56,48},{64,56},{72,6... | collective-permute-start | bytes 18440 | tf_op jit(solution)/shard_map/ppermute | solution.py:30
  493.5 11.4 %collective-permute-start.98 = (f32[1,16,384]{2,1,0:T(8,128)S(1)}, f32[1,16,384]{2,1,0:T(8,128)S(1)}, u32[]{:S(2)}, u32[]{:S(2)}) collective-permute-start(f32[1,16,384]{2,1,0:T(8,128)S(1)} %slice.2031), channel_id=1, source_target_pairs={{8,0},{16,8},{24,16},{32,24},{40,32},{48,40},{56,48},{64,56},{72,6... | collective-permute-start | bytes 73736 | tf_op jit(solution)/shard_map/ppermute | solution.py:30
  521.2 11.3 %collective-permute-start.104 = (f32[1,16,384]{2,1,0:T(8,128)S(1)}, f32[1,16,384]{2,1,0:T(8,128)S(1)}, u32[]{:S(2)}, u32[]{:S(2)}) collective-permute-start(f32[1,16,384]{2,1,0:T(8,128)S(1)} %slice.2049), channel_id=1, source_target_pairs={{8,0},{16,8},{24,16},{32,24},{40,32},{48,40},{56,48},{64,56},{72,6... | collective-permute-start | bytes 73736 | tf_op jit(solution)/shard_map/ppermute | solution.py:30
  (112 other events, 1197.7 us)
where the time goes:
time: 538 us; the launch traced here: 534 us
  starting transfers between devices  340 us (63%)
  local copies, waits for them, and re-layouts  81.1 us (15%)
  waiting for transfers between devices  66.8 us (12%)
  other arithmetic  43.4 us (8%)
    ppermute x30, starting transfers between devices, from_behind(): lax.ppermute(value, axis, [(source, source + steps) for source in range(i...  122 us
    ppermute x38, starting transfers between devices, with_halo(): lax.ppermute(lax.slice_in_dim(block, block.shape[dim] - width, None, axis...  119 us
    ppermute x38, starting transfers between devices, with_halo(): lax.ppermute(lax.slice_in_dim(block, 0, width, axis=dim), axis, backward)  99.1 us
    reshape x3, local copies, waits for them, and re-layouts, coarsen_sum(): field.reshape(lead + (shape[-3] // 2, 2, shape[-2] // 2, 2, shape[-1] //...  59.7 us
    ppermute x30, waiting for transfers between devices, from_behind(): lax.ppermute(value, axis, [(source, source + steps) for source in range(i...  34.8 us
    ppermute x38, waiting for transfers between devices, with_halo(): lax.ppermute(lax.slice_in_dim(block, block.shape[dim] - width, None, axis...  31.9 us
    reduce_sum x8, other arithmetic, coarsen_sum(): return jnp.sum(split, axis=(-5, -3, -1))  22.7 us
  transfers between devices with their start and end apart: 106, of which 42 were waited for; matrix products, arithmetic and copies ran while one was open for 6% of the time, Pallas kernels for 0%

commit v1 on v0

v1 whole, which is shorter than its diff:
```python
import functools

import jax
import jax.numpy as jnp
from jax import lax
from jax.experimental import pallas as pl
from jax.experimental.pallas import tpu as pltpu
from jax.sharding import Mesh, PartitionSpec as P

DAMPING = 0.5
MASS = 0.02
NARROW = ("y", "core")
F32 = jnp.float32
BF16 = jnp.bfloat16


def cyclic(count, step):
    return [(i, (i + step) % count) for i in range(count)]


def after(v, axis):
    return pltpu.roll(v, v.shape[axis] - 1, axis)


def before(v, axis):
    return pltpu.roll(v, 1, axis)


def times01(v, matrix):
    high = v.astype(BF16)
    rest = v - high.astype(F32)
    mid = rest.astype(BF16)
    low = (rest - mid.astype(F32)).astype(BF16)
    out = jnp.dot(high, matrix, preferred_element_type=F32)
    out = out + jnp.dot(mid, matrix, preferred_element_type=F32)
    return out + jnp.dot(low, matrix, preferred_element_type=F32)


def pair_sum_matrix(fine, coarse, factor):
    i = lax.broadcasted_iota(jnp.int32, (fine, coarse), 0)
    j = lax.broadcasted_iota(jnp.int32, (fine, coarse), 1)
    return jnp.where((i >> 1) == j, factor, 0.0).astype(BF16)


def copy_matrix(coarse, fine):
    j = lax.broadcasted_iota(jnp.int32, (coarse, fine), 0)
    i = lax.broadcasted_iota(jnp.int32, (coarse, fine), 1)
    return jnp.where((i >> 1) == j, 1.0, 0.0).astype(BF16)


class Level:
    def __init__(self, rows, lanes, wrap_x, wrap_y, gx, gy, gz, m, w, ms, base):
        self.rows, self.lanes = rows, lanes
        self.wrap_x, self.wrap_y = wrap_x, wrap_y
        self.gx, self.gy, self.gz, self.m, self.w, self.ms = gx, gy, gz, m, w, ms
        self.base = base

    def masks(self):
        row = lax.broadcasted_iota(jnp.int32, (self.rows, self.lanes), 0)
        lane = lax.broadcasted_iota(jnp.int32, (self.rows, self.lanes), 1)
        return (row == 0, row == self.rows - 1, lane == 0, lane == self.lanes - 1)


def after_in(v, axis, level, masks):
    r = after(v, axis)
    if axis == 0 and level.wrap_y:
        r = jnp.where(masks[1], 0.0, r)
    if axis == 1 and level.wrap_x:
        r = jnp.where(masks[3], 0.0, r)
    return r


def before_in(v, axis, level, masks):
    r = before(v, axis)
    if axis == 0 and level.wrap_y:
        r = jnp.where(masks[0], 0.0, r)
    if axis == 1 and level.wrap_x:
        r = jnp.where(masks[2], 0.0, r)
    return r


def coefficients(level, rho, lo, hi):
    masks = level.masks()

    def shear(z):
        d = rho(z)
        return d * d * d

    def plane(z, _):
        zb = z + level.base
        d = rho(z)
        dn = rho(z + 1)
        g = d * d * d
        gn = dn * dn * dn
        gp = shear(z - 1)
        m = g * (0.5 + d)
        mn = gn * (0.5 + dn)
        gx = 0.5 * (g + after(g, 1))
        gy = 0.5 * (g + after(g, 0))
        gz = 0.5 * (g + gn)
        total = MASS + gz + 0.5 * (g + gp)
        extra = None
        if level.wrap_x:
            gx = jnp.where(masks[3], 0.0, gx)
            extra = jnp.where(masks[2] | masks[3], 0.5 * g, 0.0)
        if level.wrap_y:
            gy = jnp.where(masks[1], 0.0, gy)
            more = jnp.where(masks[0] | masks[1], 0.5 * g, 0.0)
            extra = more if extra is None else extra + more
        if extra is not None:
            level.ms[zb] = MASS + extra
            total = total + extra
        total = total + (gx + before(gx, 1)) + (gy + before(gy, 0)) + m
        inside = d > 0.0
        level.gx[zb] = gx
        level.gy[zb] = gy
        level.gz[zb] = gz
        level.m[zb] = m
        level.w[0, zb] = jnp.where(inside, DAMPING / (total + mn), 0.0)
        level.w[1, zb] = jnp.where(inside, DAMPING / (total + after_in(m, 0, level, masks)), 0.0)
        level.w[2, zb] = jnp.where(inside, DAMPING / (total + after_in(m, 1, level, masks)), 0.0)
        return 0

    g0 = shear(lo - 1)
    level.gz[lo - 1 + level.base] = 0.5 * (g0 + shear(lo))
    dh = rho(hi)
    level.m[hi + level.base] = dh * dh * dh * (0.5 + dh)
    lax.fori_loop(lo, hi, plane, 0)


def operate(level, u, lo, hi, s_ref, f_ref, emit):
    masks = level.masks()

    def stress(z):
        uz, uy, ux = u(0, z), u(1, z), u(2, z)
        div = (uz - u(0, z - 1)) + (uy - before_in(uy, 0, level, masks))
        div = div + (ux - before_in(ux, 1, level, masks))
        return level.m[z + level.base] * div

    s_ref[...] = stress(lo)
    gz0 = level.gz[lo - 1 + level.base]
    for c in range(3):
        f_ref[c] = gz0 * (u(c, lo - 1) - u(c, lo))

    def plane(z, _):
        zb = z + level.base
        s = s_ref[...]
        sn = stress(z + 1)
        s_ref[...] = sn
        gx, gy, gz = level.gx[zb], level.gy[zb], level.gz[zb]
        for c in range(3):
            v = u(c, z)
            fz = gz * (v - u(c, z + 1))
            fx = gx * (v - after(v, 1))
            fy = gy * (v - after(v, 0))
            if c == 0:
                grad = s - sn
            elif c == 1:
                grad = s - after_in(s, 0, level, masks)
            else:
                grad = s - after_in(s, 1, level, masks)
            mass = MASS if level.ms is None else level.ms[zb]
            a = mass * v + (fz - f_ref[c]) + (fx - before(fx, 1)) + (fy - before(fy, 0)) + grad
            f_ref[c] = fz
            emit(z, c, v, a)
        return 0

    lax.fori_loop(lo, hi, plane, 0)


def compact_rows(scratch, v):
    parts = []
    rows = v.shape[0]
    for k in range(v.shape[1] // 128):
        ref = scratch.at[k]
        ref[pl.ds(0, rows), :] = v[:, 128 * k : 128 * (k + 1)]
        parts.append(
            ref[pl.ds(0, rows // 2, stride=2), :] + ref[pl.ds(1, rows // 2, stride=2), :]
        )
    return parts[0] if len(parts) == 1 else jnp.concatenate(parts, axis=1)


def copy_rows(scratch, v):
    rows = v.shape[0]
    for k in range(v.shape[1] // 128):
        ref = scratch.at[k]
        part = v[:, 128 * k : 128 * (k + 1)]
        ref[pl.ds(0, rows, stride=2), :] = part
        ref[pl.ds(1, rows, stride=2), :] = part


def cell_mask(rows, own, high, low, n, last):
    row = lax.broadcasted_iota(jnp.int32, (rows, 128), 0)
    bad_high = (row >= own) & (row < own + high) & (n == last)
    bad_low = (row >= rows - low) & (n == 0)
    return jnp.where(bad_high | bad_low, 0.0, 1.0)


def down0(idx, x1, lo, hi, b, gx, gy, gz, m, w, ms, ep, l1, rho, e1, rz, s_ref, f_ref, pack):
    wide, narrow = idx[0], idx[1]
    rowmask = jnp.concatenate([cell_mask(24, 16, 4, 4, narrow, 7)] * 3, axis=1)
    below = jnp.where(wide == 0, 0.0, 1.0) * rowmask
    above = jnp.where(wide == 15, 0.0, 1.0) * rowmask
    for z in range(4):
        rho[z] = lo[9 + z] * below
        rho[12 + z] = hi[9 + z] * above
    for z in range(8):
        rho[4 + z] = x1[3, z] * rowmask
    for c in range(3):
        for z in range(3):
            b[c, 1 + z] = lo[3 * c + z]
            b[c, 12 + z] = hi[3 * c + z]
        for z in range(8):
            b[c, 4 + z] = x1[c, z]
    level = Level(24, 384, True, False, gx, gy, gz, m, w, ms, 0)
    coefficients(level, lambda z: rho[z], 1, 15)

    def first(z, _):
        for c in range(3):
            e1[c, z] = w[c, z] * b[c, z]
        return 0

    lax.fori_loop(1, 15, first, 0)

    def sweep(z, c, v, a):
        ep[c, z] = v + w[c, z] * (b[c, z] - a)

    operate(level, lambda c, z: e1[c, z], 2, 14, s_ref, f_ref, sweep)
    rz[...] = jnp.zeros_like(rz)

    def residual(z, c, v, a):
        r = b[c, z] - a
        k = (z >> 1) - 2
        rz[c, k] = rz[c, k] + r[:16]

    operate(level, lambda c, z: ep[c, z], 4, 12, s_ref, f_ref, residual)
    half = pair_sum_matrix(384, 256, 0.5)
    v = times01(rz[...].reshape(192, 384), half)
    l1[0:12] = compact_rows(pack, v).reshape(12, 8, 256)
    eighth = pair_sum_matrix(384, 256, 0.125)
    d = jnp.stack([rho[2 * k + 2, :16] + rho[2 * k + 3, :16] for k in range(6)])
    l1[12:18] = compact_rows(pack, times01(d.reshape(96, 384), eighth)).reshape(6, 8, 256)


def down1(idx, own, lo, hi, b, gx, gy, gz, m, w, ep, chunk, rho, e1, rz, s_ref, f_ref, pack):
    wide, narrow = idx[0], idx[1]
    rowmask = jnp.concatenate([cell_mask(24, 8, 8, 8, narrow, 7)] * 2, axis=1)
    below = jnp.where(wide == 0, 0.0, 1.0) * rowmask
    above = jnp.where(wide == 15, 0.0, 1.0) * rowmask
    for z in range(5):
        rho[z] = lo[12 + z] * below
        rho[9 + z] = hi[12 + z] * above
    for z in range(4):
        rho[5 + z] = own[13 + z] * rowmask
        for c in range(3):
            b[c, 1 + z] = lo[4 * c + z]
            b[c, 5 + z] = own[4 * c + z]
            b[c, 9 + z] = hi[4 * c + z]
    level = Level(24, 256, False, False, gx, gy, gz, m, w, None, 0)
    coefficients(level, lambda z: rho[z], 1, 13)

    def first(z, _):
        for c in range(3):
            e1[c, z] = w[c, z] * b[c, z]
        return 0

    lax.fori_loop(1, 13, first, 0)

    def sweep(z, c, v, a):
        ep[c, z] = v + w[c, z] * (b[c, z] - a)

    operate(level, lambda c, z: e1[c, z], 2, 12, s_ref, f_ref, sweep)
    rz[...] = jnp.zeros_like(rz)

    def residual(z, c, v, a):
        r = b[c, z] - a
        k = ((z + 1) >> 1) - 3
        rz[c, k] = rz[c, k] + r[:8]

    operate(level, lambda c, z: ep[c, z], 5, 9, s_ref, f_ref, residual)
    rz[3, 0] = 0.25 * (rho[5, :8] + rho[6, :8])
    rz[3, 1] = 0.25 * (rho[7, :8] + rho[8, :8])
    half = pair_sum_matrix(256, 128, 0.5)
    v = compact_rows(pack, times01(rz[...].reshape(64, 256), half))
    lane = lax.broadcasted_iota(jnp.int32, (8, 128), 1)
    d = v[24:32]
    for c in range(3):
        moved = d if c == 3 else pltpu.roll(d, (96 - 32 * c) % 128, 1)
        chunk[:, 128 * c : 128 * (c + 1)] = jnp.where(lane < 96, v[8 * c : 8 * c + 8], moved)


def rest(
    idx, mine, other,
    b1, gx1, gy1, gz1, m1, w1, ep1,
    b0, gx0, gy0, gz0, m0, w0, ms0, ep0,
    out,
    rho2, b2, gx2, gy2, gz2, m2, w2, ms2, ea, ep2,
    rho3, b3, gx3, gy3, gz3, m3, w3, ms3, ec, ed,
    rz, rd, pack, s2, f2, s3, f3, ua, ub, va, vb, s1, f1, xa, xb, s0, f0,
):
    wide, narrow, core = idx[0], idx[1], idx[2]
    row8 = lax.broadcasted_iota(jnp.int32, (8, 128), 0)
    lane8 = lax.broadcasted_iota(jnp.int32, (8, 128), 1)
    zero2 = jnp.zeros((32, 128), F32)
    zero3 = jnp.zeros((16, 128), F32)
    for z in (0, 1, 2, 3, 36, 37, 38, 39):
        rho2[z] = zero2
        for ref in (gx2, gy2, gz2, m2, ms2):
            ref[z] = zero2
        for c in range(3):
            w2[c, z] = zero2
            b2[c, z] = zero2
            ea[c, z] = zero2
            ep2[c, z] = zero2
    for z in (0, 1, 18, 19):
        rho3[z] = zero3
        for ref in (gx3, gy3, gz3, m3, ms3):
            ref[z] = zero3
        for c in range(3):
            w3[c, z] = zero3
            ec[c, z] = zero3
            ed[c, z] = zero3

    def unpack(k, _):
        z = 2 * k + 4
        for y in range(4):
            a, c_ = mine[4 * k + y], other[4 * k + y]
            even = jnp.where(core == 0, a, c_)
            odd = jnp.where(core == 0, c_, a)
            rest_d = []
            for c in range(3):
                e = even[:, 128 * c : 128 * (c + 1)]
                o = odd[:, 128 * c : 128 * (c + 1)]
                first = jnp.where(row8 < 4, e, pltpu.roll(o, 4, 0))
                second = jnp.where(row8 < 4, pltpu.roll(e, 4, 0), o)
                b2[c, z, pl.ds(8 * y, 8), :] = jnp.where(lane8 < 96, first, 0.0)
                b2[c, z + 1, pl.ds(8 * y, 8), :] = jnp.where(lane8 < 96, second, 0.0)
                turn = (128 - (96 - 32 * c)) % 128
                rest_d.append((pltpu.roll(first, turn, 1), pltpu.roll(second, turn, 1)))
            for s in range(2):
                d = jnp.where(
                    lane8 < 32, rest_d[0][s], jnp.where(lane8 < 64, rest_d[1][s], rest_d[2][s])
                )
                rho2[z + s, pl.ds(8 * y, 8), :] = jnp.where(lane8 < 96, d, 0.0)
        return 0

    lax.fori_loop(0, 16, unpack, 0)

    level2 = Level(32, 128, False, True, gx2, gy2, gz2, m2, w2, ms2, 0)
    coefficients(level2, lambda z: rho2[z], 4, 36)

    def first2(z, _):
        for c in range(3):
            ea[c, z] = w2[c, z] * b2[c, z]
        return 0

    lax.fori_loop(4, 36, first2, 0)

    def sweep2(z, c, v, a):
        ep2[c, z] = v + w2[c, z] * (b2[c, z] - a)

    operate(level2, lambda c, z: ea[c, z], 4, 36, s2, f2, sweep2)
    rz[...] = jnp.zeros_like(rz)

    def residual2(z, c, v, a):
        k = (z >> 1) - 2
        rz[c, k] = rz[c, k] + (b2[c, z] - a)

    operate(level2, lambda c, z: ep2[c, z], 4, 36, s2, f2, residual2)

    def dens3(z, _):
        rz[3, z] = 0.25 * (rho2[2 * z + 4] + rho2[2 * z + 5])
        return 0

    lax.fori_loop(0, 16, dens3, 0)
    half = pair_sum_matrix(128, 128, 0.5)
    for c in range(4):
        v = compact_rows(pack, times01(rz[c].reshape(512, 128), half)).reshape(16, 16, 128)
        if c < 3:
            b3[c, 2:18] = v
        else:
            rho3[2:18] = v

    level3 = Level(16, 128, False, True, gx3, gy3, gz3, m3, w3, ms3, 0)
    coefficients(level3, lambda z: rho3[z], 2, 18)

    def first3(z, _):
        for c in range(3):
            ec[c, z] = w3[c, z] * b3[c, z]
        return 0

    lax.fori_loop(2, 18, first3, 0)

    for src, dst in ((ec, ed), (ed, ec), (ec, ed)):

        def sweep3(z, c, v, a, dst=dst):
            dst[c, z] = v + w3[c, z] * (b3[c, z] - a)

        operate(level3, lambda c, z, src=src: src[c, z], 2, 18, s3, f3, sweep3)

    dup = copy_matrix(128, 128)
    for c in range(3):
        copy_rows(pack, times01(ed[c, pl.ds(wide, 5)].reshape(80, 128), dup))
        for k in range(5):
            for s in range(2):
                z = 2 * k + s
                zb = 2 * wide + z
                inside = w2[0, zb] > 0.0
                up = pack[0, pl.ds(32 * k, 32), :]
                ua[c, z] = ep2[c, zb] + jnp.where(inside, up, 0.0)
    at2 = Level(32, 128, False, True, gx2, gy2, gz2, m2, w2, ms2, 2 * wide)

    def post2a(z, c, v, a):
        zb = z + 2 * wide
        ub[c, z] = v + w2[c, zb] * (b2[c, zb] - a)

    operate(at2, lambda c, z: ua[c, z], 1, 9, s2, f2, post2a)

    def post2b(z, c, v, a):
        zb = z + 2 * wide
        ua[c, z] = v + w2[c, zb] * (b2[c, zb] - a)

    operate(at2, lambda c, z: ub[c, z], 2, 8, s2, f2, post2b)

    wide1 = copy_matrix(128, 256)
    turn = idx[3]
    for c in range(3):
        parts = []
        for k in range(6):
            t = pltpu.roll(ua[c, 2 + k], turn, 0)
            parts += [t[0:8], t[24:32]]
        copy_rows(pack, times01(jnp.concatenate(parts, axis=0), wide1))
        for z in range(1, 11):
            k = z // 2
            inside = w1[0, z + 1] > 0.0
            top = jnp.concatenate([pack[j, pl.ds(32 * k, 16), :] for j in range(2)], axis=1)
            bot = jnp.concatenate([pack[j, pl.ds(32 * k + 24, 8), :] for j in range(2)], axis=1)
            up = jnp.concatenate([top, bot], axis=0)
            va[c, z + 1] = ep1[c, z + 1] + jnp.where(inside, up, 0.0)
    level1 = Level(24, 256, False, False, gx1, gy1, gz1, m1, w1, None, 0)

    def post1a(z, c, v, a):
        vb[c, z] = v + w1[c, z] * (b1[c, z] - a)

    operate(level1, lambda c, z: va[c, z], 3, 11, s1, f1, post1a)

    def post1b(z, c, v, a):
        va[c, z] = v + w1[c, z] * (b1[c, z] - a)

    operate(level1, lambda c, z: vb[c, z], 4, 10, s1, f1, post1b)

    wide0 = copy_matrix(256, 384)
    row = lax.broadcasted_iota(jnp.int32, (8, 256), 0)
    for c in range(3):
        parts = []
        for k in range(6):
            t = va[c, 4 + k]
            parts += [t[0:8], jnp.where(row < 2, t[8:16], pltpu.roll(t[16:24], 4, 0))]
        copy_rows(pack, times01(jnp.concatenate(parts, axis=0), wide0))
        for z in range(-2, 10):
            k = (z + 2) // 2
            inside = w0[0, z + 4] > 0.0
            up = jnp.concatenate([pack[j, pl.ds(32 * k, 24), :] for j in range(3)], axis=1)
            xa[c, z + 4] = ep0[c, z + 4] + jnp.where(inside, up, 0.0)
    level0 = Level(24, 384, True, False, gx0, gy0, gz0, m0, w0, ms0, 0)

    def post0a(z, c, v, a):
        xb[c, z] = v + w0[c, z] * (b0[c, z] - a)

    operate(level0, lambda c, z: xa[c, z], 3, 13, s0, f0, post0a)

    def post0b(z, c, v, a):
        out[c, z - 4] = (v + w0[c, z] * (b0[c, z] - a))[:16]

    operate(level0, lambda c, z: xb[c, z], 4, 12, s0, f0, post0b)


def call(kernel, outs, scratch, args, flops):
    vmem = pl.BlockSpec(memory_space=pltpu.VMEM)
    size = sum(4 * int(a.size) for a in args)
    size += sum(4 * functools.reduce(lambda p, q: p * q, s) for s in outs)
    return pl.pallas_call(
        kernel,
        out_shape=[jax.ShapeDtypeStruct(s, F32) for s in outs],
        in_specs=[pl.BlockSpec(memory_space=pltpu.SMEM)] + [vmem] * (len(args) - 1),
        out_specs=[vmem] * len(outs),
        scratch_shapes=[pltpu.VMEM(s, F32) for s in scratch],
        compiler_params=pltpu.CompilerParams(vmem_limit_bytes=56 * 1024 * 1024),
        cost_estimate=pl.CostEstimate(flops=flops, bytes_accessed=size, transcendentals=0),
    )(*args)


def shards(load, density):
    wide = lax.axis_index("wide")
    narrow = lax.axis_index(NARROW)
    core = lax.axis_index("core")
    idx = jnp.stack([wide, narrow, core, lax.rem(32 - 4 * narrow, 32)]).astype(jnp.int32)

    x0 = jnp.concatenate([load, density[None]], axis=0)
    low = lax.ppermute(x0[:, :, 12:], NARROW, cyclic(8, 1))
    high = lax.ppermute(x0[:, :, :4], NARROW, cyclic(8, -1))
    x1 = jnp.concatenate([x0, high, low], axis=2)
    up = jnp.concatenate([x1[:3, 5:].reshape(9, 24, 384), x1[3, 4:]], axis=0)
    down = jnp.concatenate([x1[:3, :3].reshape(9, 24, 384), x1[3, :4]], axis=0)
    lo = lax.ppermute(up, "wide", cyclic(16, 1))
    hi = lax.ppermute(down, "wide", cyclic(16, -1))
    p0 = (16, 24, 384)
    b0, gx0, gy0, gz0, m0, w0, ms0, ep0, l1 = call(
        down0,
        [(3,) + p0, p0, p0, p0, p0, (3,) + p0, p0, (3,) + p0, (18, 8, 256)],
        [p0, (3,) + p0, (3, 4, 16, 384), (24, 384), (3, 24, 384), (2, 192, 128)],
        [idx, x1, lo, hi],
        10**8,
    )

    low = lax.ppermute(l1, NARROW, cyclic(8, 1))
    high = lax.ppermute(l1, NARROW, cyclic(8, -1))
    own = jnp.concatenate([l1, high, low], axis=1)
    lo = lax.ppermute(own[:17], "wide", cyclic(16, 1))
    hi = lax.ppermute(jnp.concatenate([own[:12], own[13:18]], axis=0), "wide", cyclic(16, -1))
    p1 = (14, 24, 256)
    b1, gx1, gy1, gz1, m1, w1, ep1, chunk = call(
        down1,
        [(3,) + p1, p1, p1, p1, p1, (3,) + p1, (3,) + p1, (8, 384)],
        [p1, (3,) + p1, (4, 2, 8, 256), (24, 256), (3, 24, 256), (1, 64, 128)],
        [idx, own, lo, hi],
        10**8,
    )

    mine = lax.all_to_all(jnp.broadcast_to(chunk[None], (64, 8, 384)), ("wide", "y"), 0, 0)
    other = lax.ppermute(mine, "core", cyclic(2, 1))
    p2, p3 = (40, 32, 128), (20, 16, 128)
    u2 = (3, 10, 32, 128)
    (out,) = call(
        rest,
        [(3, 8, 16, 384)],
        [p2, (3,) + p2, p2, p2, p2, p2, (3,) + p2, p2, (3,) + p2, (3,) + p2]
        + [p3, (3,) + p3, p3, p3, p3, p3, (3,) + p3, p3, (3,) + p3, (3,) + p3]
        + [(4, 16, 32, 128), (8, 128), (3, 512, 128)]
        + [(32, 128), (3, 32, 128), (16, 128), (3, 16, 128), u2, u2]
        + [(3,) + p1, (3,) + p1, (24, 256), (3, 24, 256)]
        + [(3,) + p0, (3,) + p0, (24, 384), (3, 24, 384)],
        [idx, mine, other, b1, gx1, gy1, gz1, m1, w1, ep1, b0, gx0, gy0, gz0, m0, w0, ms0, ep0],
        3 * 10**8,
    )
    return out


def solution(mesh):
    split = Mesh(mesh.devices.reshape(16, 4, 2), ("wide", "y", "core"))
    in_specs = (P(None, "wide", NARROW, None), P("wide", NARROW, None))
    out_specs = P(None, "wide", NARROW, None)
    return jax.shard_map(shards, mesh=split, in_specs=in_specs, out_specs=out_specs, check_vma=False)
```

time: 538 us -> 144 us (0.27)
  the two profiles are of different devices: /device:TPU:115 before, /device:TPU:1 now
where the time goes in v1:
time: 144 us
  Pallas kernels  63.9 us (44%)
  blocking collectives  29.8 us (21%)
  starting transfers between devices  21.5 us (15%)
  waiting for transfers between devices  18.9 us (13%)
  local copies, waits for them, and re-layouts  7.34 us (5%)
  other arithmetic  2.17 us (2%)
    pallas_call x3, Pallas kernels, call(): pl.pallas_call(kernel, out_shape=[jax.ShapeDtypeStruct(s, F32) for s in o...  63.9 us
    all_to_all x1, blocking collectives, shards(): lax.all_to_all(jnp.broadcast_to(chunk[None], (64, 8, 384)), ('wide', 'y')...  29.8 us
    unnamed x22, local copies, waits for them, and re-layouts  6.44 us
    ppermute x1, waiting for transfers between devices, shards(): lo = lax.ppermute(up, 'wide', cyclic(16, 1))  6.28 us
    ppermute x1, waiting for transfers between devices, shards(): lo = lax.ppermute(own[:17], 'wide', cyclic(16, 1))  5.22 us
    ppermute x1, starting transfers between devices, shards(): high = lax.ppermute(l1, NARROW, cyclic(8, -1))  4.85 us
    ppermute x1, starting transfers between devices, shards(): hi = lax.ppermute(down, 'wide', cyclic(16, -1))  4.81 us
    ppermute x1, starting transfers between devices, shards(): lax.ppermute(jnp.concatenate([own[:12], own[13:18]], axis=0), 'wide', cyc...  4.39 us
  transfers between devices with their start and end apart: 9, of which 6 were waited for; matrix products, arithmetic and copies ran while one was open for 1% of the time, Pallas kernels for 0%

profile of v1, /device:TPU:1, one launch (start us, length us, event | category | flops | bytes accessed | tf_op | source)
XLA Modules:
  0.0 143.7 jit_solution(5947395291942813200)
XLA Ops:
  0.0 1.3 pad_maximum_fusion.5
  1.3 1.4 collective-permute-start
  2.7 1.3 collective-permute-start.1
  4.0 3.3 %collective-permute-done = f32[4,8,4,384]{3,2,1,0:T(4,128)S(1)} collective-permute-done((f32[4,8,4,384]{3,2,1,0:T(4,128)S(1)}, f32[4,8,4,384]{3,2,1,0:T(4,128)S(1)}, u32[]{:S(2)}, u32[]{:S(2)}) %collective-permute-start) | collective-permute-done | bytes 196640 | tf_op jit(solution)/shard_map/ppermute | solution.py:501
  7.4 0.1 pad_maximum_fusion.x1
  7.6 0.9 copy-done
  8.5 1.2 collective-permute-start.2
  9.8 4.8 %collective-permute-start.3 = (f32[13,24,384]{2,1,0:T(8,128)S(1)}, f32[13,24,384]{2,1,0:T(8,128)S(1)}, u32[]{:S(2)}, u32[]{:S(2)}) collective-permute-start(f32[13,24,384]{2,1,0:T(8,128)S(1)} %pad_maximum_fusion.2), channel_id=1, source_target_pairs={{0,120},{8,0},{16,8},{24,16},{32,24},{40,32},{48,40},{56,48},{64,5... | collective-permute-start | bytes 1437704 | tf_op jit(solution)/shard_map/ppermute | solution.py:506
  14.6 0.7 pad_add_fusion.idx
  15.2 6.3 %collective-permute-done.2.lo = f32[13,24,384]{2,1,0:T(8,128)S(1)} collective-permute-done((f32[13,24,384]{2,1,0:T(8,128)S(1)}, f32[13,24,384]{2,1,0:T(8,128)S(1)}, u32[]{:S(2)}, u32[]{:S(2)}) %collective-permute-start.2) | collective-permute-done | bytes 479264 | tf_op jit(solution)/shard_map/ppermute | solution.py:505
  21.5 0.8 copy-done.6
  22.3 0.8 copy-done.7
  23.1 11.7 %shard_map.28 = (f32[3,16,24,384]{3,2,1,0:T(8,128)}, f32[16,24,384]{2,1,0:T(8,128)}, f32[16,24,384]{2,1,0:T(8,128)}, f32[16,24,384]{2,1,0:T(8,128)}, f32[16,24,3...) custom-call(s32[4]{0:T(128)} %pad_add_fusion.idx, ...), custom_call_target="tpu_custom_call" | custom-call | flops 100000000 | bytes 10543120 | tf_op jit(solution)/shard_map/pallas_call | solution.py:482
  34.8 4.9 %collective-permute-start.4 = (f32[18,8,256]{2,1,0:T(8,128)}, f32[18,8,256]{2,1,0:T(8,128)S(1)}, u32[]{:S(2)}, u32[]{:S(2)}) collective-permute-start(f32[18,8,256]{2,1,0:T(8,128)} %get-tuple-element.22), channel_id=1, source_target_pairs={{0,7},{1,0},{2,1},{3,2},{4,3},{5,4},{6,5},{7,6},{8,15},{9,8},{10,9... | collective-permute-start | bytes 442376 | tf_op jit(solution)/shard_map/ppermute | solution.py:517
  39.6 1.4 collective-permute-start.5
  41.0 1.0 constant_dynamic-update-slice_fusion.2
  41.9 2.1 %collective-permute-done.4 = f32[18,8,256]{2,1,0:T(8,128)S(1)} collective-permute-done((f32[18,8,256]{2,1,0:T(8,128)}, f32[18,8,256]{2,1,0:T(8,128)S(1)}, u32[]{:S(2)}, u32[]{:S(2)}) %collective-permute-start.4) | collective-permute-done | bytes 147488 | tf_op jit(solution)/shard_map/ppermute | solution.py:517
  44.0 0.1 collective-permute-done.5
  44.2 0.0 copy-start.1
  44.3 0.1 collective-permute-start.6
  44.4 0.5 copy-done.1
  44.9 4.4 %collective-permute-start.7 = (f32[17,24,256]{2,1,0:T(8,128)S(1)}, f32[17,24,256]{2,1,0:T(8,128)S(1)}, u32[]{:S(2)}, u32[]{:S(2)}) collective-permute-start(f32[17,24,256]{2,1,0:T(8,128)S(1)} %pad_maximum_fusion.3), channel_id=1, source_target_pairs={{0,120},{8,0},{16,8},{24,16},{32,24},{40,32},{48,40},{56,48},{64,5... | collective-permute-start | bytes 1253384 | tf_op jit(solution)/shard_map/ppermute | solution.py:520
  49.3 5.2 %collective-permute-done.6.lo = f32[17,24,256]{2,1,0:T(8,128)S(1)} collective-permute-done((f32[17,24,256]{2,1,0:T(8,128)S(1)}, f32[17,24,256]{2,1,0:T(8,128)S(1)}, u32[]{:S(2)}, u32[]{:S(2)}) %collective-permute-start.6) | collective-permute-done | bytes 417824 | tf_op jit(solution)/shard_map/ppermute | solution.py:519
  54.5 0.8 copy-done.8
  55.3 0.8 copy-done.9
  56.1 8.0 %shard_map.29 = (f32[3,14,24,256]{3,2,1,0:T(8,128)}, f32[14,24,256]{2,1,0:T(8,128)}, f32[14,24,256]{2,1,0:T(8,128)}, f32[14,24,256]{2,1,0:T(8,128)}, f32[14,24,2...) custom-call(s32[4]{0:T(128)} %pad_add_fusion.idx, ...), custom_call_target="tpu_custom_call" | custom-call | flops 100000000 | bytes 5763088 | tf_op jit(solution)/shard_map/pallas_call | solution.py:482
  64.2 0.8 broadcast_in_dim.10
  64.9 29.8 %all_to_all.5.mine = f32[64,8,384]{2,1,0:T(8,128)S(1)} all-to-all(f32[64,8,384]{2,1,0:T(8,128)S(1)} %broadcast_in_dim.10), channel_id=1, replica_groups=mesh['wide'=16,'y'=4,'core'=2] {'wide','y'}, dimensions={0} | all-to-all | bytes 1572864 | tf_op jit(solution)/shard_map/all_to_all | solution.py:530
  94.8 2.0 %collective-permute-start.8 = (f32[64,8,384]{2,1,0:T(8,128)S(1)}, f32[64,8,384]{2,1,0:T(8,128)S(1)}, u32[]{:S(2)}, u32[]{:S(2)}) collective-permute-start(f32[64,8,384]{2,1,0:T(8,128)S(1)} %all_to_all.5.mine), channel_id=1, source_target_pairs={{0,1},{1,0},{2,3},{3,2},{4,5},{5,4},{6,7},{7,6},{8,9},{9,8},{10,11... | collective-permute-start | bytes 2359304 | tf_op jit(solution)/shard_map/ppermute | solution.py:531
  96.8 1.9 %collective-permute-done.8.other = f32[64,8,384]{2,1,0:T(8,128)S(1)} collective-permute-done((f32[64,8,384]{2,1,0:T(8,128)S(1)}, f32[64,8,384]{2,1,0:T(8,128)S(1)}, u32[]{:S(2)}, u32[]{:S(2)}) %collective-permute-start.8) | collective-permute-done | bytes 786464 | tf_op jit(solution)/shard_map/ppermute | solution.py:531
  98.7 0.9 copy-done.5
  99.6 44.1 %shard_map.30 = f32[3,8,16,384]{3,2,1,0:T(8,128)} custom-call(s32[4]{0:T(128)} %pad_add_fusion.idx, f32[64,8,384]{2,1,0:T(8,128)} %copy-done.2, f32[64,8,384]{2,1,0:T(8,128)} %copy-done.5, f32[3,14,24,256]{3,2,1,0:T(8,128)} %get-tuple-element.24.b1, f32[14,24,256]{2,1,0:T(8,128)} %get-tuple-element.25.gx1, f32[14,24,256]{2,1,0:T(8,128)} %get-tuple-element.26.gy1, ...), custom_call_target="tpu_custom_call" | custom-call | flops 300000000 | bytes 14893072 | tf_op jit(solution)/shard_map/pallas_call | solution.py:482
  (25 shorter events, 0.3 us)
Async XLA Ops:
  0.0 7.4 %copy-start.3 = (f32[3,8,16,384]{3,2,1,0:T(8,128)S(1)}, f32[3,8,16,384]{3,2,1,0:T(8,128)}, u32[]{:S(2)}) copy-start(f32[3,8,16,384]{3,2,1,0:T(8,128)} %param.2) | copy-start | bytes 1769476
  0.0 7.4 %copy-start.4 = (f32[8,16,384]{2,1,0:T(8,128)S(1)}, f32[8,16,384]{2,1,0:T(8,128)}, u32[]{:S(2)}) copy-start(f32[8,16,384]{2,1,0:T(8,128)} %param.3) | copy-start | bytes 589828
  1.3 6.1 %collective-permute-start = (f32[4,8,4,384]{3,2,1,0:T(4,128)S(1)}, f32[4,8,4,384]{3,2,1,0:T(4,128)S(1)}, u32[]{:S(2)}, u32[]{:S(2)}) collective-permute-start(f32[4,8,4,384]{3,2,1,0:T(4,128)S(1)} %get-tuple-element.43), channel_id=1, source_target_pairs={{0,7},{1,0},{2,1},{3,2},{4,3},{5,4},{6,5},{7,6},{8,15},{9,8},{10,9... | collective-permute-start | bytes 589832 | tf_op jit(solution)/shard_map/ppermute | solution.py:501
  2.7 4.6 %collective-permute-start.1 = (f32[4,8,4,384]{3,2,1,0:T(4,128)S(1)}, f32[4,8,4,384]{3,2,1,0:T(4,128)S(1)}, u32[]{:S(2)}, u32[]{:S(2)}) collective-permute-start(f32[4,8,4,384]{3,2,1,0:T(4,128)S(1)} %get-tuple-element.44), channel_id=1, source_target_pairs={{0,1},{1,2},{2,3},{3,4},{4,5},{5,6},{6,7},{7,0},{8,9},{9,10},{10,1... | collective-permute-start | bytes 589832 | tf_op jit(solution)/shard_map/ppermute | solution.py:500
  7.5 1.0 copy-start
  8.5 13.0 %collective-permute-start.2 = (f32[13,24,384]{2,1,0:T(8,128)S(1)}, f32[13,24,384]{2,1,0:T(8,128)S(1)}, u32[]{:S(2)}, u32[]{:S(2)}) collective-permute-start(f32[13,24,384]{2,1,0:T(8,128)S(1)} %pad_maximum_fusion.1), channel_id=1, source_target_pairs={{0,8},{8,16},{16,24},{24,32},{32,40},{40,48},{48,56},{56,64},{64,7... | collective-permute-start | bytes 1437704 | tf_op jit(solution)/shard_map/ppermute | solution.py:505
  9.8 11.8 %collective-permute-start.3 = (f32[13,24,384]{2,1,0:T(8,128)S(1)}, f32[13,24,384]{2,1,0:T(8,128)S(1)}, u32[]{:S(2)}, u32[]{:S(2)}) collective-permute-start(f32[13,24,384]{2,1,0:T(8,128)S(1)} %pad_maximum_fusion.2), channel_id=1, source_target_pairs={{0,120},{8,0},{16,8},{24,16},{32,24},{40,32},{48,40},{56,48},{64,5... | collective-permute-start | bytes 1437704 | tf_op jit(solution)/shard_map/ppermute | solution.py:506
  21.5 0.8 copy-start.6
  22.3 0.8 copy-start.7
  34.8 9.3 %collective-permute-start.4 = (f32[18,8,256]{2,1,0:T(8,128)}, f32[18,8,256]{2,1,0:T(8,128)S(1)}, u32[]{:S(2)}, u32[]{:S(2)}) collective-permute-start(f32[18,8,256]{2,1,0:T(8,128)} %get-tuple-element.22), channel_id=1, source_target_pairs={{0,7},{1,0},{2,1},{3,2},{4,3},{5,4},{6,5},{7,6},{8,15},{9,8},{10,9... | collective-permute-start | bytes 442376 | tf_op jit(solution)/shard_map/ppermute | solution.py:517
  39.6 4.5 %collective-permute-start.5 = (f32[18,8,256]{2,1,0:T(8,128)}, f32[18,8,256]{2,1,0:T(8,128)S(1)}, u32[]{:S(2)}, u32[]{:S(2)}) collective-permute-start(f32[18,8,256]{2,1,0:T(8,128)} %get-tuple-element.22), channel_id=1, source_target_pairs={{0,1},{1,2},{2,3},{3,4},{4,5},{5,6},{6,7},{7,0},{8,9},{9,10},{10,1... | collective-permute-start | bytes 442376 | tf_op jit(solution)/shard_map/ppermute | solution.py:516
  44.2 0.8 copy-start.1
  44.3 10.3 %collective-permute-start.6 = (f32[17,24,256]{2,1,0:T(8,128)S(1)}, f32[17,24,256]{2,1,0:T(8,128)S(1)}, u32[]{:S(2)}, u32[]{:S(2)}) collective-permute-start(f32[17,24,256]{2,1,0:T(8,128)S(1)} %slice.40), channel_id=1, source_target_pairs={{0,8},{8,16},{16,24},{24,32},{32,40},{40,48},{48,56},{56,64},{64,7... | collective-permute-start | bytes 1253384 | tf_op jit(solution)/shard_map/ppermute | solution.py:519
  44.9 9.6 %collective-permute-start.7 = (f32[17,24,256]{2,1,0:T(8,128)S(1)}, f32[17,24,256]{2,1,0:T(8,128)S(1)}, u32[]{:S(2)}, u32[]{:S(2)}) collective-permute-start(f32[17,24,256]{2,1,0:T(8,128)S(1)} %pad_maximum_fusion.3), channel_id=1, source_target_pairs={{0,120},{8,0},{16,8},{24,16},{32,24},{40,32},{48,40},{56,48},{64,5... | collective-permute-start | bytes 1253384 | tf_op jit(solution)/shard_map/ppermute | solution.py:520
  54.5 0.8 copy-start.8
  55.3 0.8 copy-start.9
  94.8 3.9 %copy-start.2 = (f32[64,8,384]{2,1,0:T(8,128)}, f32[64,8,384]{2,1,0:T(8,128)S(1)}, u32[]{:S(2)}) copy-start(f32[64,8,384]{2,1,0:T(8,128)S(1)} %all_to_all.5.mine) | copy-start | bytes 2359300
  94.8 3.9 %collective-permute-start.8 = (f32[64,8,384]{2,1,0:T(8,128)S(1)}, f32[64,8,384]{2,1,0:T(8,128)S(1)}, u32[]{:S(2)}, u32[]{:S(2)}) collective-permute-start(f32[64,8,384]{2,1,0:T(8,128)S(1)} %all_to_all.5.mine), channel_id=1, source_target_pairs={{0,1},{1,0},{2,3},{3,2},{4,5},{5,4},{6,7},{7,6},{8,9},{9,8},{10,11... | collective-permute-start | bytes 2359304 | tf_op jit(solution)/shard_map/ppermute | solution.py:531
  98.7 0.9 copy-start.5

commit v2 on v0

v2 whole, which is shorter than its diff:
```python
import functools

import jax
import jax.numpy as jnp
from jax import lax
from jax.experimental import pallas as pl
from jax.experimental.pallas import tpu as pltpu
from jax.sharding import Mesh, PartitionSpec as P

DAMPING = 0.5
MASS = 0.02
NARROW = ("y", "core")
F32 = jnp.float32
BF16 = jnp.bfloat16


def cyclic(count, step):
    return [(i, (i + step) % count) for i in range(count)]


def after_y(v):
    return jnp.concatenate([v[1:], pltpu.roll(v[0], 7, 0)[None]], axis=0)


def before_y(v):
    return jnp.concatenate([pltpu.roll(v[v.shape[0] - 1], 1, 0)[None], v[:-1]], axis=0)


def after_x(v):
    return pltpu.roll(v, v.shape[2] - 1, 2)


def before_x(v):
    return pltpu.roll(v, 1, 2)


def times01(v, matrix):
    high = v.astype(BF16)
    rest = v - high.astype(F32)
    mid = rest.astype(BF16)
    low = (rest - mid.astype(F32)).astype(BF16)
    out = jnp.dot(high, matrix, preferred_element_type=F32)
    out = out + jnp.dot(mid, matrix, preferred_element_type=F32)
    return out + jnp.dot(low, matrix, preferred_element_type=F32)


def pair_sum_matrix(fine, coarse, start, factor):
    i = lax.broadcasted_iota(jnp.int32, (fine, coarse), 0)
    j = lax.broadcasted_iota(jnp.int32, (fine, coarse), 1)
    return jnp.where((i >> 1) + start == j, factor, 0.0).astype(BF16)


def copy_matrix(coarse, fine):
    j = lax.broadcasted_iota(jnp.int32, (coarse, fine), 0)
    i = lax.broadcasted_iota(jnp.int32, (coarse, fine), 1)
    return jnp.where((i >> 1) == j, 1.0, 0.0).astype(BF16)


def lane_tiles(v):
    return [v[..., 128 * k : 128 * (k + 1)] for k in range(v.shape[-1] // 128)]


def join(parts):
    return parts[0] if len(parts) == 1 else jnp.concatenate(parts, axis=-1)


def interleaved(ref, tiles, *at):
    lanes = ref.shape[len(at)]
    return jnp.stack(
        [
            join([ref[(*at, k, pl.ds(t, 8, stride=tiles), slice(None))] for k in range(lanes)])
            for t in range(tiles)
        ]
    )


def to_natural(ref, v, *at):
    tiles = v.shape[0]
    for t in range(tiles):
        for k, part in enumerate(lane_tiles(v[t])):
            ref[(*at, k, pl.ds(t, 8, stride=tiles), slice(None))] = part


def row_pairs(ref, start, *at):
    parts = []
    for k in range(ref.shape[len(at)]):
        a = ref[(*at, k, pl.ds(start, 8, stride=2), slice(None))]
        b = ref[(*at, k, pl.ds(start + 1, 8, stride=2), slice(None))]
        parts.append(a + b)
    return join(parts)


def copy_rows(ref, v, start, *at):
    for k, part in enumerate(lane_tiles(v)):
        ref[(*at, k, pl.ds(start, 8, stride=2), slice(None))] = part
        ref[(*at, k, pl.ds(start + 1, 8, stride=2), slice(None))] = part


class Level:
    def __init__(self, tiles, lanes, wrap_x, wrap_y, gx, gy, gz, m, w, ms):
        self.shape = (tiles, 8, lanes)
        self.wrap_x, self.wrap_y = wrap_x, wrap_y
        self.gx, self.gy, self.gz, self.m, self.w, self.ms = gx, gy, gz, m, w, ms

    def masks(self):
        tiles, _, lanes = self.shape
        t = lax.broadcasted_iota(jnp.int32, self.shape, 0)
        s = lax.broadcasted_iota(jnp.int32, self.shape, 1)
        lane = lax.broadcasted_iota(jnp.int32, self.shape, 2)
        row = tiles * s + t
        return (row == 0, row == 8 * tiles - 1, lane == 0, lane == lanes - 1)

    def after(self, v, axis, masks):
        r = after_y(v) if axis == 1 else after_x(v)
        if axis == 1 and self.wrap_y:
            r = jnp.where(masks[1], 0.0, r)
        if axis == 2 and self.wrap_x:
            r = jnp.where(masks[3], 0.0, r)
        return r

    def before(self, v, axis, masks):
        r = before_y(v) if axis == 1 else before_x(v)
        if axis == 1 and self.wrap_y:
            r = jnp.where(masks[0], 0.0, r)
        if axis == 2 and self.wrap_x:
            r = jnp.where(masks[2], 0.0, r)
        return r


def coefficients(level, rho, lo, hi):
    masks = level.masks()

    def shear(z):
        d = rho[z]
        return d * d * d

    def plane(z, _):
        d = rho[z]
        dn = rho[z + 1]
        g = d * d * d
        gn = dn * dn * dn
        gp = shear(z - 1)
        m = g * (0.5 + d)
        mn = gn * (0.5 + dn)
        gx = 0.5 * (g + after_x(g))
        gy = 0.5 * (g + after_y(g))
        gz = 0.5 * (g + gn)
        total = MASS + gz + 0.5 * (g + gp)
        extra = None
        if level.wrap_x:
            gx = jnp.where(masks[3], 0.0, gx)
            extra = jnp.where(masks[2] | masks[3], 0.5 * g, 0.0)
        if level.wrap_y:
            gy = jnp.where(masks[1], 0.0, gy)
            more = jnp.where(masks[0] | masks[1], 0.5 * g, 0.0)
            extra = more if extra is None else extra + more
        if extra is not None:
            level.ms[z] = MASS + extra
            total = total + extra
        total = total + (gx + before_x(gx)) + (gy + before_y(gy)) + m
        inside = d > 0.0
        level.gx[z] = gx
        level.gy[z] = gy
        level.gz[z] = gz
        level.m[z] = m
        level.w[0, z] = jnp.where(inside, DAMPING / (total + mn), 0.0)
        level.w[1, z] = jnp.where(inside, DAMPING / (total + level.after(m, 1, masks)), 0.0)
        level.w[2, z] = jnp.where(inside, DAMPING / (total + level.after(m, 2, masks)), 0.0)
        return 0

    level.gz[lo - 1] = 0.5 * (shear(lo - 1) + shear(lo))
    last = rho[hi]
    level.m[hi] = last * last * last * (0.5 + last)
    lax.fori_loop(lo, hi, plane, 0)


def operate(level, u, lo, hi, s_ref, f_ref, emit):
    masks = level.masks()

    def stress(z):
        uz, uy, ux = u[0, z], u[1, z], u[2, z]
        div = (uz - u[0, z - 1]) + (uy - level.before(uy, 1, masks))
        return level.m[z] * (div + (ux - level.before(ux, 2, masks)))

    s_ref[...] = stress(lo)
    for c in range(3):
        f_ref[c] = level.gz[lo - 1] * (u[c, lo - 1] - u[c, lo])

    def plane(z, _):
        s = s_ref[...]
        sn = stress(z + 1)
        s_ref[...] = sn
        gx, gy, gz = level.gx[z], level.gy[z], level.gz[z]
        for c in range(3):
            v = u[c, z]
            fz = gz * (v - u[c, z + 1])
            fx = gx * (v - after_x(v))
            fy = gy * (v - after_y(v))
            grad = s - (sn if c == 0 else level.after(s, c, masks))
            mass = MASS if level.ms is None else level.ms[z]
            a = mass * v + (fz - f_ref[c]) + (fx - before_x(fx)) + (fy - before_y(fy)) + grad
            f_ref[c] = fz
            emit(z, c, v, a)
        return 0

    lax.fori_loop(lo, hi, plane, 0)


def scaled(w, b, e, lo, hi):
    def plane(z, _):
        for c in range(3):
            e[c, z] = w[c, z] * b[c, z]
        return 0

    lax.fori_loop(lo, hi, plane, 0)


def smoothed(level, b, src, dst, lo, hi, s_ref, f_ref):
    def emit(z, c, v, a):
        dst[c, z] = v + level.w[c, z] * (b[c, z] - a)

    operate(level, src, lo, hi, s_ref, f_ref, emit)


def in_grid(shape, own, high, n, last):
    t = lax.broadcasted_iota(jnp.int32, shape, 0)
    s = lax.broadcasted_iota(jnp.int32, shape, 1)
    row = shape[0] * s + t
    bad_high = (row >= own) & (row < own + high) & (n == last)
    bad_low = (row >= own + high) & (n == 0)
    return jnp.where(bad_high | bad_low, 0.0, 1.0)


def down0(
    idx, load, dens, rows, lo, hi,
    b, gx, gy, gz, m, w, ms, ep, edge_low, edge_high, l1,
    nat, rho, e1, rz, back, s_ref, f_ref,
):
    wide, narrow = idx[0], idx[1]
    for c in range(4):
        for z in range(8):
            own = dens[z] if c == 3 else load[c, z]
            for k in range(3):
                nat[c, z + 3, k, 0:16] = own[:, 128 * k : 128 * (k + 1)]
                nat[c, z + 3, k, 16:24] = rows[c, z, :, 128 * k : 128 * (k + 1)]
    for c in range(4):
        for j in range(3 if c == 3 else 2):
            for k in range(3):
                nat[c, j + (0 if c == 3 else 1), k] = lo[2 * c + j, :, 128 * k : 128 * (k + 1)]
                nat[c, j + 11, k] = hi[2 * c + j, :, 128 * k : 128 * (k + 1)]
    grid = in_grid((3, 8, 384), 16, 4, narrow, 7)
    below = jnp.where(wide == 0, 0.0, 1.0) * grid
    above = jnp.where(wide == 15, 0.0, 1.0) * grid
    for z in range(14):
        rho[z] = interleaved(nat, 3, 3, z) * (below if z < 3 else above if z > 10 else grid)
    level = Level(3, 384, True, False, gx, gy, gz, m, w, ms)
    coefficients(level, rho, 1, 13)

    def first(z, _):
        for c in range(3):
            v = interleaved(nat, 3, c, z)
            b[c, z] = v
            e1[c, z] = w[c, z] * v
        return 0

    lax.fori_loop(1, 13, first, 0)
    smoothed(level, b, e1, ep, 2, 12, s_ref, f_ref)
    for c in range(3):
        edge_low[c] = ep[c, 4]
        edge_high[c] = ep[c, 9]
    rz[...] = jnp.zeros_like(rz)

    def residual(z, c, v, a):
        k = ((z + 1) >> 1) - 2
        rz[c, k] = rz[c, k] + (b[c, z] - a)

    operate(level, ep, 3, 11, s_ref, f_ref, residual)
    even, odd = [], []
    for c in range(3):
        for k in range(4):
            to_natural(back, rz[c, k], c, k)
            (odd if k % 2 else even).append(row_pairs(back, 0, c, k))
    for k in range(6):
        d = 0.25 * (row_pairs(nat, 0, 3, 2 * k + 1) + row_pairs(nat, 0, 3, 2 * k + 2))
        if k == 0:
            d = d * jnp.where(wide == 0, 0.0, 1.0)
        if k == 5:
            d = d * jnp.where(wide == 15, 0.0, 1.0)
        (odd if k % 2 else even).append(d)
    left = pair_sum_matrix(384, 384, 0, 0.5)
    right = pair_sum_matrix(384, 384, 192, 0.5)
    out = times01(jnp.concatenate(even, axis=0), left)
    out = out + times01(jnp.concatenate(odd, axis=0), right)
    l1[...] = out.reshape(9, 8, 384)


def halves(v):
    lane = lax.broadcasted_iota(jnp.int32, (v.shape[0], 256), 1)
    first = jnp.where(lane < 192, v[:, :256], 0.0)
    second = jnp.where(lane < 192, pltpu.roll(v, 192, 1)[:, :256], 0.0)
    return first, second


def down1(
    idx, own, after, before, lo, hi,
    b, gx, gy, gz, m, w, ep, l2,
    nat, rho, e1, rz, back, s_ref, f_ref,
):
    wide, narrow = idx[0], idx[1]
    row = lax.broadcasted_iota(jnp.int32, (8, 256), 0)

    def put(c, z, r, v):
        for k in range(2):
            nat[c, z, k, pl.ds(r, 8), :] = v[:, 128 * k : 128 * (k + 1)]

    for c in range(4):
        for q in range(3 if c == 3 else 2):
            i = 2 * c + q
            zo = 2 * q - 1 if c == 3 else 2 * q
            for r, ref in ((0, own), (8, after), (16, before)):
                for s, v in enumerate(halves(ref[i])):
                    if 0 <= zo + s < 4:
                        put(c, zo + s + 5, r, v)
            for shift, ref in ((-4, lo), (4, hi)):
                if c < 3:
                    tiles = [halves(ref[pl.ds(16 * i + 8 * r, 8), :]) for r in range(2)]
                else:
                    tiles = [halves(ref[pl.ds(96 + 24 * q + 8 * r, 8), :]) for r in range(3)]
                for s in range(2):
                    z = zo + s + shift
                    if 0 <= z < 4:
                        continue
                    put(c, z + 5, 0, tiles[0][s])
                    if c < 3:
                        put(c, z + 5, 8, jnp.where(row < 4, tiles[1][s], 0.0))
                        put(c, z + 5, 16, jnp.where(row >= 4, tiles[1][s], 0.0))
                    else:
                        put(c, z + 5, 8, tiles[1][s])
                        put(c, z + 5, 16, tiles[2][s])
    grid = in_grid((3, 8, 256), 8, 8, narrow, 7)
    below = jnp.where(wide == 0, 0.0, 1.0) * grid
    above = jnp.where(wide == 15, 0.0, 1.0) * grid
    for z in range(14):
        rho[z] = interleaved(nat, 3, 3, z) * (below if z < 5 else above if z > 8 else grid)
    level = Level(3, 256, False, False, gx, gy, gz, m, w, None)
    coefficients(level, rho, 1, 13)

    def first(z, _):
        for c in range(3):
            v = interleaved(nat, 3, c, z)
            b[c, z] = v
            e1[c, z] = w[c, z] * v
        return 0

    lax.fori_loop(1, 13, first, 0)
    smoothed(level, b, e1, ep, 2, 12, s_ref, f_ref)
    rz[...] = jnp.zeros_like(rz)

    def residual(z, c, v, a):
        k = ((z + 1) >> 1) - 2
        rz[c, k] = rz[c, k] + (b[c, z] - a)

    operate(level, ep, 3, 11, s_ref, f_ref, residual)
    parts = []
    for c in range(3):
        for k in range(4):
            to_natural(back, rz[c, k], c, k)
            parts.append(jnp.where(row < 6, row_pairs(back, 0, c, k), row_pairs(back, 8, c, k)))
    for k in range(6):
        d = [row_pairs(nat, r, 3, 2 * k + 1) + row_pairs(nat, r, 3, 2 * k + 2) for r in (0, 8)]
        parts.append(0.25 * jnp.where(row < 6, d[0], d[1]))
    out = times01(jnp.concatenate(parts, axis=0), pair_sum_matrix(256, 128, 0, 0.5))
    l2[...] = out.reshape(len(parts), 8, 128)


def down2(
    idx, own, lo, lo2, hi, hi2,
    b, gx, gy, gz, m, w, ep, chunk,
    rho, e1, s_ref, f_ref,
):
    wide, narrow = idx[0], idx[1]
    t = lax.broadcasted_iota(jnp.int32, (2, 8, 128), 0)
    s = lax.broadcasted_iota(jnp.int32, (2, 8, 128), 1)
    row = 2 * s + t
    y = 4 * narrow + jnp.where(row < 10, row, row - 16)
    grid = jnp.where((y >= 0) & (y < 32), 1.0, 0.0)

    def rows(ref, i):
        return jnp.stack([ref[i, pl.ds(k, 8, stride=2), :] for k in range(2)])

    for z in range(14):
        if z < 4:
            ref, i = (lo2 if z < 2 else lo), 6 + z % 2
        elif z < 10:
            ref, i = own, 12 + z - 4
        else:
            ref, i = (hi if z < 12 else hi2), 6 + z % 2
        zg = 2 * wide + z - 6
        factor = jnp.where((zg >= 0) & (zg < 32), 1.0, 0.0)
        rho[z] = rows(ref, i) * (grid * factor)
    for c in range(3):
        for z in range(1, 13):
            if z < 5:
                ref, i = (lo2 if z < 3 else lo), 2 * c + (z - 1) % 2
            elif z < 9:
                ref, i = own, 4 * c + z - 5
            else:
                ref, i = (hi if z < 11 else hi2), 2 * c + (z - 9) % 2
            b[c, z] = rows(ref, i)
    level = Level(2, 128, False, False, gx, gy, gz, m, w, None)
    coefficients(level, rho, 1, 13)
    scaled(w, b, e1, 1, 13)
    smoothed(level, b, e1, ep, 2, 12, s_ref, f_ref)
    row8 = lax.broadcasted_iota(jnp.int32, (8, 128), 0)
    sums = [0.25 * (rho[6] + rho[7])]

    def residual(z, c, v, a):
        e1[c, z] = b[c, z] - a

    operate(level, ep, 6, 8, s_ref, f_ref, residual)
    total = jnp.zeros((8, 128), F32)
    for c in range(4):
        v = e1[c, 6] + e1[c, 7] if c < 3 else sums[0]
        v = v[0] + v[1]
        v = pltpu.roll(v, 2 * c, 0) if c else v
        total = jnp.where((row8 >> 1) == c, v, total)
    chunk[...] = times01(total, pair_sum_matrix(128, 128, 0, 0.5))


def rest(
    idx, mine, other, edge0, edge9,
    b2, gx2, gy2, gz2, m2, w2, ep2,
    b1, gx1, gy1, gz1, m1, w1, ep1,
    b0, gx0, gy0, gz0, m0, w0, ms0, ep0,
    out,
    rho3, b3, gx3, gy3, gz3, m3, w3, ms3, ec, ed,
    nat2, nat1, nat0, s3, f3, ua, ub, s2, f2, va, vb, s1, f1, xa, xb, s0, f0,
):
    wide, turn, core = idx[0], idx[2], idx[3]
    zero3 = jnp.zeros((2, 8, 128), F32)
    for z in (1, 18):
        rho3[z] = zero3
    for z in (0, 1, 18, 19):
        for c in range(3):
            ec[c, z] = zero3
            ed[c, z] = zero3

    def unpack(z, _):
        for c in range(4):
            for t in range(2):
                own = mine[z, pl.ds(2 * c + t, 4, stride=8), :]
                off = other[z, pl.ds(2 * c + t, 4, stride=8), :]
                even = jnp.where(core == 0, own, off)
                odd = jnp.where(core == 0, off, own)
                if c < 3:
                    b3[c, z + 2, t, pl.ds(0, 4, stride=2), :] = even
                    b3[c, z + 2, t, pl.ds(1, 4, stride=2), :] = odd
                else:
                    rho3[z + 2, t, pl.ds(0, 4, stride=2), :] = even
                    rho3[z + 2, t, pl.ds(1, 4, stride=2), :] = odd
        return 0

    lax.fori_loop(0, 16, unpack, 0)
    level3 = Level(2, 128, False, True, gx3, gy3, gz3, m3, w3, ms3)
    coefficients(level3, rho3, 2, 18)
    scaled(w3, b3, ec, 2, 18)
    for src, dst in ((ec, ed), (ed, ec), (ec, ed)):
        smoothed(level3, b3, src, dst, 2, 18, s3, f3)

    row8 = lax.broadcasted_iota(jnp.int32, (8, 128), 0)
    parts = []
    for c in range(3):
        for k in range(5):
            v = ed[c, wide + k]
            r = jnp.stack([pltpu.roll(v[0], turn, 0), pltpu.roll(v[1], turn, 0)])
            to_natural(nat2, r, c, k)
            parts.append(jnp.where(row8 < 4, nat2[c, k, 0, 0:8], nat2[c, k, 0, 8:16]))
    up = times01(jnp.concatenate(parts, axis=0), copy_matrix(128, 128))
    for c in range(3):
        for k in range(5):
            tile = up[8 * (5 * c + k) : 8 * (5 * c + k) + 8]
            both = jnp.stack([tile, tile])
            for z in (2 * k + 2, 2 * k + 3):
                ua[c, z] = jnp.where(w2[0, z] > 0.0, ep2[c, z] + both, 0.0)
    level2 = Level(2, 128, False, False, gx2, gy2, gz2, m2, w2, None)
    smoothed(level2, b2, ua, ub, 3, 11, s2, f2)
    smoothed(level2, b2, ub, ua, 4, 10, s2, f2)

    parts = []
    for c in range(3):
        for k in range(6):
            to_natural(nat2, ua[c, 4 + k], c, k)
            parts += [nat2[c, k, 0, 0:8], nat2[c, k, 0, 8:16]]
    up = times01(jnp.concatenate(parts, axis=0), copy_matrix(128, 256))
    for c in range(3):
        for k in range(6):
            at = 16 * (6 * c + k)
            copy_rows(nat1, up[at + 8 : at + 16], 8, c, k)
            copy_rows(nat1, up[at : at + 8], 0, c, k)
            both = interleaved(nat1, 3, c, k)
            for z in (2 * k + 1, 2 * k + 2):
                if 2 <= z < 12:
                    va[c, z] = jnp.where(w1[0, z] > 0.0, ep1[c, z] + both, 0.0)
    level1 = Level(3, 256, False, False, gx1, gy1, gz1, m1, w1, None)
    smoothed(level1, b1, va, vb, 3, 11, s1, f1)
    smoothed(level1, b1, vb, va, 4, 10, s1, f1)

    row8 = lax.broadcasted_iota(jnp.int32, (8, 256), 0)
    parts = []
    for c in range(3):
        for k in range(6):
            to_natural(nat1, va[c, 4 + k], c, k)
            t = [join([nat1[c, k, j, 8 * r : 8 * r + 8] for j in range(2)]) for r in range(3)]
            parts += [t[0], jnp.where(row8 < 2, t[1], pltpu.roll(t[2], 4, 0))]
    up = times01(jnp.concatenate(parts, axis=0), copy_matrix(256, 384))
    for c in range(3):
        for k in range(6):
            at = 16 * (6 * c + k)
            copy_rows(nat0, up[at + 8 : at + 16], 16, c, k)
            copy_rows(nat0, up[at : at + 8], 0, c, k)
            both = interleaved(nat0, 3, c, k)
            for z in (2 * k + 1, 2 * k + 2):
                old = edge0[c] if z == 1 else edge9[c] if z == 12 else ep0[c, z]
                xa[c, z] = jnp.where(w0[0, z] > 0.0, old + both, 0.0)
    level0 = Level(3, 384, True, False, gx0, gy0, gz0, m0, w0, ms0)
    smoothed(level0, b0, xa, xb, 2, 12, s0, f0)

    def last(z, c, v, a):
        to_natural(nat0, v + w0[c, z] * (b0[c, z] - a), c, 0)
        for k in range(3):
            out[c, z - 3, :, 128 * k : 128 * (k + 1)] = nat0[c, 0, k, 0:16]

    operate(level0, xb, 3, 11, s0, f0, last)


def call(kernel, outs, scratch, args, flops, mib):
    vmem = pl.BlockSpec(memory_space=pltpu.VMEM)
    size = sum(4 * int(a.size) for a in args)
    size += sum(4 * functools.reduce(lambda p, q: p * q, s) for s in outs)
    return pl.pallas_call(
        kernel,
        out_shape=[jax.ShapeDtypeStruct(s, F32) for s in outs],
        in_specs=[pl.BlockSpec(memory_space=pltpu.SMEM)] + [vmem] * (len(args) - 1),
        out_specs=[vmem] * len(outs),
        scratch_shapes=[pltpu.VMEM(s, F32) for s in scratch],
        compiler_params=pltpu.CompilerParams(vmem_limit_bytes=mib * 1024 * 1024),
        cost_estimate=pl.CostEstimate(flops=flops, bytes_accessed=size, transcendentals=0),
    )(*args)


def shards(load, density):
    wide = lax.axis_index("wide")
    narrow = lax.axis_index(NARROW)
    turn = lax.rem(8 - narrow, 8)
    idx = jnp.stack([wide, narrow, turn, lax.axis_index("core")]).astype(jnp.int32)

    def next_rows(v):
        return lax.ppermute(v, NARROW, cyclic(8, -1))

    def previous_rows(v):
        return lax.ppermute(v, NARROW, cyclic(8, 1))

    def above(v, steps=1):
        return lax.ppermute(v, "wide", cyclic(16, -steps))

    def below(v, steps=1):
        return lax.ppermute(v, "wide", cyclic(16, steps))

    low = previous_rows(jnp.concatenate([load[:, :, 12:], density[None, :, 12:]], axis=0))
    high = next_rows(jnp.concatenate([load[:, :, :4], density[None, :, :4]], axis=0))
    rows = jnp.concatenate([high, low], axis=2)

    def planes(lz, dz):
        l = jnp.concatenate([load[:, lz], rows[:3, lz]], axis=2).reshape(6, 24, 384)
        d = jnp.concatenate([density[dz], rows[3, dz]], axis=1)
        return jnp.concatenate([l, d], axis=0)

    lo = below(planes(slice(6, 8), slice(5, 8)))
    hi = above(planes(slice(0, 2), slice(0, 3)))
    p0, c0 = (14, 3, 8, 384), (3, 8, 384)
    b0, gx0, gy0, gz0, m0, w0, ms0, ep0, edge_low, edge_high, l1 = call(
        down0,
        [(3,) + p0, p0, p0, p0, p0, (3,) + p0, p0, (3,) + p0, (3,) + c0, (3,) + c0, (9, 8, 384)],
        [(4, 14, 3, 24, 128), p0, (3,) + p0, (3, 4) + c0, (3, 4, 3, 24, 128), c0, (3,) + c0],
        [idx, load, density, rows, lo, hi],
        10**7,
        17,
    )

    after, before = next_rows(l1), previous_rows(l1)
    bz = jnp.concatenate([l1[:6], after[:6, :4], before[:6, 4:]], axis=1).reshape(96, 384)
    dz = jnp.concatenate([l1[6:], after[6:], before[6:]], axis=1).reshape(72, 384)
    slab = jnp.concatenate([bz, dz], axis=0)
    lo, hi = below(slab), above(slab)
    edge_low, edge_high, _ = lax.optimization_barrier((edge_low, edge_high, slab))
    edge9, edge0 = above(edge_low), below(edge_high)
    p1, c1 = (14, 3, 8, 256), (3, 8, 256)
    b1, gx1, gy1, gz1, m1, w1, ep1, l2 = call(
        down1,
        [(3,) + p1, p1, p1, p1, p1, (3,) + p1, (3,) + p1, (18, 8, 128)],
        [(4, 14, 2, 24, 128), p1, (3,) + p1, (3, 4) + c1, (3, 4, 2, 24, 128), c1, (3,) + c1],
        [idx, l1, after, before, lo, hi],
        10**7,
        10,
    )

    after, before = next_rows(l2), previous_rows(l2)
    own = jnp.concatenate([l2[:, :4], after[:, :6], before[:, 6:], before[:, :4]], axis=1)
    up = jnp.concatenate([own[4 * c : 4 * c + 2] for c in range(3)] + [own[12:14]], axis=0)
    down = jnp.concatenate([own[4 * c + 2 : 4 * c + 4] for c in range(3)] + [own[16:18]], axis=0)
    lo, hi, lo2, hi2 = below(up), above(down), below(up, 2), above(down, 2)
    p2, c2 = (14, 2, 8, 128), (2, 8, 128)
    b2, gx2, gy2, gz2, m2, w2, ep2, chunk = call(
        down2,
        [(3,) + p2, p2, p2, p2, p2, (3,) + p2, (3,) + p2, (8, 128)],
        [p2, (3,) + p2, c2, (3,) + c2],
        [idx, own, lo, lo2, hi, hi2],
        10**6,
        5,
    )

    everywhere = jnp.broadcast_to(chunk[None], (64, 8, 128))
    mine = lax.all_to_all(everywhere, ("wide", "y"), 0, 0).reshape(16, 32, 128)
    other = lax.ppermute(mine, "core", cyclic(2, 1))
    p3, c3 = (20, 2, 8, 128), (2, 8, 128)
    (out,) = call(
        rest,
        [(3, 8, 16, 384)],
        [p3, (3,) + p3, p3, p3, p3, p3, (3,) + p3, p3, (3,) + p3, (3,) + p3]
        + [(3, 6, 1, 16, 128), (3, 6, 2, 24, 128), (3, 6, 3, 32, 128)]
        + [c3, (3,) + c3, (3,) + p2, (3,) + p2, c2, (3,) + c2]
        + [(3,) + p1, (3,) + p1, c1, (3,) + c1, (3,) + p0, (3,) + p0, c0, (3,) + c0],
        [idx, mine, other, edge0, edge9]
        + [b2, gx2, gy2, gz2, m2, w2, ep2]
        + [b1, gx1, gy1, gz1, m1, w1, ep1]
        + [b0, gx0, gy0, gz0, m0, w0, ms0, ep0],
        10**8,
        28,
    )
    return out


def solution(mesh):
    split = Mesh(mesh.devices.reshape(16, 4, 2), ("wide",) + NARROW)
    in_specs = (P(None, "wide", NARROW, None), P("wide", NARROW, None))
    out_specs = P(None, "wide", NARROW, None)
    return jax.shard_map(shards, mesh=split, in_specs=in_specs, out_specs=out_specs, check_vma=False)
```

time: 538 us -> 130 us (0.24)
  the two profiles are of different devices: /device:TPU:115 before, /device:TPU:1 now
where the time goes in v2:
time: 130 us
  Pallas kernels  40.6 us (31%)
  waiting for transfers between devices  38.2 us (29%)
  starting transfers between devices  26.8 us (21%)
  blocking collectives  21.4 us (16%)
  local copies, waits for them, and re-layouts  2.3 us (2%)
    pallas_call x4, Pallas kernels, call(): pl.pallas_call(kernel, out_shape=[jax.ShapeDtypeStruct(s, F32) for s in o...  40.6 us
    all_to_all x1, blocking collectives, shards(): mine = lax.all_to_all(everywhere, ('wide', 'y'), 0, 0).reshape(16, 32, 128)  21.4 us
    ppermute x5, starting transfers between devices, above(): return lax.ppermute(v, 'wide', cyclic(16, -steps))  17.6 us
    ppermute x5, waiting for transfers between devices, above(): return lax.ppermute(v, 'wide', cyclic(16, -steps))  13.9 us
    ppermute x5, waiting for transfers between devices, below(): return lax.ppermute(v, 'wide', cyclic(16, steps))  11.9 us
    ppermute x3, waiting for transfers between devices, next_rows(): return lax.ppermute(v, NARROW, cyclic(8, -1))  7.5 us
    ppermute x3, starting transfers between devices, previous_rows(): return lax.ppermute(v, NARROW, cyclic(8, 1))  4.98 us
    ppermute x3, waiting for transfers between devices, previous_rows(): return lax.ppermute(v, NARROW, cyclic(8, 1))  4.94 us
  transfers between devices with their start and end apart: 17, of which 13 were waited for; matrix products, arithmetic and copies ran while one was open for 0% of the time, Pallas kernels for 0%

profile of v2, /device:TPU:1, one launch (start us, length us, event | category | flops | bytes accessed | tf_op | source)
XLA Modules:
  0.0 130.1 jit_solution(9239633431720393836)
XLA Ops:
  0.0 1.0 slice_bitcast_fusion.1
  1.0 1.1 fusion.7
  2.2 2.7 %collective-permute-start.1 = (f32[4,8,4,384]{3,2,1,0:T(4,128)S(1)}, f32[4,8,4,384]{3,2,1,0:T(4,128)S(1)}, u32[]{:S(2)}, u32[]{:S(2)}) collective-permute-start(f32[4,8,4,384]{3,2,1,0:T(4,128)S(1)} %pad_maximum_fusion.5), channel_id=1, source_target_pairs={{0,1},{1,2},{2,3},{3,4},{4,5},{5,6},{6,7},{7,0},{8,9},{9,10},{10,1... | collective-permute-start | bytes 589832 | tf_op jit(solution)/shard_map/ppermute | solution.py:561
  5.0 2.5 %collective-permute-done.1 = f32[4,8,4,384]{3,2,1,0:T(4,128)S(1)} collective-permute-done((f32[4,8,4,384]{3,2,1,0:T(4,128)S(1)}, f32[4,8,4,384]{3,2,1,0:T(4,128)S(1)}, u32[]{:S(2)}, u32[]{:S(2)}) %collective-permute-start.1) | collective-permute-done | bytes 196640 | tf_op jit(solution)/shard_map/ppermute | solution.py:561
  7.5 2.5 %collective-permute-done = f32[4,8,4,384]{3,2,1,0:T(4,128)S(1)} collective-permute-done((f32[4,8,4,384]{3,2,1,0:T(4,128)S(1)}, f32[4,8,4,384]{3,2,1,0:T(4,128)S(1)}, u32[]{:S(2)}, u32[]{:S(2)}) %collective-permute-start) | collective-permute-done | bytes 196640 | tf_op jit(solution)/shard_map/ppermute | solution.py:558
  10.2 6.0 %collective-permute-start.3 = (f32[9,24,384]{2,1,0:T(8,128)S(1)}, f32[9,24,384]{2,1,0:T(8,128)S(1)}, u32[]{:S(2)}, u32[]{:S(2)}) collective-permute-start(f32[9,24,384]{2,1,0:T(8,128)S(1)} %maximum_maximum_fusion.1), channel_id=1, source_target_pairs={{0,120},{8,0},{16,8},{24,16},{32,24},{40,32},{48,40},{56,48},{64,5... | collective-permute-start | bytes 995336 | tf_op jit(solution)/shard_map/ppermute | solution.py:564
  16.3 0.1 pad_add_fusion.idx
  16.4 0.1 pad_maximum_fusion.rows
  16.5 7.0 %collective-permute-done.3.hi = f32[9,24,384]{2,1,0:T(8,128)S(1)} collective-permute-done((f32[9,24,384]{2,1,0:T(8,128)S(1)}, f32[9,24,384]{2,1,0:T(8,128)S(1)}, u32[]{:S(2)}, u32[]{:S(2)}) %collective-permute-start.3) | collective-permute-done | bytes 331808 | tf_op jit(solution)/shard_map/ppermute | solution.py:564
  23.5 5.3 %collective-permute-done.2.lo = f32[9,24,384]{2,1,0:T(8,128)S(1)} collective-permute-done((f32[9,24,384]{2,1,0:T(8,128)S(1)}, f32[9,24,384]{2,1,0:T(8,128)S(1)}, u32[]{:S(2)}, u32[]{:S(2)}) %collective-permute-start.2) | collective-permute-done | bytes 331808 | tf_op jit(solution)/shard_map/ppermute | solution.py:567
  28.8 7.4 %shard_map.28 = (f32[3,14,3,8,384]{4,3,2,1,0:T(8,128)S(1)}, f32[14,3,8,384]{3,2,1,0:T(8,128)S(1)}, f32[14,3,8,384]{3,2,1,0:T(8,128)S(1)}, f32[14,3,8,384]{3,2,1,...) custom-call(s32[4]{0:T(128)S(1)} %pad_add_fusion.idx, ...), custom_call_target="tpu_custom_call" | custom-call | flops 10000000 | bytes 9400336 | tf_op jit(solution)/shard_map/pallas_call | solution.py:540
  36.2 1.3 %collective-permute-start.5 = (f32[9,8,384]{2,1,0:T(8,128)S(1)}, f32[9,8,384]{2,1,0:T(8,128)S(1)}, u32[]{:S(2)}, u32[]{:S(2)}) collective-permute-start(f32[9,8,384]{2,1,0:T(8,128)S(1)} %get-tuple-element.34.own), channel_id=1, source_target_pairs={{0,1},{1,2},{2,3},{3,4},{4,5},{5,6},{6,7},{7,0},{8,9},{9,10},{10,1... | collective-permute-start | bytes 331784 | tf_op jit(solution)/shard_map/ppermute | solution.py:561
  37.5 1.7 %collective-permute-done.5.before = f32[9,8,384]{2,1,0:T(8,128)S(1)} collective-permute-done((f32[9,8,384]{2,1,0:T(8,128)S(1)}, f32[9,8,384]{2,1,0:T(8,128)S(1)}, u32[]{:S(2)}, u32[]{:S(2)}) %collective-permute-start.5) | collective-permute-done | bytes 110624 | tf_op jit(solution)/shard_map/ppermute | solution.py:561
  39.2 2.7 %collective-permute-done.4.after = f32[9,8,384]{2,1,0:T(8,128)S(1)} collective-permute-done((f32[9,8,384]{2,1,0:T(8,128)S(1)}, f32[9,8,384]{2,1,0:T(8,128)S(1)}, u32[]{:S(2)}, u32[]{:S(2)}) %collective-permute-start.4) | collective-permute-done | bytes 110624 | tf_op jit(solution)/shard_map/ppermute | solution.py:558
  42.1 1.5 %collective-permute-start.6 = (f32[168,384]{1,0:T(8,128)S(1)}, f32[168,384]{1,0:T(8,128)S(1)}, u32[]{:S(2)}, u32[]{:S(2)}) collective-permute-start(f32[168,384]{1,0:T(8,128)S(1)} %pad_maximum_fusion.1), channel_id=1, source_target_pairs={{0,8},{8,16},{16,24},{24,32},{32,40},{40,48},{48,56},{56,64},{64,7... | collective-permute-start | bytes 774152 | tf_op jit(solution)/shard_map/ppermute | solution.py:567
  43.6 5.6 %collective-permute-done.7.hi = f32[168,384]{1,0:T(8,128)S(1)} collective-permute-done((f32[168,384]{1,0:T(8,128)S(1)}, f32[168,384]{1,0:T(8,128)S(1)}, u32[]{:S(2)}, u32[]{:S(2)}) %collective-permute-start.7) | collective-permute-done | bytes 258080 | tf_op jit(solution)/shard_map/ppermute | solution.py:564
  49.2 3.3 %collective-permute-done.6.lo = f32[168,384]{1,0:T(8,128)S(1)} collective-permute-done((f32[168,384]{1,0:T(8,128)S(1)}, f32[168,384]{1,0:T(8,128)S(1)}, u32[]{:S(2)}, u32[]{:S(2)}) %collective-permute-start.6) | collective-permute-done | bytes 258080 | tf_op jit(solution)/shard_map/ppermute | solution.py:567
  52.5 6.7 %shard_map.29 = (f32[3,14,3,8,256]{4,3,2,1,0:T(8,128)S(1)}, f32[14,3,8,256]{3,2,1,0:T(8,128)S(1)}, f32[14,3,8,256]{3,2,1,0:T(8,128)S(1)}, f32[14,3,8,256]{3,2,1,...) custom-call(s32[4]{0:T(128)S(1)} %pad_add_fusion.idx, ...), custom_call_target="tpu_custom_call" | custom-call | flops 10000000 | bytes 5394448 | tf_op jit(solution)/shard_map/pallas_call | solution.py:540
  59.2 1.0 collective-permute-start.9
  60.1 0.8 collective-permute-start.8
  60.9 0.7 collective-permute-done.9
  61.6 2.2 %collective-permute-done.8 = f32[18,8,128]{2,1,0:T(8,128)S(1)} collective-permute-done((f32[18,8,128]{2,1,0:T(8,128)S(1)}, f32[18,8,128]{2,1,0:T(8,128)S(1)}, u32[]{:S(2)}, u32[]{:S(2)}) %collective-permute-start.8) | collective-permute-done | bytes 73760 | tf_op jit(solution)/shard_map/ppermute | solution.py:558
  64.2 5.0 %collective-permute-start.13 = (f32[8,16,128]{2,1,0:T(8,128)S(1)}, f32[8,16,128]{2,1,0:T(8,128)S(1)}, u32[]{:S(2)}, u32[]{:S(2)}) collective-permute-start(f32[8,16,128]{2,1,0:T(8,128)S(1)} %pad_maximum_fusion.10), channel_id=1, source_target_pairs={{0,112},{8,120},{16,0},{24,8},{32,16},{40,24},{48,32},{56,40},{64,... | collective-permute-start | bytes 196616 | tf_op jit(solution)/shard_map/ppermute | solution.py:564
  69.2 2.0 %collective-permute-start.12 = (f32[8,16,128]{2,1,0:T(8,128)S(1)}, f32[8,16,128]{2,1,0:T(8,128)S(1)}, u32[]{:S(2)}, u32[]{:S(2)}) collective-permute-start(f32[8,16,128]{2,1,0:T(8,128)S(1)} %pad_maximum_fusion.10), channel_id=1, source_target_pairs={{0,120},{8,0},{16,8},{24,16},{32,24},{40,32},{48,40},{56,48},{64,5... | collective-permute-start | bytes 196616 | tf_op jit(solution)/shard_map/ppermute | solution.py:564
  71.3 1.3 %collective-permute-done.12.hi = f32[8,16,128]{2,1,0:T(8,128)S(1)} collective-permute-done((f32[8,16,128]{2,1,0:T(8,128)S(1)}, f32[8,16,128]{2,1,0:T(8,128)S(1)}, u32[]{:S(2)}, u32[]{:S(2)}) %collective-permute-start.12) | collective-permute-done | bytes 65568 | tf_op jit(solution)/shard_map/ppermute | solution.py:564
  72.6 4.6 %shard_map.30 = (f32[3,14,2,8,128]{4,3,2,1,0:T(8,128)S(1)}, f32[14,2,8,128]{3,2,1,0:T(8,128)S(1)}, f32[14,2,8,128]{3,2,1,0:T(8,128)S(1)}, f32[14,2,8,128]{3,2,1,...) custom-call(s32[4]{0:T(128)S(1)} %pad_add_fusion.idx, ...), custom_call_target="tpu_custom_call" | custom-call | flops 1000000 | bytes 1904656 | tf_op jit(solution)/shard_map/pallas_call | solution.py:540
  77.3 21.4 %all_to_all.5 = f32[64,8,128]{2,1,0:T(8,128)S(1)} all-to-all(f32[64,8,128]{2,1,0:T(8,128)S(1)} %broadcast_in_dim.14), channel_id=1, replica_groups=mesh['wide'=16,'y'=4,'core'=2] {'wide','y'}, dimensions={0} | all-to-all | bytes 524288 | tf_op jit(solution)/shard_map/all_to_all | solution.py:623
  98.7 1.5 %collective-permute-start.14 = (f32[16,32,128]{2,1,0:T(8,128)S(1)}, f32[16,32,128]{2,1,0:T(8,128)S(1)}, u32[]{:S(2)}, u32[]{:S(2)}) collective-permute-start(f32[16,32,128]{2,1,0:T(8,128)S(1)} %bitcast.18), channel_id=1, source_target_pairs={{0,1},{1,0},{2,3},{3,2},{4,5},{5,4},{6,7},{7,6},{8,9},{9,8},{10,11... | collective-permute-start | bytes 786440 | tf_op jit(solution)/shard_map/ppermute | solution.py:624
  100.2 0.3 collective-permute-start.15
  100.5 4.5 %collective-permute-start.16 = (f32[3,3,8,384]{3,2,1,0:T(8,128)S(1)}, f32[3,3,8,384]{3,2,1,0:T(8,128)S(1)}, u32[]{:S(2)}, u32[]{:S(2)}) collective-permute-start(f32[3,3,8,384]{3,2,1,0:T(8,128)S(1)} %get-tuple-element.40), channel_id=1, source_target_pairs={{0,120},{8,0},{16,8},{24,16},{32,24},{40,32},{48,40},{56,48},{64,5... | collective-permute-start | bytes 331784 | tf_op jit(solution)/shard_map/ppermute | solution.py:564
  104.9 3.2 %collective-permute-done.15.edge0 = f32[3,3,8,384]{3,2,1,0:T(8,128)S(1)} collective-permute-done((f32[3,3,8,384]{3,2,1,0:T(8,128)S(1)}, f32[3,3,8,384]{3,2,1,0:T(8,128)S(1)}, u32[]{:S(2)}, u32[]{:S(2)}) %collective-permute-start.15) | collective-permute-done | bytes 110624 | tf_op jit(solution)/shard_map/ppermute | solution.py:567
  108.2 21.9 %shard_map.31 = f32[3,8,16,384]{3,2,1,0:T(8,128)} custom-call(s32[4]{0:T(128)S(1)} %pad_add_fusion.idx, f32[16,32,128]{2,1,0:T(8,128)S(1)} %bitcast.19, f32[16,32,128]{2,1,0:T(8,128)S(1)} %collective-permute-done.14.other, f32[3,3,8,384]{3,2,1,0:T(8,128)S(1)} %collective-permute-done.15.edge0, f32[3,3,8,384]{3,2,1,0:T(8,128)S(1)} %collective-permute-done.16.edge9, ...), custom_call_target="tpu_custom_call" | custom-call | flops 100000000 | bytes 14524432 | tf_op jit(solution)/shard_map/pallas_call | solution.py:540
  (41 shorter events, 0.9 us)
Async XLA Ops:
  0.0 5.0 %copy-start.1 = (f32[8,16,384]{2,1,0:T(8,128)S(1)}, f32[8,16,384]{2,1,0:T(8,128)}, u32[]{:S(2)}) copy-start(f32[8,16,384]{2,1,0:T(8,128)} %dens.1) | copy-start | bytes 589828
  0.0 5.0 %copy-start = (f32[3,8,16,384]{3,2,1,0:T(8,128)S(1)}, f32[3,8,16,384]{3,2,1,0:T(8,128)}, u32[]{:S(2)}) copy-start(f32[3,8,16,384]{3,2,1,0:T(8,128)} %load.1) | copy-start | bytes 1769476
  2.2 5.3 %collective-permute-start.1 = (f32[4,8,4,384]{3,2,1,0:T(4,128)S(1)}, f32[4,8,4,384]{3,2,1,0:T(4,128)S(1)}, u32[]{:S(2)}, u32[]{:S(2)}) collective-permute-start(f32[4,8,4,384]{3,2,1,0:T(4,128)S(1)} %pad_maximum_fusion.5), channel_id=1, source_target_pairs={{0,1},{1,2},{2,3},{3,4},{4,5},{5,6},{6,7},{7,0},{8,9},{9,10},{10,1... | collective-permute-start | bytes 589832 | tf_op jit(solution)/shard_map/ppermute | solution.py:561
  5.0 5.1 %collective-permute-start = (f32[4,8,4,384]{3,2,1,0:T(4,128)S(1)}, f32[4,8,4,384]{3,2,1,0:T(4,128)S(1)}, u32[]{:S(2)}, u32[]{:S(2)}) collective-permute-start(f32[4,8,4,384]{3,2,1,0:T(4,128)S(1)} %pad_maximum_fusion.4), channel_id=1, source_target_pairs={{0,7},{1,0},{2,1},{3,2},{4,3},{5,4},{6,5},{7,6},{8,15},{9,8},{10,9... | collective-permute-start | bytes 589832 | tf_op jit(solution)/shard_map/ppermute | solution.py:558
  10.2 13.3 %collective-permute-start.3 = (f32[9,24,384]{2,1,0:T(8,128)S(1)}, f32[9,24,384]{2,1,0:T(8,128)S(1)}, u32[]{:S(2)}, u32[]{:S(2)}) collective-permute-start(f32[9,24,384]{2,1,0:T(8,128)S(1)} %maximum_maximum_fusion.1), channel_id=1, source_target_pairs={{0,120},{8,0},{16,8},{24,16},{32,24},{40,32},{48,40},{56,48},{64,5... | collective-permute-start | bytes 995336 | tf_op jit(solution)/shard_map/ppermute | solution.py:564
  16.2 12.5 %collective-permute-start.2 = (f32[9,24,384]{2,1,0:T(8,128)S(1)}, f32[9,24,384]{2,1,0:T(8,128)S(1)}, u32[]{:S(2)}, u32[]{:S(2)}) collective-permute-start(f32[9,24,384]{2,1,0:T(8,128)S(1)} %maximum_maximum_fusion), channel_id=1, source_target_pairs={{0,8},{8,16},{16,24},{24,32},{32,40},{40,48},{48,56},{56,64},{64,7... | collective-permute-start | bytes 995336 | tf_op jit(solution)/shard_map/ppermute | solution.py:567
  36.2 3.1 %collective-permute-start.5 = (f32[9,8,384]{2,1,0:T(8,128)S(1)}, f32[9,8,384]{2,1,0:T(8,128)S(1)}, u32[]{:S(2)}, u32[]{:S(2)}) collective-permute-start(f32[9,8,384]{2,1,0:T(8,128)S(1)} %get-tuple-element.34.own), channel_id=1, source_target_pairs={{0,1},{1,2},{2,3},{3,4},{4,5},{5,6},{6,7},{7,0},{8,9},{9,10},{10,1... | collective-permute-start | bytes 331784 | tf_op jit(solution)/shard_map/ppermute | solution.py:561
  37.5 4.5 %collective-permute-start.4 = (f32[9,8,384]{2,1,0:T(8,128)S(1)}, f32[9,8,384]{2,1,0:T(8,128)S(1)}, u32[]{:S(2)}, u32[]{:S(2)}) collective-permute-start(f32[9,8,384]{2,1,0:T(8,128)S(1)} %get-tuple-element.34.own), channel_id=1, source_target_pairs={{0,7},{1,0},{2,1},{3,2},{4,3},{5,4},{6,5},{7,6},{8,15},{9,8},{10,9... | collective-permute-start | bytes 331784 | tf_op jit(solution)/shard_map/ppermute | solution.py:558
  42.1 7.1 %collective-permute-start.7 = (f32[168,384]{1,0:T(8,128)S(1)}, f32[168,384]{1,0:T(8,128)S(1)}, u32[]{:S(2)}, u32[]{:S(2)}) collective-permute-start(f32[168,384]{1,0:T(8,128)S(1)} %pad_maximum_fusion.1), channel_id=1, source_target_pairs={{0,120},{8,0},{16,8},{24,16},{32,24},{40,32},{48,40},{56,48},{64,5... | collective-permute-start | bytes 774152 | tf_op jit(solution)/shard_map/ppermute | solution.py:564
  42.1 10.3 %collective-permute-start.6 = (f32[168,384]{1,0:T(8,128)S(1)}, f32[168,384]{1,0:T(8,128)S(1)}, u32[]{:S(2)}, u32[]{:S(2)}) collective-permute-start(f32[168,384]{1,0:T(8,128)S(1)} %pad_maximum_fusion.1), channel_id=1, source_target_pairs={{0,8},{8,16},{16,24},{24,32},{32,40},{40,48},{48,56},{56,64},{64,7... | collective-permute-start | bytes 774152 | tf_op jit(solution)/shard_map/ppermute | solution.py:567
  59.2 2.5 %collective-permute-start.9 = (f32[18,8,128]{2,1,0:T(8,128)S(1)}, f32[18,8,128]{2,1,0:T(8,128)S(1)}, u32[]{:S(2)}, u32[]{:S(2)}) collective-permute-start(f32[18,8,128]{2,1,0:T(8,128)S(1)} %get-tuple-element.35), channel_id=1, source_target_pairs={{0,1},{1,2},{2,3},{3,4},{4,5},{5,6},{6,7},{7,0},{8,9},{9,10},{10,1... | collective-permute-start | bytes 221192 | tf_op jit(solution)/shard_map/ppermute | solution.py:561
  60.1 3.8 %collective-permute-start.8 = (f32[18,8,128]{2,1,0:T(8,128)S(1)}, f32[18,8,128]{2,1,0:T(8,128)S(1)}, u32[]{:S(2)}, u32[]{:S(2)}) collective-permute-start(f32[18,8,128]{2,1,0:T(8,128)S(1)} %get-tuple-element.35), channel_id=1, source_target_pairs={{0,7},{1,0},{2,1},{3,2},{4,3},{5,4},{6,5},{7,6},{8,15},{9,8},{10,9... | collective-permute-start | bytes 221192 | tf_op jit(solution)/shard_map/ppermute | solution.py:558
  64.0 7.2 %collective-permute-start.11 = (f32[8,16,128]{2,1,0:T(8,128)S(1)}, f32[8,16,128]{2,1,0:T(8,128)S(1)}, u32[]{:S(2)}, u32[]{:S(2)}) collective-permute-start(f32[8,16,128]{2,1,0:T(8,128)S(1)} %pad_maximum_fusion.9), channel_id=1, source_target_pairs={{0,16},{8,24},{16,32},{24,40},{32,48},{40,56},{48,64},{56,72},{64,... | collective-permute-start | bytes 196616 | tf_op jit(solution)/shard_map/ppermute | solution.py:567
  64.1 7.2 %collective-permute-start.10 = (f32[8,16,128]{2,1,0:T(8,128)S(1)}, f32[8,16,128]{2,1,0:T(8,128)S(1)}, u32[]{:S(2)}, u32[]{:S(2)}) collective-permute-start(f32[8,16,128]{2,1,0:T(8,128)S(1)} %pad_maximum_fusion.9), channel_id=1, source_target_pairs={{0,8},{8,16},{16,24},{24,32},{32,40},{40,48},{48,56},{56,64},{64,7... | collective-permute-start | bytes 196616 | tf_op jit(solution)/shard_map/ppermute | solution.py:567
  64.2 7.1 %collective-permute-start.13 = (f32[8,16,128]{2,1,0:T(8,128)S(1)}, f32[8,16,128]{2,1,0:T(8,128)S(1)}, u32[]{:S(2)}, u32[]{:S(2)}) collective-permute-start(f32[8,16,128]{2,1,0:T(8,128)S(1)} %pad_maximum_fusion.10), channel_id=1, source_target_pairs={{0,112},{8,120},{16,0},{24,8},{32,16},{40,24},{48,32},{56,40},{64,... | collective-permute-start | bytes 196616 | tf_op jit(solution)/shard_map/ppermute | solution.py:564
  69.2 3.4 %collective-permute-start.12 = (f32[8,16,128]{2,1,0:T(8,128)S(1)}, f32[8,16,128]{2,1,0:T(8,128)S(1)}, u32[]{:S(2)}, u32[]{:S(2)}) collective-permute-start(f32[8,16,128]{2,1,0:T(8,128)S(1)} %pad_maximum_fusion.10), channel_id=1, source_target_pairs={{0,120},{8,0},{16,8},{24,16},{32,24},{40,32},{48,40},{56,48},{64,5... | collective-permute-start | bytes 196616 | tf_op jit(solution)/shard_map/ppermute | solution.py:564
  98.7 9.5 %collective-permute-start.14 = (f32[16,32,128]{2,1,0:T(8,128)S(1)}, f32[16,32,128]{2,1,0:T(8,128)S(1)}, u32[]{:S(2)}, u32[]{:S(2)}) collective-permute-start(f32[16,32,128]{2,1,0:T(8,128)S(1)} %bitcast.18), channel_id=1, source_target_pairs={{0,1},{1,0},{2,3},{3,2},{4,5},{5,4},{6,7},{7,6},{8,9},{9,8},{10,11... | collective-permute-start | bytes 786440 | tf_op jit(solution)/shard_map/ppermute | solution.py:624
  100.2 8.0 %collective-permute-start.15 = (f32[3,3,8,384]{3,2,1,0:T(8,128)S(1)}, f32[3,3,8,384]{3,2,1,0:T(8,128)S(1)}, u32[]{:S(2)}, u32[]{:S(2)}) collective-permute-start(f32[3,3,8,384]{3,2,1,0:T(8,128)S(1)} %get-tuple-element.39), channel_id=1, source_target_pairs={{0,8},{8,16},{16,24},{24,32},{32,40},{40,48},{48,56},{56,64},{64,7... | collective-permute-start | bytes 331784 | tf_op jit(solution)/shard_map/ppermute | solution.py:567
  100.5 7.7 %collective-permute-start.16 = (f32[3,3,8,384]{3,2,1,0:T(8,128)S(1)}, f32[3,3,8,384]{3,2,1,0:T(8,128)S(1)}, u32[]{:S(2)}, u32[]{:S(2)}) collective-permute-start(f32[3,3,8,384]{3,2,1,0:T(8,128)S(1)} %get-tuple-element.40), channel_id=1, source_target_pairs={{0,120},{8,0},{16,8},{24,16},{32,24},{40,32},{48,40},{56,48},{64,5... | collective-permute-start | bytes 331784 | tf_op jit(solution)/shard_map/ppermute | solution.py:564

commit v3 on v2

--- a/solution.py
+++ b/solution.py
@@ -96,11 +96,23 @@
         ref[(*at, k, pl.ds(start + 1, 8, stride=2), slice(None))] = part
 
 
+UNROLL = {2: 5, 6: 5, 9: 5}
+
+
+def planes_loop(level, lo, hi, body):
+    tiles, _, lanes = level.shape
+    unroll = UNROLL[tiles * (lanes // 128)]
+    while (hi - lo) % unroll:
+        unroll -= 1
+    lax.fori_loop(lo, hi, body, 0, unroll=unroll)
+
+
 class Level:
-    def __init__(self, tiles, lanes, wrap_x, wrap_y, gx, gy, gz, m, w, ms):
+    def __init__(self, tiles, lanes, wrap_x, wrap_y, gx, gxm, gy, gz, m, w, ms):
         self.shape = (tiles, 8, lanes)
         self.wrap_x, self.wrap_y = wrap_x, wrap_y
-        self.gx, self.gy, self.gz, self.m, self.w, self.ms = gx, gy, gz, m, w, ms
+        self.gx, self.gxm, self.gy, self.gz = gx, gxm, gy, gz
+        self.m, self.w, self.ms = m, w, ms
 
     def masks(self):
         tiles, _, lanes = self.shape
@@ -143,12 +155,14 @@
         m = g * (0.5 + d)
         mn = gn * (0.5 + dn)
         gx = 0.5 * (g + after_x(g))
+        gxm = 0.5 * (g + before_x(g))
         gy = 0.5 * (g + after_y(g))
         gz = 0.5 * (g + gn)
         total = MASS + gz + 0.5 * (g + gp)
         extra = None
         if level.wrap_x:
             gx = jnp.where(masks[3], 0.0, gx)
+            gxm = jnp.where(masks[2], 0.0, gxm)
             extra = jnp.where(masks[2] | masks[3], 0.5 * g, 0.0)
         if level.wrap_y:
             gy = jnp.where(masks[1], 0.0, gy)
@@ -157,9 +171,10 @@
         if extra is not None:
             level.ms[z] = MASS + extra
             total = total + extra
-        total = total + (gx + before_x(gx)) + (gy + before_y(gy)) + m
+        total = total + (gx + gxm) + (gy + before_y(gy)) + m
         inside = d > 0.0
         level.gx[z] = gx
+        level.gxm[z] = gxm
         level.gy[z] = gy
         level.gz[z] = gz
         level.m[z] = m
@@ -171,7 +186,7 @@
     level.gz[lo - 1] = 0.5 * (shear(lo - 1) + shear(lo))
     last = rho[hi]
     level.m[hi] = last * last * last * (0.5 + last)
-    lax.fori_loop(lo, hi, plane, 0)
+    planes_loop(level, lo, hi, plane)
 
 
 def operate(level, u, lo, hi, s_ref, f_ref, emit):
@@ -190,20 +205,20 @@
         s = s_ref[...]
         sn = stress(z + 1)
         s_ref[...] = sn
-        gx, gy, gz = level.gx[z], level.gy[z], level.gz[z]
+        gx, gxm, gy, gz = level.gx[z], level.gxm[z], level.gy[z], level.gz[z]
         for c in range(3):
             v = u[c, z]
             fz = gz * (v - u[c, z + 1])
-            fx = gx * (v - after_x(v))
+            fx = gx * (v - after_x(v)) + gxm * (v - before_x(v))
             fy = gy * (v - after_y(v))
             grad = s - (sn if c == 0 else level.after(s, c, masks))
             mass = MASS if level.ms is None else level.ms[z]
-            a = mass * v + (fz - f_ref[c]) + (fx - before_x(fx)) + (fy - before_y(fy)) + grad
+            a = mass * v + (fz - f_ref[c]) + fx + (fy - before_y(fy)) + grad
             f_ref[c] = fz
             emit(z, c, v, a)
         return 0
 
-    lax.fori_loop(lo, hi, plane, 0)
+    planes_loop(level, lo, hi, plane)
 
 
 def scaled(w, b, e, lo, hi):
@@ -212,7 +227,8 @@
             e[c, z] = w[c, z] * b[c, z]
         return 0
 
-    lax.fori_loop(lo, hi, plane, 0)
+    unroll = next(k for k in (4, 5, 3, 2, 1) if (hi - lo) % k == 0)
+    lax.fori_loop(lo, hi, plane, 0, unroll=unroll)
 
 
 def smoothed(level, b, src, dst, lo, hi, s_ref, f_ref):
@@ -233,7 +249,7 @@
 
 def down0(
     idx, load, dens, rows, lo, hi,
-    b, gx, gy, gz, m, w, ms, ep, edge_low, edge_high, l1,
+    b, gx, gxm, gy, gz, m, w, ms, ep, edge_low, edge_high, l1,
     nat, rho, e1, rz, back, s_ref, f_ref,
 ):
     wide, narrow = idx[0], idx[1]
@@ -253,7 +269,7 @@
     above = jnp.where(wide == 15, 0.0, 1.0) * grid
     for z in range(14):
         rho[z] = interleaved(nat, 3, 3, z) * (below if z < 3 else above if z > 10 else grid)
-    level = Level(3, 384, True, False, gx, gy, gz, m, w, ms)
+    level = Level(3, 384, True, False, gx, gxm, gy, gz, m, w, ms)
     coefficients(level, rho, 1, 13)
 
     def first(z, _):
@@ -263,11 +279,13 @@
             e1[c, z] = w[c, z] * v
         return 0
 
-    lax.fori_loop(1, 13, first, 0)
+    lax.fori_loop(1, 13, first, 0, unroll=3)
     smoothed(level, b, e1, ep, 2, 12, s_ref, f_ref)
     for c in range(3):
-        edge_low[c] = ep[c, 4]
-        edge_high[c] = ep[c, 9]
+        for t in range(3):
+            for k in range(3):
+                edge_low[c, t, k] = ep[c, 4, t, :, 128 * k : 128 * (k + 1)]
+                edge_high[c, t, k] = ep[c, 9, t, :, 128 * k : 128 * (k + 1)]
     rz[...] = jnp.zeros_like(rz)
 
     def residual(z, c, v, a):
@@ -303,7 +321,7 @@
 
 def down1(
     idx, own, after, before, lo, hi,
-    b, gx, gy, gz, m, w, ep, l2,
+    b, gx, gxm, gy, gz, m, w, ep, l2,
     nat, rho, e1, rz, back, s_ref, f_ref,
 ):
     wide, narrow = idx[0], idx[1]
@@ -342,7 +360,7 @@
     above = jnp.where(wide == 15, 0.0, 1.0) * grid
     for z in range(14):
         rho[z] = interleaved(nat, 3, 3, z) * (below if z < 5 else above if z > 8 else grid)
-    level = Level(3, 256, False, False, gx, gy, gz, m, w, None)
+    level = Level(3, 256, False, False, gx, gxm, gy, gz, m, w, None)
     coefficients(level, rho, 1, 13)
 
     def first(z, _):
@@ -352,7 +370,7 @@
             e1[c, z] = w[c, z] * v
         return 0
 
-    lax.fori_loop(1, 13, first, 0)
+    lax.fori_loop(1, 13, first, 0, unroll=3)
     smoothed(level, b, e1, ep, 2, 12, s_ref, f_ref)
     rz[...] = jnp.zeros_like(rz)
 
@@ -375,7 +393,7 @@
 
 def down2(
     idx, own, lo, lo2, hi, hi2,
-    b, gx, gy, gz, m, w, ep, chunk,
+    b, gx, gxm, gy, gz, m, w, ep, chunk,
     rho, e1, s_ref, f_ref,
 ):
     wide, narrow = idx[0], idx[1]
@@ -386,7 +404,9 @@
     grid = jnp.where((y >= 0) & (y < 32), 1.0, 0.0)
 
     def rows(ref, i):
-        return jnp.stack([ref[i, pl.ds(k, 8, stride=2), :] for k in range(2)])
+        if ref is own:
+            return jnp.stack([ref[i, pl.ds(k, 8, stride=2), :] for k in range(2)])
+        return jnp.stack([ref[pl.ds(16 * i + k, 8, stride=2), :] for k in range(2)])
 
     for z in range(14):
         if z < 4:
@@ -407,7 +427,7 @@
             else:
                 ref, i = (hi if z < 11 else hi2), 2 * c + (z - 9) % 2
             b[c, z] = rows(ref, i)
-    level = Level(2, 128, False, False, gx, gy, gz, m, w, None)
+    level = Level(2, 128, False, False, gx, gxm, gy, gz, m, w, None)
     coefficients(level, rho, 1, 13)
     scaled(w, b, e1, 1, 13)
     smoothed(level, b, e1, ep, 2, 12, s_ref, f_ref)
@@ -428,12 +448,12 @@
 
 
 def rest(
-    idx, mine, other, edge0, edge9,
-    b2, gx2, gy2, gz2, m2, w2, ep2,
-    b1, gx1, gy1, gz1, m1, w1, ep1,
-    b0, gx0, gy0, gz0, m0, w0, ms0, ep0,
+    idx, mine, other, lo, hi,
+    b2, gx2, gxm2, gy2, gz2, m2, w2, ep2,
+    b1, gx1, gxm1, gy1, gz1, m1, w1, ep1,
+    b0, gx0, gxm0, gy0, gz0, m0, w0, ms0, ep0,
     out,
-    rho3, b3, gx3, gy3, gz3, m3, w3, ms3, ec, ed,
+    rho3, b3, gx3, gxm3, gy3, gz3, m3, w3, ms3, ec, ed,
     nat2, nat1, nat0, s3, f3, ua, ub, s2, f2, va, vb, s1, f1, xa, xb, s0, f0,
 ):
     wide, turn, core = idx[0], idx[2], idx[3]
@@ -450,18 +470,13 @@
             for t in range(2):
                 own = mine[z, pl.ds(2 * c + t, 4, stride=8), :]
                 off = other[z, pl.ds(2 * c + t, 4, stride=8), :]
-                even = jnp.where(core == 0, own, off)
-                odd = jnp.where(core == 0, off, own)
-                if c < 3:
-                    b3[c, z + 2, t, pl.ds(0, 4, stride=2), :] = even
-                    b3[c, z + 2, t, pl.ds(1, 4, stride=2), :] = odd
-                else:
-                    rho3[z + 2, t, pl.ds(0, 4, stride=2), :] = even
-                    rho3[z + 2, t, pl.ds(1, 4, stride=2), :] = odd
+                ref = rho3.at[z + 2, t] if c == 3 else b3.at[c, z + 2, t]
+                ref[pl.ds(0, 4, stride=2), :] = jnp.where(core == 0, own, off)
+                ref[pl.ds(1, 4, stride=2), :] = jnp.where(core == 0, off, own)
         return 0
 
-    lax.fori_loop(0, 16, unpack, 0)
-    level3 = Level(2, 128, False, True, gx3, gy3, gz3, m3, w3, ms3)
+    lax.fori_loop(0, 16, unpack, 0, unroll=4)
+    level3 = Level(2, 128, False, True, gx3, gxm3, gy3, gz3, m3, w3, ms3)
     coefficients(level3, rho3, 2, 18)
     scaled(w3, b3, ec, 2, 18)
     for src, dst in ((ec, ed), (ed, ec), (ec, ed)):
@@ -482,7 +497,7 @@
             both = jnp.stack([tile, tile])
             for z in (2 * k + 2, 2 * k + 3):
                 ua[c, z] = jnp.where(w2[0, z] > 0.0, ep2[c, z] + both, 0.0)
-    level2 = Level(2, 128, False, False, gx2, gy2, gz2, m2, w2, None)
+    level2 = Level(2, 128, False, False, gx2, gxm2, gy2, gz2, m2, w2, None)
     smoothed(level2, b2, ua, ub, 3, 11, s2, f2)
     smoothed(level2, b2, ub, ua, 4, 10, s2, f2)
 
@@ -501,9 +516,13 @@
             for z in (2 * k + 1, 2 * k + 2):
                 if 2 <= z < 12:
                     va[c, z] = jnp.where(w1[0, z] > 0.0, ep1[c, z] + both, 0.0)
-    level1 = Level(3, 256, False, False, gx1, gy1, gz1, m1, w1, None)
+    level1 = Level(3, 256, False, False, gx1, gxm1, gy1, gz1, m1, w1, None)
     smoothed(level1, b1, va, vb, 3, 11, s1, f1)
     smoothed(level1, b1, vb, va, 4, 10, s1, f1)
+
+    def edge(ref, c):
+        at = [[128 + 8 * (9 * c + 3 * t + k) for k in range(3)] for t in range(3)]
+        return jnp.stack([join([ref[r : r + 8, :] for r in line]) for line in at])
 
     row8 = lax.broadcasted_iota(jnp.int32, (8, 256), 0)
     parts = []
@@ -520,9 +539,9 @@
             copy_rows(nat0, up[at : at + 8], 0, c, k)
             both = interleaved(nat0, 3, c, k)
             for z in (2 * k + 1, 2 * k + 2):
-                old = edge0[c] if z == 1 else edge9[c] if z == 12 else ep0[c, z]
+                old = edge(lo, c) if z == 1 else edge(hi, c) if z == 12 else ep0[c, z]
                 xa[c, z] = jnp.where(w0[0, z] > 0.0, old + both, 0.0)
-    level0 = Level(3, 384, True, False, gx0, gy0, gz0, m0, w0, ms0)
+    level0 = Level(3, 384, True, False, gx0, gxm0, gy0, gz0, m0, w0, ms0)
     smoothed(level0, b0, xa, xb, 2, 12, s0, f0)
 
     def last(z, c, v, a):
@@ -578,9 +597,9 @@
     lo = below(planes(slice(6, 8), slice(5, 8)))
     hi = above(planes(slice(0, 2), slice(0, 3)))
     p0, c0 = (14, 3, 8, 384), (3, 8, 384)
-    b0, gx0, gy0, gz0, m0, w0, ms0, ep0, edge_low, edge_high, l1 = call(
+    b0, gx0, gxm0, gy0, gz0, m0, w0, ms0, ep0, edge_low, edge_high, l1 = call(
         down0,
-        [(3,) + p0, p0, p0, p0, p0, (3,) + p0, p0, (3,) + p0, (3,) + c0, (3,) + c0, (9, 8, 384)],
+        [(3,) + p0, p0, p0, p0, p0, p0, (3,) + p0, p0, (3,) + p0, (3, 3, 3, 8, 128), (3, 3, 3, 8, 128), (9, 8, 384)],
         [(4, 14, 3, 24, 128), p0, (3,) + p0, (3, 4) + c0, (3, 4, 3, 24, 128), c0, (3,) + c0],
         [idx, load, density, rows, lo, hi],
         10**7,
@@ -592,12 +611,10 @@
     dz = jnp.concatenate([l1[6:], after[6:], before[6:]], axis=1).reshape(72, 384)
     slab = jnp.concatenate([bz, dz], axis=0)
     lo, hi = below(slab), above(slab)
-    edge_low, edge_high, _ = lax.optimization_barrier((edge_low, edge_high, slab))
-    edge9, edge0 = above(edge_low), below(edge_high)
     p1, c1 = (14, 3, 8, 256), (3, 8, 256)
-    b1, gx1, gy1, gz1, m1, w1, ep1, l2 = call(
+    b1, gx1, gxm1, gy1, gz1, m1, w1, ep1, l2 = call(
         down1,
-        [(3,) + p1, p1, p1, p1, p1, (3,) + p1, (3,) + p1, (18, 8, 128)],
+        [(3,) + p1, p1, p1, p1, p1, p1, (3,) + p1, (3,) + p1, (18, 8, 128)],
         [(4, 14, 2, 24, 128), p1, (3,) + p1, (3, 4) + c1, (3, 4, 2, 24, 128), c1, (3,) + c1],
         [idx, l1, after, before, lo, hi],
         10**7,
@@ -608,11 +625,14 @@
     own = jnp.concatenate([l2[:, :4], after[:, :6], before[:, 6:], before[:, :4]], axis=1)
     up = jnp.concatenate([own[4 * c : 4 * c + 2] for c in range(3)] + [own[12:14]], axis=0)
     down = jnp.concatenate([own[4 * c + 2 : 4 * c + 4] for c in range(3)] + [own[16:18]], axis=0)
-    lo, hi, lo2, hi2 = below(up), above(down), below(up, 2), above(down, 2)
+    up, down = up.reshape(128, 128), down.reshape(128, 128)
+    lo = below(jnp.concatenate([up, edge_high.reshape(216, 128)], axis=0))
+    hi = above(jnp.concatenate([down, edge_low.reshape(216, 128)], axis=0))
+    lo2, hi2 = below(up, 2), above(down, 2)
     p2, c2 = (14, 2, 8, 128), (2, 8, 128)
-    b2, gx2, gy2, gz2, m2, w2, ep2, chunk = call(
+    b2, gx2, gxm2, gy2, gz2, m2, w2, ep2, chunk = call(
         down2,
-        [(3,) + p2, p2, p2, p2, p2, (3,) + p2, (3,) + p2, (8, 128)],
+        [(3,) + p2, p2, p2, p2, p2, p2, (3,) + p2, (3,) + p2, (8, 128)],
         [p2, (3,) + p2, c2, (3,) + c2],
         [idx, own, lo, lo2, hi, hi2],
         10**6,
@@ -626,14 +646,14 @@
     (out,) = call(
         rest,
         [(3, 8, 16, 384)],
-        [p3, (3,) + p3, p3, p3, p3, p3, (3,) + p3, p3, (3,) + p3, (3,) + p3]
+        [p3, (3,) + p3, p3, p3, p3, p3, p3, (3,) + p3, p3, (3,) + p3, (3,) + p3]
         + [(3, 6, 1, 16, 128), (3, 6, 2, 24, 128), (3, 6, 3, 32, 128)]
         + [c3, (3,) + c3, (3,) + p2, (3,) + p2, c2, (3,) + c2]
         + [(3,) + p1, (3,) + p1, c1, (3,) + c1, (3,) + p0, (3,) + p0, c0, (3,) + c0],
-        [idx, mine, other, edge0, edge9]
-        + [b2, gx2, gy2, gz2, m2, w2, ep2]
-        + [b1, gx1, gy1, gz1, m1, w1, ep1]
-        + [b0, gx0, gy0, gz0, m0, w0, ms0, ep0],
+        [idx, mine, other, lo, hi]
+        + [b2, gx2, gxm2, gy2, gz2, m2, w2, ep2]
+        + [b1, gx1, gxm1, gy1, gz1, m1, w1, ep1]
+        + [b0, gx0, gxm0, gy0, gz0, m0, w0, ms0, ep0],
         10**8,
         28,
     )

time: 130 us -> 106 us (0.82)
  Pallas kernels: 40.6 us -> 19.7 us
  starting transfers between devices: 26.8 us -> 24.8 us
  waiting for transfers between devices: 38.2 us -> 36.4 us
    pallas_call x4, Pallas kernels: 40.6 us -> 19.7 us  [call(): pl.pallas_call(kernel, out_shape=[jax.ShapeDtypeStruct(s, F32) for s in o...]
    ppermute x5 -> x4, waiting for transfers between devices: 11.9 us -> 10.2 us  [below(): return lax.ppermute(v, 'wide', cyclic(16, steps))]
    ppermute x5 -> x4, starting transfers between devices: 17.6 us -> 16 us  [above(): return lax.ppermute(v, 'wide', cyclic(16, -steps))]
    ppermute x5 -> x4, waiting for transfers between devices: 13.9 us -> 12.6 us  [above(): return lax.ppermute(v, 'wide', cyclic(16, -steps))]
  transfers between devices with their start and end apart: 17 -> 15, of which waited for: 13 -> 12; matrix products, arithmetic and copies ran while one was open for 0% -> 0% of each run, Pallas kernels for 0% -> 0%
where the time goes in v3:
time: 106 us; the launch traced here: 105 us
  waiting for transfers between devices  36.4 us (34%)
  starting transfers between devices  24.8 us (23%)
  blocking collectives  21.4 us (20%)
  Pallas kernels  19.7 us (19%)
  local copies, waits for them, and re-layouts  2.29 us (2%)
    all_to_all x1, blocking collectives, shards(): mine = lax.all_to_all(everywhere, ('wide', 'y'), 0, 0).reshape(16, 32, 128)  21.4 us
    pallas_call x4, Pallas kernels, call(): pl.pallas_call(kernel, out_shape=[jax.ShapeDtypeStruct(s, F32) for s in o...  19.7 us
    ppermute x4, starting transfers between devices, above(): return lax.ppermute(v, 'wide', cyclic(16, -steps))  16 us
    ppermute x4, waiting for transfers between devices, above(): return lax.ppermute(v, 'wide', cyclic(16, -steps))  12.6 us
    ppermute x4, waiting for transfers between devices, below(): return lax.ppermute(v, 'wide', cyclic(16, steps))  10.2 us
    ppermute x3, waiting for transfers between devices, next_rows(): return lax.ppermute(v, NARROW, cyclic(8, -1))  7.5 us
    ppermute x3, starting transfers between devices, previous_rows(): return lax.ppermute(v, NARROW, cyclic(8, 1))  4.98 us
    ppermute x3, waiting for transfers between devices, previous_rows(): return lax.ppermute(v, NARROW, cyclic(8, 1))  4.94 us
  transfers between devices with their start and end apart: 15, of which 12 were waited for; matrix products, arithmetic and copies ran while one was open for 0% of the time, Pallas kernels for 0%

profile of v3, /device:TPU:1, one launch (start us, length us, event | category | flops | bytes accessed | tf_op | source)
XLA Modules:
  0.0 105.5 jit_solution(2219263021196142774)
XLA Ops:
  0.0 1.0 slice_bitcast_fusion.1
  1.0 1.1 %fusion.7 = (f32[3,8,4,384]{3,2,1,0:T(4,128)S(1)}, f32[3,8,4,384]{3,2,1,0:T(4,128)S(1)}) fusion(f32[3,8,16,384]{3,2,1,0:T(8,128)} %load.1), kind=kLoop, calls=%fused_computation.33 | loop fusion | bytes 589824 | tf_op jit(solution)/shard_map/slice | solution.py:589
  2.2 2.7 %collective-permute-start.1 = (f32[4,8,4,384]{3,2,1,0:T(4,128)S(1)}, f32[4,8,4,384]{3,2,1,0:T(4,128)S(1)}, u32[]{:S(2)}, u32[]{:S(2)}) collective-permute-start(f32[4,8,4,384]{3,2,1,0:T(4,128)S(1)} %pad_maximum_fusion.5), channel_id=1, source_target_pairs={{0,1},{1,2},{2,3},{3,4},{4,5},{5,6},{6,7},{7,0},{8,9},{9,10},{10,1... | collective-permute-start | bytes 589832 | tf_op jit(solution)/shard_map/ppermute | solution.py:580
  5.0 2.5 %collective-permute-done.1 = f32[4,8,4,384]{3,2,1,0:T(4,128)S(1)} collective-permute-done((f32[4,8,4,384]{3,2,1,0:T(4,128)S(1)}, f32[4,8,4,384]{3,2,1,0:T(4,128)S(1)}, u32[]{:S(2)}, u32[]{:S(2)}) %collective-permute-start.1) | collective-permute-done | bytes 196640 | tf_op jit(solution)/shard_map/ppermute | solution.py:580
  7.5 2.5 %collective-permute-done = f32[4,8,4,384]{3,2,1,0:T(4,128)S(1)} collective-permute-done((f32[4,8,4,384]{3,2,1,0:T(4,128)S(1)}, f32[4,8,4,384]{3,2,1,0:T(4,128)S(1)}, u32[]{:S(2)}, u32[]{:S(2)}) %collective-permute-start) | collective-permute-done | bytes 196640 | tf_op jit(solution)/shard_map/ppermute | solution.py:577
  10.2 6.0 %collective-permute-start.3 = (f32[9,24,384]{2,1,0:T(8,128)S(1)}, f32[9,24,384]{2,1,0:T(8,128)S(1)}, u32[]{:S(2)}, u32[]{:S(2)}) collective-permute-start(f32[9,24,384]{2,1,0:T(8,128)S(1)} %maximum_maximum_fusion.1), channel_id=1, source_target_pairs={{0,120},{8,0},{16,8},{24,16},{32,24},{40,32},{48,40},{56,48},{64,5... | collective-permute-start | bytes 995336 | tf_op jit(solution)/shard_map/ppermute | solution.py:583
  16.2 0.1 collective-permute-start.2
  16.3 0.1 pad_add_fusion.idx
  16.4 0.1 pad_maximum_fusion.rows
  16.5 7.0 %collective-permute-done.3.hi = f32[9,24,384]{2,1,0:T(8,128)S(1)} collective-permute-done((f32[9,24,384]{2,1,0:T(8,128)S(1)}, f32[9,24,384]{2,1,0:T(8,128)S(1)}, u32[]{:S(2)}, u32[]{:S(2)}) %collective-permute-start.3) | collective-permute-done | bytes 331808 | tf_op jit(solution)/shard_map/ppermute | solution.py:583
  23.5 5.3 %collective-permute-done.2.lo = f32[9,24,384]{2,1,0:T(8,128)S(1)} collective-permute-done((f32[9,24,384]{2,1,0:T(8,128)S(1)}, f32[9,24,384]{2,1,0:T(8,128)S(1)}, u32[]{:S(2)}, u32[]{:S(2)}) %collective-permute-start.2) | collective-permute-done | bytes 331808 | tf_op jit(solution)/shard_map/ppermute | solution.py:586
  28.8 4.6 %shard_map.28 = (f32[3,14,3,8,384]{4,3,2,1,0:T(8,128)S(1)}, f32[14,3,8,384]{3,2,1,0:T(8,128)S(1)}, f32[14,3,8,384]{3,2,1,0:T(8,128)S(1)}, f32[14,3,8,384]{3,2,1,...) custom-call(s32[4]{0:T(128)S(1)} %pad_add_fusion.idx, ...), custom_call_target="tpu_custom_call" | custom-call | flops 10000000 | bytes 9916432 | tf_op jit(solution)/shard_map/pallas_call | solution.py:559
  33.4 1.3 %collective-permute-start.5 = (f32[9,8,384]{2,1,0:T(8,128)S(1)}, f32[9,8,384]{2,1,0:T(8,128)S(1)}, u32[]{:S(2)}, u32[]{:S(2)}) collective-permute-start(f32[9,8,384]{2,1,0:T(8,128)S(1)} %get-tuple-element.35.own), channel_id=1, source_target_pairs={{0,1},{1,2},{2,3},{3,4},{4,5},{5,6},{6,7},{7,0},{8,9},{9,10},{10,1... | collective-permute-start | bytes 331784 | tf_op jit(solution)/shard_map/ppermute | solution.py:580
  34.7 1.7 %collective-permute-done.5.before = f32[9,8,384]{2,1,0:T(8,128)S(1)} collective-permute-done((f32[9,8,384]{2,1,0:T(8,128)S(1)}, f32[9,8,384]{2,1,0:T(8,128)S(1)}, u32[]{:S(2)}, u32[]{:S(2)}) %collective-permute-start.5) | collective-permute-done | bytes 110624 | tf_op jit(solution)/shard_map/ppermute | solution.py:580
  36.5 2.7 %collective-permute-done.4.after = f32[9,8,384]{2,1,0:T(8,128)S(1)} collective-permute-done((f32[9,8,384]{2,1,0:T(8,128)S(1)}, f32[9,8,384]{2,1,0:T(8,128)S(1)}, u32[]{:S(2)}, u32[]{:S(2)}) %collective-permute-start.4) | collective-permute-done | bytes 110624 | tf_op jit(solution)/shard_map/ppermute | solution.py:577
  39.3 0.1 collective-permute-start.7
  39.4 1.5 %collective-permute-start.6 = (f32[168,384]{1,0:T(8,128)S(1)}, f32[168,384]{1,0:T(8,128)S(1)}, u32[]{:S(2)}, u32[]{:S(2)}) collective-permute-start(f32[168,384]{1,0:T(8,128)S(1)} %pad_maximum_fusion.1), channel_id=1, source_target_pairs={{0,8},{8,16},{16,24},{24,32},{32,40},{40,48},{48,56},{56,64},{64,7... | collective-permute-start | bytes 774152 | tf_op jit(solution)/shard_map/ppermute | solution.py:586
  40.8 5.6 %collective-permute-done.7.hi = f32[168,384]{1,0:T(8,128)S(1)} collective-permute-done((f32[168,384]{1,0:T(8,128)S(1)}, f32[168,384]{1,0:T(8,128)S(1)}, u32[]{:S(2)}, u32[]{:S(2)}) %collective-permute-start.7) | collective-permute-done | bytes 258080 | tf_op jit(solution)/shard_map/ppermute | solution.py:583
  46.4 3.3 %collective-permute-done.6.lo = f32[168,384]{1,0:T(8,128)S(1)} collective-permute-done((f32[168,384]{1,0:T(8,128)S(1)}, f32[168,384]{1,0:T(8,128)S(1)}, u32[]{:S(2)}, u32[]{:S(2)}) %collective-permute-start.6) | collective-permute-done | bytes 258080 | tf_op jit(solution)/shard_map/ppermute | solution.py:586
  49.7 3.4 %shard_map.29 = (f32[3,14,3,8,256]{4,3,2,1,0:T(8,128)S(1)}, f32[14,3,8,256]{3,2,1,0:T(8,128)S(1)}, f32[14,3,8,256]{3,2,1,0:T(8,128)S(1)}, f32[14,3,8,256]{3,2,1,...) custom-call(s32[4]{0:T(128)S(1)} %pad_add_fusion.idx, ...), custom_call_target="tpu_custom_call" | custom-call | flops 10000000 | bytes 5738512 | tf_op jit(solution)/shard_map/pallas_call | solution.py:559
  53.1 1.0 collective-permute-start.9
  54.1 0.8 collective-permute-start.8
  54.8 0.7 collective-permute-done.9
  55.6 2.3 %collective-permute-done.8 = f32[18,8,128]{2,1,0:T(8,128)S(1)} collective-permute-done((f32[18,8,128]{2,1,0:T(8,128)S(1)}, f32[18,8,128]{2,1,0:T(8,128)S(1)}, u32[]{:S(2)}, u32[]{:S(2)}) %collective-permute-start.8) | collective-permute-done | bytes 73760 | tf_op jit(solution)/shard_map/ppermute | solution.py:577
  58.1 4.8 %collective-permute-start.12 = (f32[344,128]{1,0:T(8,128)S(1)}, f32[344,128]{1,0:T(8,128)S(1)}, u32[]{:S(2)}, u32[]{:S(2)}) collective-permute-start(f32[344,128]{1,0:T(8,128)S(1)} %pad_maximum_fusion.7), channel_id=1, source_target_pairs={{0,120},{8,0},{16,8},{24,16},{32,24},{40,32},{48,40},{56,48},{64,5... | collective-permute-start | bytes 528392 | tf_op jit(solution)/shard_map/ppermute | solution.py:583
  62.9 5.1 %collective-permute-start.13 = (f32[128,128]{1,0:T(8,128)S(1)}, f32[128,128]{1,0:T(8,128)S(1)}, u32[]{:S(2)}, u32[]{:S(2)}) collective-permute-start(f32[128,128]{1,0:T(8,128)S(1)} %bitcast.33), channel_id=1, source_target_pairs={{0,112},{8,120},{16,0},{24,8},{32,16},{40,24},{48,32},{56,40},{64,... | collective-permute-start | bytes 196616 | tf_op jit(solution)/shard_map/ppermute | solution.py:583
  68.0 1.6 %collective-permute-done.11.lo2 = f32[128,128]{1,0:T(8,128)S(1)} collective-permute-done((f32[128,128]{1,0:T(8,128)S(1)}, f32[128,128]{1,0:T(8,128)S(1)}, u32[]{:S(2)}, u32[]{:S(2)}) %collective-permute-start.11) | collective-permute-done | bytes 65568 | tf_op jit(solution)/shard_map/ppermute | solution.py:586
  69.7 1.6 %shard_map.30 = (f32[3,14,2,8,128]{4,3,2,1,0:T(8,128)S(1)}, f32[14,2,8,128]{3,2,1,0:T(8,128)S(1)}, f32[14,2,8,128]{3,2,1,0:T(8,128)S(1)}, f32[14,2,8,128]{3,2,1,...) custom-call(s32[4]{0:T(128)S(1)} %pad_add_fusion.idx, ...), custom_call_target="tpu_custom_call" | custom-call | flops 1000000 | bytes 2240528 | tf_op jit(solution)/shard_map/pallas_call | solution.py:559
  71.3 21.4 %all_to_all.5 = f32[64,8,128]{2,1,0:T(8,128)S(1)} all-to-all(f32[64,8,128]{2,1,0:T(8,128)S(1)} %broadcast_in_dim.14), channel_id=1, replica_groups=mesh['wide'=16,'y'=4,'core'=2] {'wide','y'}, dimensions={0} | all-to-all | bytes 524288 | tf_op jit(solution)/shard_map/all_to_all | solution.py:643
  92.7 1.5 %collective-permute-start.14 = (f32[16,32,128]{2,1,0:T(8,128)S(1)}, f32[16,32,128]{2,1,0:T(8,128)S(1)}, u32[]{:S(2)}, u32[]{:S(2)}) collective-permute-start(f32[16,32,128]{2,1,0:T(8,128)S(1)} %bitcast.22), channel_id=1, source_target_pairs={{0,1},{1,0},{2,3},{3,2},{4,5},{5,4},{6,7},{7,6},{8,9},{9,8},{10,11... | collective-permute-start | bytes 786440 | tf_op jit(solution)/shard_map/ppermute | solution.py:644
  94.2 1.2 %collective-permute-done.14.other = f32[16,32,128]{2,1,0:T(8,128)S(1)} collective-permute-done((f32[16,32,128]{2,1,0:T(8,128)S(1)}, f32[16,32,128]{2,1,0:T(8,128)S(1)}, u32[]{:S(2)}, u32[]{:S(2)}) %collective-permute-start.14) | collective-permute-done | bytes 262176 | tf_op jit(solution)/shard_map/ppermute | solution.py:644
  95.4 10.1 %shard_map.31 = f32[3,8,16,384]{3,2,1,0:T(8,128)} custom-call(s32[4]{0:T(128)S(1)} %pad_add_fusion.idx, f32[16,32,128]{2,1,0:T(8,128)S(1)} %bitcast.23, f32[16,32,128]{2,1,0:T(8,128)S(1)} %collective-permute-done.14.other, f32[344,128]{1,0:T(8,128)S(1)} %collective-permute-done.10.lo, f32[344,128]{1,0:T(8,128)S(1)} %collective-permute-done.12.hi, ...), custom_call_target="tpu_custom_call" | custom-call | flops 100000000 | bytes 15630352 | tf_op jit(solution)/shard_map/pallas_call | solution.py:559
  (39 shorter events, 0.6 us)
Async XLA Ops:
  0.0 5.0 %copy-start.1 = (f32[8,16,384]{2,1,0:T(8,128)S(1)}, f32[8,16,384]{2,1,0:T(8,128)}, u32[]{:S(2)}) copy-start(f32[8,16,384]{2,1,0:T(8,128)} %dens.1) | copy-start | bytes 589828
  0.0 5.0 %copy-start = (f32[3,8,16,384]{3,2,1,0:T(8,128)S(1)}, f32[3,8,16,384]{3,2,1,0:T(8,128)}, u32[]{:S(2)}) copy-start(f32[3,8,16,384]{3,2,1,0:T(8,128)} %load.1) | copy-start | bytes 1769476
  2.2 5.3 %collective-permute-start.1 = (f32[4,8,4,384]{3,2,1,0:T(4,128)S(1)}, f32[4,8,4,384]{3,2,1,0:T(4,128)S(1)}, u32[]{:S(2)}, u32[]{:S(2)}) collective-permute-start(f32[4,8,4,384]{3,2,1,0:T(4,128)S(1)} %pad_maximum_fusion.5), channel_id=1, source_target_pairs={{0,1},{1,2},{2,3},{3,4},{4,5},{5,6},{6,7},{7,0},{8,9},{9,10},{10,1... | collective-permute-start | bytes 589832 | tf_op jit(solution)/shard_map/ppermute | solution.py:580
  5.0 5.1 %collective-permute-start = (f32[4,8,4,384]{3,2,1,0:T(4,128)S(1)}, f32[4,8,4,384]{3,2,1,0:T(4,128)S(1)}, u32[]{:S(2)}, u32[]{:S(2)}) collective-permute-start(f32[4,8,4,384]{3,2,1,0:T(4,128)S(1)} %pad_maximum_fusion.4), channel_id=1, source_target_pairs={{0,7},{1,0},{2,1},{3,2},{4,3},{5,4},{6,5},{7,6},{8,15},{9,8},{10,9... | collective-permute-start | bytes 589832 | tf_op jit(solution)/shard_map/ppermute | solution.py:577
  10.2 13.3 %collective-permute-start.3 = (f32[9,24,384]{2,1,0:T(8,128)S(1)}, f32[9,24,384]{2,1,0:T(8,128)S(1)}, u32[]{:S(2)}, u32[]{:S(2)}) collective-permute-start(f32[9,24,384]{2,1,0:T(8,128)S(1)} %maximum_maximum_fusion.1), channel_id=1, source_target_pairs={{0,120},{8,0},{16,8},{24,16},{32,24},{40,32},{48,40},{56,48},{64,5... | collective-permute-start | bytes 995336 | tf_op jit(solution)/shard_map/ppermute | solution.py:583
  16.2 12.5 %collective-permute-start.2 = (f32[9,24,384]{2,1,0:T(8,128)S(1)}, f32[9,24,384]{2,1,0:T(8,128)S(1)}, u32[]{:S(2)}, u32[]{:S(2)}) collective-permute-start(f32[9,24,384]{2,1,0:T(8,128)S(1)} %maximum_maximum_fusion), channel_id=1, source_target_pairs={{0,8},{8,16},{16,24},{24,32},{32,40},{40,48},{48,56},{56,64},{64,7... | collective-permute-start | bytes 995336 | tf_op jit(solution)/shard_map/ppermute | solution.py:586
  33.4 3.1 %collective-permute-start.5 = (f32[9,8,384]{2,1,0:T(8,128)S(1)}, f32[9,8,384]{2,1,0:T(8,128)S(1)}, u32[]{:S(2)}, u32[]{:S(2)}) collective-permute-start(f32[9,8,384]{2,1,0:T(8,128)S(1)} %get-tuple-element.35.own), channel_id=1, source_target_pairs={{0,1},{1,2},{2,3},{3,4},{4,5},{5,6},{6,7},{7,0},{8,9},{9,10},{10,1... | collective-permute-start | bytes 331784 | tf_op jit(solution)/shard_map/ppermute | solution.py:580
  34.7 4.5 %collective-permute-start.4 = (f32[9,8,384]{2,1,0:T(8,128)S(1)}, f32[9,8,384]{2,1,0:T(8,128)S(1)}, u32[]{:S(2)}, u32[]{:S(2)}) collective-permute-start(f32[9,8,384]{2,1,0:T(8,128)S(1)} %get-tuple-element.35.own), channel_id=1, source_target_pairs={{0,7},{1,0},{2,1},{3,2},{4,3},{5,4},{6,5},{7,6},{8,15},{9,8},{10,9... | collective-permute-start | bytes 331784 | tf_op jit(solution)/shard_map/ppermute | solution.py:577
  39.3 7.1 %collective-permute-start.7 = (f32[168,384]{1,0:T(8,128)S(1)}, f32[168,384]{1,0:T(8,128)S(1)}, u32[]{:S(2)}, u32[]{:S(2)}) collective-permute-start(f32[168,384]{1,0:T(8,128)S(1)} %pad_maximum_fusion.1), channel_id=1, source_target_pairs={{0,120},{8,0},{16,8},{24,16},{32,24},{40,32},{48,40},{56,48},{64,5... | collective-permute-start | bytes 774152 | tf_op jit(solution)/shard_map/ppermute | solution.py:583
  39.4 10.3 %collective-permute-start.6 = (f32[168,384]{1,0:T(8,128)S(1)}, f32[168,384]{1,0:T(8,128)S(1)}, u32[]{:S(2)}, u32[]{:S(2)}) collective-permute-start(f32[168,384]{1,0:T(8,128)S(1)} %pad_maximum_fusion.1), channel_id=1, source_target_pairs={{0,8},{8,16},{16,24},{24,32},{32,40},{40,48},{48,56},{56,64},{64,7... | collective-permute-start | bytes 774152 | tf_op jit(solution)/shard_map/ppermute | solution.py:586
  53.1 2.5 %collective-permute-start.9 = (f32[18,8,128]{2,1,0:T(8,128)S(1)}, f32[18,8,128]{2,1,0:T(8,128)S(1)}, u32[]{:S(2)}, u32[]{:S(2)}) collective-permute-start(f32[18,8,128]{2,1,0:T(8,128)S(1)} %get-tuple-element.36), channel_id=1, source_target_pairs={{0,1},{1,2},{2,3},{3,4},{4,5},{5,6},{6,7},{7,0},{8,9},{9,10},{10,1... | collective-permute-start | bytes 221192 | tf_op jit(solution)/shard_map/ppermute | solution.py:580
  54.1 3.8 %collective-permute-start.8 = (f32[18,8,128]{2,1,0:T(8,128)S(1)}, f32[18,8,128]{2,1,0:T(8,128)S(1)}, u32[]{:S(2)}, u32[]{:S(2)}) collective-permute-start(f32[18,8,128]{2,1,0:T(8,128)S(1)} %get-tuple-element.36), channel_id=1, source_target_pairs={{0,7},{1,0},{2,1},{3,2},{4,3},{5,4},{6,5},{7,6},{8,15},{9,8},{10,9... | collective-permute-start | bytes 221192 | tf_op jit(solution)/shard_map/ppermute | solution.py:577
  58.0 11.7 %collective-permute-start.10 = (f32[344,128]{1,0:T(8,128)S(1)}, f32[344,128]{1,0:T(8,128)S(1)}, u32[]{:S(2)}, u32[]{:S(2)}) collective-permute-start(f32[344,128]{1,0:T(8,128)S(1)} %pad_maximum_fusion.6), channel_id=1, source_target_pairs={{0,8},{8,16},{16,24},{24,32},{32,40},{40,48},{48,56},{56,64},{64,7... | collective-permute-start | bytes 528392 | tf_op jit(solution)/shard_map/ppermute | solution.py:586
  58.1 11.6 %collective-permute-start.12 = (f32[344,128]{1,0:T(8,128)S(1)}, f32[344,128]{1,0:T(8,128)S(1)}, u32[]{:S(2)}, u32[]{:S(2)}) collective-permute-start(f32[344,128]{1,0:T(8,128)S(1)} %pad_maximum_fusion.7), channel_id=1, source_target_pairs={{0,120},{8,0},{16,8},{24,16},{32,24},{40,32},{48,40},{56,48},{64,5... | collective-permute-start | bytes 528392 | tf_op jit(solution)/shard_map/ppermute | solution.py:583
  62.9 6.7 %collective-permute-start.11 = (f32[128,128]{1,0:T(8,128)S(1)}, f32[128,128]{1,0:T(8,128)S(1)}, u32[]{:S(2)}, u32[]{:S(2)}) collective-permute-start(f32[128,128]{1,0:T(8,128)S(1)} %bitcast.31), channel_id=1, source_target_pairs={{0,16},{8,24},{16,32},{24,40},{32,48},{40,56},{48,64},{56,72},{64,... | collective-permute-start | bytes 196616 | tf_op jit(solution)/shard_map/ppermute | solution.py:586
  62.9 6.7 %collective-permute-start.13 = (f32[128,128]{1,0:T(8,128)S(1)}, f32[128,128]{1,0:T(8,128)S(1)}, u32[]{:S(2)}, u32[]{:S(2)}) collective-permute-start(f32[128,128]{1,0:T(8,128)S(1)} %bitcast.33), channel_id=1, source_target_pairs={{0,112},{8,120},{16,0},{24,8},{32,16},{40,24},{48,32},{56,40},{64,... | collective-permute-start | bytes 196616 | tf_op jit(solution)/shard_map/ppermute | solution.py:583
  92.7 2.6 %collective-permute-start.14 = (f32[16,32,128]{2,1,0:T(8,128)S(1)}, f32[16,32,128]{2,1,0:T(8,128)S(1)}, u32[]{:S(2)}, u32[]{:S(2)}) collective-permute-start(f32[16,32,128]{2,1,0:T(8,128)S(1)} %bitcast.22), channel_id=1, source_target_pairs={{0,1},{1,0},{2,3},{3,2},{4,5},{5,4},{6,7},{7,6},{8,9},{9,8},{10,11... | collective-permute-start | bytes 786440 | tf_op jit(solution)/shard_map/ppermute | solution.py:644

commit v4 on v3

--- a/solution.py
+++ b/solution.py
@@ -96,7 +96,7 @@
         ref[(*at, k, pl.ds(start + 1, 8, stride=2), slice(None))] = part
 
 
-UNROLL = {2: 5, 6: 5, 9: 5}
+UNROLL = {2: 5, 4: 5, 6: 5, 9: 5}
 
 
 def planes_loop(level, lo, hi, body):
@@ -254,16 +254,18 @@
 ):
     wide, narrow = idx[0], idx[1]
     for c in range(4):
-        for z in range(8):
-            own = dens[z] if c == 3 else load[c, z]
+        first = 0 if c == 3 else 1
+        for z in range(first, 14 - first):
+            if z < 3:
+                own = lo[2 * c + z - first]
+            elif z < 11:
+                own = dens[z - 3] if c == 3 else load[c, z - 3]
+            else:
+                own = hi[2 * c + z - 11]
+            halo = rows[12 * c + z - first]
             for k in range(3):
-                nat[c, z + 3, k, 0:16] = own[:, 128 * k : 128 * (k + 1)]
-                nat[c, z + 3, k, 16:24] = rows[c, z, :, 128 * k : 128 * (k + 1)]
-    for c in range(4):
-        for j in range(3 if c == 3 else 2):
-            for k in range(3):
-                nat[c, j + (0 if c == 3 else 1), k] = lo[2 * c + j, :, 128 * k : 128 * (k + 1)]
-                nat[c, j + 11, k] = hi[2 * c + j, :, 128 * k : 128 * (k + 1)]
+                nat[c, z, k, 0:16] = own[:, 128 * k : 128 * (k + 1)]
+                nat[c, z, k, 16:24] = halo[:, 128 * k : 128 * (k + 1)]
     grid = in_grid((3, 8, 384), 16, 4, narrow, 7)
     below = jnp.where(wide == 0, 0.0, 1.0) * grid
     above = jnp.where(wide == 15, 0.0, 1.0) * grid
@@ -282,10 +284,8 @@
     lax.fori_loop(1, 13, first, 0, unroll=3)
     smoothed(level, b, e1, ep, 2, 12, s_ref, f_ref)
     for c in range(3):
-        for t in range(3):
-            for k in range(3):
-                edge_low[c, t, k] = ep[c, 4, t, :, 128 * k : 128 * (k + 1)]
-                edge_high[c, t, k] = ep[c, 9, t, :, 128 * k : 128 * (k + 1)]
+        edge_low[c] = ep[c, 4]
+        edge_high[c] = ep[c, 9]
     rz[...] = jnp.zeros_like(rz)
 
     def residual(z, c, v, a):
@@ -320,8 +320,8 @@
 
 
 def down1(
-    idx, own, after, before, lo, hi,
-    b, gx, gxm, gy, gz, m, w, ep, l2,
+    idx, own, lo, hi, after, before,
+    b, gx, gxm, gy, gz, m, w, ep, chunk,
     nat, rho, e1, rz, back, s_ref, f_ref,
 ):
     wide, narrow = idx[0], idx[1]
@@ -335,23 +335,21 @@
         for q in range(3 if c == 3 else 2):
             i = 2 * c + q
             zo = 2 * q - 1 if c == 3 else 2 * q
-            for r, ref in ((0, own), (8, after), (16, before)):
-                for s, v in enumerate(halves(ref[i])):
-                    if 0 <= zo + s < 4:
-                        put(c, zo + s + 5, r, v)
-            for shift, ref in ((-4, lo), (4, hi)):
-                if c < 3:
-                    tiles = [halves(ref[pl.ds(16 * i + 8 * r, 8), :]) for r in range(2)]
-                else:
-                    tiles = [halves(ref[pl.ds(96 + 24 * q + 8 * r, 8), :]) for r in range(3)]
+            for source, (shift, ref) in enumerate(((0, own), (-4, lo), (4, hi))):
+                tiles = [halves(ref[i])]
+                j = 6 * source + i
+                at = j // 2 if c < 3 else 9 + 3 * source + q
+                for k, ref in enumerate((after, before)):
+                    v = ref[at]
+                    tiles.append(halves(pltpu.roll(v, 4, 0) if c < 3 and j % 2 != k else v))
                 for s in range(2):
                     z = zo + s + shift
-                    if 0 <= z < 4:
+                    if (0 <= z < 4) != (shift == 0):
                         continue
                     put(c, z + 5, 0, tiles[0][s])
                     if c < 3:
                         put(c, z + 5, 8, jnp.where(row < 4, tiles[1][s], 0.0))
-                        put(c, z + 5, 16, jnp.where(row >= 4, tiles[1][s], 0.0))
+                        put(c, z + 5, 16, jnp.where(row >= 4, tiles[2][s], 0.0))
                     else:
                         put(c, z + 5, 8, tiles[1][s])
                         put(c, z + 5, 16, tiles[2][s])
@@ -375,89 +373,54 @@
     rz[...] = jnp.zeros_like(rz)
 
     def residual(z, c, v, a):
-        k = ((z + 1) >> 1) - 2
+        k = ((z + 1) >> 1) - 3
         rz[c, k] = rz[c, k] + (b[c, z] - a)
 
-    operate(level, ep, 3, 11, s_ref, f_ref, residual)
+    operate(level, ep, 5, 9, s_ref, f_ref, residual)
     parts = []
     for c in range(3):
-        for k in range(4):
+        for k in range(2):
             to_natural(back, rz[c, k], c, k)
-            parts.append(jnp.where(row < 6, row_pairs(back, 0, c, k), row_pairs(back, 8, c, k)))
-    for k in range(6):
-        d = [row_pairs(nat, r, 3, 2 * k + 1) + row_pairs(nat, r, 3, 2 * k + 2) for r in (0, 8)]
-        parts.append(0.25 * jnp.where(row < 6, d[0], d[1]))
+            parts.append(row_pairs(back, 0, c, k))
+    for k in range(2):
+        d = row_pairs(nat, 0, 3, 2 * k + 5) + row_pairs(nat, 0, 3, 2 * k + 6)
+        parts.append(0.25 * d)
     out = times01(jnp.concatenate(parts, axis=0), pair_sum_matrix(256, 128, 0, 0.5))
-    l2[...] = out.reshape(len(parts), 8, 128)
-
-
-def down2(
-    idx, own, lo, lo2, hi, hi2,
-    b, gx, gxm, gy, gz, m, w, ep, chunk,
-    rho, e1, s_ref, f_ref,
-):
-    wide, narrow = idx[0], idx[1]
-    t = lax.broadcasted_iota(jnp.int32, (2, 8, 128), 0)
-    s = lax.broadcasted_iota(jnp.int32, (2, 8, 128), 1)
-    row = 2 * s + t
-    y = 4 * narrow + jnp.where(row < 10, row, row - 16)
-    grid = jnp.where((y >= 0) & (y < 32), 1.0, 0.0)
-
-    def rows(ref, i):
-        if ref is own:
-            return jnp.stack([ref[i, pl.ds(k, 8, stride=2), :] for k in range(2)])
-        return jnp.stack([ref[pl.ds(16 * i + k, 8, stride=2), :] for k in range(2)])
-
-    for z in range(14):
-        if z < 4:
-            ref, i = (lo2 if z < 2 else lo), 6 + z % 2
-        elif z < 10:
-            ref, i = own, 12 + z - 4
-        else:
-            ref, i = (hi if z < 12 else hi2), 6 + z % 2
-        zg = 2 * wide + z - 6
-        factor = jnp.where((zg >= 0) & (zg < 32), 1.0, 0.0)
-        rho[z] = rows(ref, i) * (grid * factor)
-    for c in range(3):
-        for z in range(1, 13):
-            if z < 5:
-                ref, i = (lo2 if z < 3 else lo), 2 * c + (z - 1) % 2
-            elif z < 9:
-                ref, i = own, 4 * c + z - 5
-            else:
-                ref, i = (hi if z < 11 else hi2), 2 * c + (z - 9) % 2
-            b[c, z] = rows(ref, i)
-    level = Level(2, 128, False, False, gx, gxm, gy, gz, m, w, None)
-    coefficients(level, rho, 1, 13)
-    scaled(w, b, e1, 1, 13)
-    smoothed(level, b, e1, ep, 2, 12, s_ref, f_ref)
     row8 = lax.broadcasted_iota(jnp.int32, (8, 128), 0)
-    sums = [0.25 * (rho[6] + rho[7])]
-
-    def residual(z, c, v, a):
-        e1[c, z] = b[c, z] - a
-
-    operate(level, ep, 6, 8, s_ref, f_ref, residual)
-    total = jnp.zeros((8, 128), F32)
+    lane = lax.broadcasted_iota(jnp.int32, (8, 128), 1)
+    four = []
     for c in range(4):
-        v = e1[c, 6] + e1[c, 7] if c < 3 else sums[0]
-        v = v[0] + v[1]
-        v = pltpu.roll(v, 2 * c, 0) if c else v
-        total = jnp.where((row8 >> 1) == c, v, total)
-    chunk[...] = times01(total, pair_sum_matrix(128, 128, 0, 0.5))
+        low, high = out[16 * c : 16 * c + 8], out[16 * c + 8 : 16 * c + 16]
+        four.append(jnp.where(row8 < 4, low, pltpu.roll(high, 4, 0)))
+    for c in range(3):
+        d = four[3] if c == 3 else pltpu.roll(four[3], 96 - 32 * c, 1)
+        chunk[c] = jnp.where(lane < 96, four[c], d)
 
 
 def rest(
     idx, mine, other, lo, hi,
-    b2, gx2, gxm2, gy2, gz2, m2, w2, ep2,
     b1, gx1, gxm1, gy1, gz1, m1, w1, ep1,
     b0, gx0, gxm0, gy0, gz0, m0, w0, ms0, ep0,
     out,
+    rho2, b2, gx2, gxm2, gy2, gz2, m2, w2, ms2, ea, ep2,
     rho3, b3, gx3, gxm3, gy3, gz3, m3, w3, ms3, ec, ed,
-    nat2, nat1, nat0, s3, f3, ua, ub, s2, f2, va, vb, s1, f1, xa, xb, s0, f0,
+    rz, nat2, nat1, nat0, s3, f3, ua, ub, s2, f2, va, vb, s1, f1, xa, xb, s0, f0,
 ):
-    wide, turn, core = idx[0], idx[2], idx[3]
+    wide, narrow = idx[0], idx[1]
+    core = narrow & 1
+    zero2 = jnp.zeros((4, 8, 128), F32)
     zero3 = jnp.zeros((2, 8, 128), F32)
+
+    def outside(i, _):
+        z = jnp.where(i < 4, i, i + 32)
+        for ref in (rho2, gx2, gxm2, gy2, gz2, m2, ms2):
+            ref[z] = zero2
+        for ref in (b2, w2, ea, ep2):
+            for c in range(3):
+                ref[c, z] = zero2
+        return 0
+
+    lax.fori_loop(0, 8, outside, 0)
     for z in (1, 18):
         rho3[z] = zero3
     for z in (0, 1, 18, 19):
@@ -465,47 +428,88 @@
             ec[c, z] = zero3
             ed[c, z] = zero3
 
-    def unpack(z, _):
-        for c in range(4):
-            for t in range(2):
-                own = mine[z, pl.ds(2 * c + t, 4, stride=8), :]
-                off = other[z, pl.ds(2 * c + t, 4, stride=8), :]
-                ref = rho3.at[z + 2, t] if c == 3 else b3.at[c, z + 2, t]
+    lane = lax.broadcasted_iota(jnp.int32, (4, 8, 128), 2)
+
+    def unpack(w, _):
+        for c in range(3):
+            for r in range(8):
+                own = mine[w, pl.ds(8 * c + r, 4, stride=24), :]
+                off = other[w, pl.ds(8 * c + r, 4, stride=24), :]
+                ref = ea.at[c, 2 * w + 4 + r // 4, r % 4]
                 ref[pl.ds(0, 4, stride=2), :] = jnp.where(core == 0, own, off)
                 ref[pl.ds(1, 4, stride=2), :] = jnp.where(core == 0, off, own)
         return 0
 
-    lax.fori_loop(0, 16, unpack, 0, unroll=4)
+    lax.fori_loop(0, 16, unpack, 0)
+
+    def split(z, _):
+        d = jnp.zeros((4, 8, 128), F32)
+        for c in range(3):
+            v = ea[c, z]
+            b2[c, z] = jnp.where(lane < 96, v, 0.0)
+            moved = pltpu.roll(v, 32 + 32 * c, 2) if c < 3 else v
+            d = jnp.where((lane >> 5) == c, moved, d)
+        rho2[z] = d
+        return 0
+
+    lax.fori_loop(4, 36, split, 0, unroll=4)
+
+    level2 = Level(4, 128, False, True, gx2, gxm2, gy2, gz2, m2, w2, ms2)
+    coefficients(level2, rho2, 4, 36)
+    scaled(w2, b2, ea, 4, 36)
+    smoothed(level2, b2, ea, ep2, 4, 36, s2, f2)
+    rz[...] = jnp.zeros_like(rz)
+
+    def residual(z, c, v, a):
+        r = b2[c, z] - a
+        k = (z >> 1) - 2
+        rz[c, k] = rz[c, k] + jnp.stack([r[0] + r[1], r[2] + r[3]])
+
+    operate(level2, ep2, 4, 36, s2, f2, residual)
+
+    def coarse_density(z, _):
+        d = 0.25 * (rho2[2 * z + 4] + rho2[2 * z + 5])
+        rz[3, z] = jnp.stack([d[0] + d[1], d[2] + d[3]])
+        return 0
+
+    lax.fori_loop(0, 16, coarse_density, 0, unroll=4)
+    half = pair_sum_matrix(128, 128, 0, 0.5)
+    for c in range(4):
+        v = times01(rz[c].reshape(256, 128), half).reshape(16, 2, 8, 128)
+        if c < 3:
+            b3[c, 2:18] = v
+        else:
+            rho3[2:18] = v
+
     level3 = Level(2, 128, False, True, gx3, gxm3, gy3, gz3, m3, w3, ms3)
     coefficients(level3, rho3, 2, 18)
     scaled(w3, b3, ec, 2, 18)
     for src, dst in ((ec, ed), (ed, ec), (ec, ed)):
         smoothed(level3, b3, src, dst, 2, 18, s3, f3)
 
-    row8 = lax.broadcasted_iota(jnp.int32, (8, 128), 0)
+    near = pl.ds(2 * wide, 10)
+    gx2, gxm2, gy2, gz2, m2, ms2 = (v.at[near] for v in (gx2, gxm2, gy2, gz2, m2, ms2))
+    b2, w2, ep2 = (v.at[:, near] for v in (b2, w2, ep2))
+    parts = [ed[c, wide + k].reshape(16, 128) for c in range(3) for k in range(5)]
+    up = times01(jnp.concatenate(parts, axis=0), copy_matrix(128, 128))
+    for c in range(3):
+        for k in range(5):
+            at = 16 * (5 * c + k)
+            t = [up[at : at + 8], up[at + 8 : at + 16]]
+            both = jnp.stack([t[0], t[0], t[1], t[1]])
+            for z in (2 * k, 2 * k + 1):
+                ua[c, z] = jnp.where(w2[0, z] > 0.0, ep2[c, z] + both, 0.0)
+    at2 = Level(4, 128, False, True, gx2, gxm2, gy2, gz2, m2, w2, ms2)
+    smoothed(at2, b2, ua, ub, 1, 9, s2, f2)
+    smoothed(at2, b2, ub, ua, 2, 8, s2, f2)
+
+    turn = (8 - narrow) & 7
     parts = []
     for c in range(3):
-        for k in range(5):
-            v = ed[c, wide + k]
-            r = jnp.stack([pltpu.roll(v[0], turn, 0), pltpu.roll(v[1], turn, 0)])
-            to_natural(nat2, r, c, k)
-            parts.append(jnp.where(row8 < 4, nat2[c, k, 0, 0:8], nat2[c, k, 0, 8:16]))
-    up = times01(jnp.concatenate(parts, axis=0), copy_matrix(128, 128))
-    for c in range(3):
-        for k in range(5):
-            tile = up[8 * (5 * c + k) : 8 * (5 * c + k) + 8]
-            both = jnp.stack([tile, tile])
-            for z in (2 * k + 2, 2 * k + 3):
-                ua[c, z] = jnp.where(w2[0, z] > 0.0, ep2[c, z] + both, 0.0)
-    level2 = Level(2, 128, False, False, gx2, gxm2, gy2, gz2, m2, w2, None)
-    smoothed(level2, b2, ua, ub, 3, 11, s2, f2)
-    smoothed(level2, b2, ub, ua, 4, 10, s2, f2)
-
-    parts = []
-    for c in range(3):
         for k in range(6):
-            to_natural(nat2, ua[c, 4 + k], c, k)
-            parts += [nat2[c, k, 0, 0:8], nat2[c, k, 0, 8:16]]
+            v = ua[c, 2 + k]
+            to_natural(nat2, jnp.stack([pltpu.roll(v[t], turn, 0) for t in range(4)]), c, k)
+            parts += [nat2[c, k, 0, 0:8], nat2[c, k, 0, 24:32]]
     up = times01(jnp.concatenate(parts, axis=0), copy_matrix(128, 256))
     for c in range(3):
         for k in range(6):
@@ -520,10 +524,6 @@
     smoothed(level1, b1, va, vb, 3, 11, s1, f1)
     smoothed(level1, b1, vb, va, 4, 10, s1, f1)
 
-    def edge(ref, c):
-        at = [[128 + 8 * (9 * c + 3 * t + k) for k in range(3)] for t in range(3)]
-        return jnp.stack([join([ref[r : r + 8, :] for r in line]) for line in at])
-
     row8 = lax.broadcasted_iota(jnp.int32, (8, 256), 0)
     parts = []
     for c in range(3):
@@ -539,7 +539,11 @@
             copy_rows(nat0, up[at : at + 8], 0, c, k)
             both = interleaved(nat0, 3, c, k)
             for z in (2 * k + 1, 2 * k + 2):
-                old = edge(lo, c) if z == 1 else edge(hi, c) if z == 12 else ep0[c, z]
+                if z in (1, 12):
+                    ref = lo if z == 1 else hi
+                    old = jnp.stack([ref[9 + 3 * c + t] for t in range(3)])
+                else:
+                    old = ep0[c, z]
                 xa[c, z] = jnp.where(w0[0, z] > 0.0, old + both, 0.0)
     level0 = Level(3, 384, True, False, gx0, gxm0, gy0, gz0, m0, w0, ms0)
     smoothed(level0, b0, xa, xb, 2, 12, s0, f0)
@@ -570,8 +574,8 @@
 def shards(load, density):
     wide = lax.axis_index("wide")
     narrow = lax.axis_index(NARROW)
-    turn = lax.rem(8 - narrow, 8)
-    idx = jnp.stack([wide, narrow, turn, lax.axis_index("core")]).astype(jnp.int32)
+    idx = jnp.stack([wide, narrow]).astype(jnp.int32)
+    load, density, idx = lax.optimization_barrier((load, density, idx))
 
     def next_rows(v):
         return lax.ppermute(v, NARROW, cyclic(8, -1))
@@ -585,77 +589,66 @@
     def below(v, steps=1):
         return lax.ppermute(v, "wide", cyclic(16, steps))
 
-    low = previous_rows(jnp.concatenate([load[:, :, 12:], density[None, :, 12:]], axis=0))
-    high = next_rows(jnp.concatenate([load[:, :, :4], density[None, :, :4]], axis=0))
-    rows = jnp.concatenate([high, low], axis=2)
-
-    def planes(lz, dz):
-        l = jnp.concatenate([load[:, lz], rows[:3, lz]], axis=2).reshape(6, 24, 384)
-        d = jnp.concatenate([density[dz], rows[3, dz]], axis=1)
-        return jnp.concatenate([l, d], axis=0)
-
-    lo = below(planes(slice(6, 8), slice(5, 8)))
-    hi = above(planes(slice(0, 2), slice(0, 3)))
+    lo = below(jnp.concatenate([load[:, 6:].reshape(6, 16, 384), density[5:]], axis=0))
+    hi = above(jnp.concatenate([load[:, :2].reshape(6, 16, 384), density[:3]], axis=0))
+
+    def rows_of(at):
+        parts = []
+        for c in range(4):
+            own = density if c == 3 else load[c]
+            end = 9 if c == 3 else 2 * c + 2
+            parts += [lo[2 * c : end, at], own[:, at], hi[2 * c : end, at]]
+        return jnp.concatenate(parts, axis=0)
+
+    low, high = previous_rows(rows_of(slice(12, 16))), next_rows(rows_of(slice(0, 4)))
+    rows = jnp.concatenate([high, low], axis=1)
     p0, c0 = (14, 3, 8, 384), (3, 8, 384)
     b0, gx0, gxm0, gy0, gz0, m0, w0, ms0, ep0, edge_low, edge_high, l1 = call(
         down0,
-        [(3,) + p0, p0, p0, p0, p0, p0, (3,) + p0, p0, (3,) + p0, (3, 3, 3, 8, 128), (3, 3, 3, 8, 128), (9, 8, 384)],
+        [(3,) + p0, p0, p0, p0, p0, p0, (3,) + p0, p0, (3,) + p0, (3,) + c0, (3,) + c0, (9, 8, 384)],
         [(4, 14, 3, 24, 128), p0, (3,) + p0, (3, 4) + c0, (3, 4, 3, 24, 128), c0, (3,) + c0],
         [idx, load, density, rows, lo, hi],
         10**7,
         17,
     )
 
-    after, before = next_rows(l1), previous_rows(l1)
-    bz = jnp.concatenate([l1[:6], after[:6, :4], before[:6, 4:]], axis=1).reshape(96, 384)
-    dz = jnp.concatenate([l1[6:], after[6:], before[6:]], axis=1).reshape(72, 384)
-    slab = jnp.concatenate([bz, dz], axis=0)
-    lo, hi = below(slab), above(slab)
+    lo = below(jnp.concatenate([l1, edge_high.reshape(9, 8, 384)], axis=0))
+    hi = above(jnp.concatenate([l1, edge_low.reshape(9, 8, 384)], axis=0))
+
+    def level1_rows(at):
+        b = [jnp.concatenate([v[0:6:2, at], v[1:6:2, at]], axis=1) for v in (l1, lo, hi)]
+        return jnp.concatenate(b + [v[6:9] for v in (l1, lo, hi)], axis=0)
+
+    after, before = next_rows(level1_rows(slice(0, 4))), previous_rows(level1_rows(slice(4, 8)))
     p1, c1 = (14, 3, 8, 256), (3, 8, 256)
-    b1, gx1, gxm1, gy1, gz1, m1, w1, ep1, l2 = call(
+    b1, gx1, gxm1, gy1, gz1, m1, w1, ep1, chunk = call(
         down1,
-        [(3,) + p1, p1, p1, p1, p1, p1, (3,) + p1, (3,) + p1, (18, 8, 128)],
+        [(3,) + p1, p1, p1, p1, p1, p1, (3,) + p1, (3,) + p1, (3, 8, 128)],
         [(4, 14, 2, 24, 128), p1, (3,) + p1, (3, 4) + c1, (3, 4, 2, 24, 128), c1, (3,) + c1],
-        [idx, l1, after, before, lo, hi],
+        [idx, l1, lo, hi, after, before],
         10**7,
         10,
     )
 
-    after, before = next_rows(l2), previous_rows(l2)
-    own = jnp.concatenate([l2[:, :4], after[:, :6], before[:, 6:], before[:, :4]], axis=1)
-    up = jnp.concatenate([own[4 * c : 4 * c + 2] for c in range(3)] + [own[12:14]], axis=0)
-    down = jnp.concatenate([own[4 * c + 2 : 4 * c + 4] for c in range(3)] + [own[16:18]], axis=0)
-    up, down = up.reshape(128, 128), down.reshape(128, 128)
-    lo = below(jnp.concatenate([up, edge_high.reshape(216, 128)], axis=0))
-    hi = above(jnp.concatenate([down, edge_low.reshape(216, 128)], axis=0))
-    lo2, hi2 = below(up, 2), above(down, 2)
-    p2, c2 = (14, 2, 8, 128), (2, 8, 128)
-    b2, gx2, gxm2, gy2, gz2, m2, w2, ep2, chunk = call(
-        down2,
-        [(3,) + p2, p2, p2, p2, p2, p2, (3,) + p2, (3,) + p2, (8, 128)],
-        [p2, (3,) + p2, c2, (3,) + c2],
-        [idx, own, lo, lo2, hi, hi2],
-        10**6,
-        5,
-    )
-
-    everywhere = jnp.broadcast_to(chunk[None], (64, 8, 128))
-    mine = lax.all_to_all(everywhere, ("wide", "y"), 0, 0).reshape(16, 32, 128)
+    chunks = jnp.broadcast_to(chunk[None], (64, 3, 8, 128))
+    mine = lax.all_to_all(chunks, ("wide", "y"), 0, 0).reshape(16, 96, 128)
     other = lax.ppermute(mine, "core", cyclic(2, 1))
+    p2, c2 = (40, 4, 8, 128), (4, 8, 128)
+    u2 = (3, 10, 4, 8, 128)
     p3, c3 = (20, 2, 8, 128), (2, 8, 128)
     (out,) = call(
         rest,
         [(3, 8, 16, 384)],
-        [p3, (3,) + p3, p3, p3, p3, p3, p3, (3,) + p3, p3, (3,) + p3, (3,) + p3]
-        + [(3, 6, 1, 16, 128), (3, 6, 2, 24, 128), (3, 6, 3, 32, 128)]
-        + [c3, (3,) + c3, (3,) + p2, (3,) + p2, c2, (3,) + c2]
+        [p2, (3,) + p2, p2, p2, p2, p2, p2, (3,) + p2, p2, (3,) + p2, (3,) + p2]
+        + [p3, (3,) + p3, p3, p3, p3, p3, p3, (3,) + p3, p3, (3,) + p3, (3,) + p3]
+        + [(4, 16, 2, 8, 128), (3, 6, 1, 32, 128), (3, 6, 2, 24, 128), (3, 6, 3, 32, 128)]
+        + [c3, (3,) + c3, u2, u2, c2, (3,) + c2]
         + [(3,) + p1, (3,) + p1, c1, (3,) + c1, (3,) + p0, (3,) + p0, c0, (3,) + c0],
         [idx, mine, other, lo, hi]
-        + [b2, gx2, gxm2, gy2, gz2, m2, w2, ep2]
         + [b1, gx1, gxm1, gy1, gz1, m1, w1, ep1]
         + [b0, gx0, gxm0, gy0, gz0, m0, w0, ms0, ep0],
         10**8,
-        28,
+        40,
     )
     return out
 

time: 106 us -> 93 us (0.88)
  waiting for transfers between devices: 36.4 us -> 20.6 us
  starting transfers between devices: 24.8 us -> 18.9 us
  Pallas kernels: 19.7 us -> 25 us
  blocking collectives: 21.4 us -> 25.4 us
    ppermute x4 -> x2, waiting for transfers between devices: 12.6 us -> 0.01 us  [above(): return lax.ppermute(v, 'wide', cyclic(16, -steps))]
    ppermute x4 -> x2, starting transfers between devices: 16 us -> 9.73 us  [above(): return lax.ppermute(v, 'wide', cyclic(16, -steps))]
    pallas_call x4 -> x3, Pallas kernels: 19.7 us -> 25 us  [call(): pl.pallas_call(kernel, out_shape=[jax.ShapeDtypeStruct(s, F32) for s in o...]
    all_to_all x1, blocking collectives: 21.4 us -> 25.4 us  [shards(): mine = lax.all_to_all(chunks, ('wide', 'y'), 0, 0).reshape(16, 96, 128)]
    ppermute x3 -> x2, waiting for transfers between devices: 4.94 us -> 2.52 us  [previous_rows(): return lax.ppermute(v, NARROW, cyclic(8, 1))]
    ppermute x4 -> x2, waiting for transfers between devices: 10.2 us -> 8.2 us  [below(): return lax.ppermute(v, 'wide', cyclic(16, steps))]
    ppermute x1, starting transfers between devices: 1.48 us -> 0.01 us  [shards(): other = lax.ppermute(mine, 'core', cyclic(2, 1))]
    ppermute x1, waiting for transfers between devices: 1.16 us -> 2.28 us  [shards(): other = lax.ppermute(mine, 'core', cyclic(2, 1))]
  transfers between devices with their start and end apart: 15 -> 9, of which waited for: 12 -> 6; matrix products, arithmetic and copies ran while one was open for 0% -> 0% of each run, Pallas kernels for 0% -> 0%
where the time goes in v4:
time: 93 us; the launch traced here: 92.8 us
  blocking collectives  25.4 us (27%)
  Pallas kernels  25 us (27%)
  waiting for transfers between devices  20.6 us (22%)
  starting transfers between devices  18.9 us (20%)
  local copies, waits for them, and re-layouts  2.38 us (3%)
    all_to_all x1, blocking collectives, shards(): mine = lax.all_to_all(chunks, ('wide', 'y'), 0, 0).reshape(16, 96, 128)  25.4 us
    pallas_call x3, Pallas kernels, call(): pl.pallas_call(kernel, out_shape=[jax.ShapeDtypeStruct(s, F32) for s in o...  25 us
    ppermute x2, starting transfers between devices, above(): return lax.ppermute(v, 'wide', cyclic(16, -steps))  9.73 us
    ppermute x2, waiting for transfers between devices, below(): return lax.ppermute(v, 'wide', cyclic(16, steps))  8.2 us
    ppermute x2, waiting for transfers between devices, next_rows(): return lax.ppermute(v, NARROW, cyclic(8, -1))  7.58 us
    ppermute x2, starting transfers between devices, previous_rows(): return lax.ppermute(v, NARROW, cyclic(8, 1))  5.35 us
    ppermute x2, waiting for transfers between devices, previous_rows(): return lax.ppermute(v, NARROW, cyclic(8, 1))  2.52 us
    ppermute x1, waiting for transfers between devices, shards(): other = lax.ppermute(mine, 'core', cyclic(2, 1))  2.28 us
  transfers between devices with their start and end apart: 9, of which 6 were waited for; matrix products, arithmetic and copies ran while one was open for 0% of the time, Pallas kernels for 0%

profile of v4, /device:TPU:1, one launch (start us, length us, event | category | flops | bytes accessed | tf_op | source)
XLA Modules:
  0.0 92.8 jit_solution(10166051960385707057)
XLA Ops:
  0.0 0.0 copy-start
  0.0 0.1 pad_add_fusion.idx
  0.1 1.0 %fusion.3 = (f32[3,16,384]{2,1,0:T(8,128)S(1)}, f32[3,16,384]{2,1,0:T(8,128)S(1)}) fusion(f32[8,16,384]{2,1,0:T(8,128)} %dens), kind=kLoop, calls=%fused_computation.48 | loop fusion | bytes 294912 | tf_op jit(solution)/shard_map/slice | solution.py:593
  1.1 1.0 %fusion = (f32[3,2,16,384]{3,2,1,0:T(8,128)S(1)}, f32[3,2,16,384]{3,2,1,0:T(8,128)S(1)}) fusion(f32[3,8,16,384]{3,2,1,0:T(8,128)} %load), kind=kLoop, calls=%fused_computation.45 | loop fusion | bytes 589824 | tf_op jit(solution)/shard_map/slice | solution.py:593
  2.1 0.0 copy-start.1
  2.1 2.1 %collective-permute-start = (f32[9,16,384]{2,1,0:T(8,128)S(1)}, f32[9,16,384]{2,1,0:T(8,128)S(1)}, u32[]{:S(2)}, u32[]{:S(2)}) collective-permute-start(f32[9,16,384]{2,1,0:T(8,128)S(1)} %pad_maximum_fusion.3), channel_id=1, source_target_pairs={{0,8},{8,16},{16,24},{24,32},{32,40},{40,48},{48,56},{56,64},{64,7... | collective-permute-start | bytes 663560 | tf_op jit(solution)/shard_map/ppermute | solution.py:590
  4.2 4.8 %collective-permute-start.1 = (f32[9,16,384]{2,1,0:T(8,128)S(1)}, f32[9,16,384]{2,1,0:T(8,128)S(1)}, u32[]{:S(2)}, u32[]{:S(2)}) collective-permute-start(f32[9,16,384]{2,1,0:T(8,128)S(1)} %pad_maximum_fusion.4), channel_id=1, source_target_pairs={{0,120},{8,0},{16,8},{24,16},{32,24},{40,32},{48,40},{56,48},{64,5... | collective-permute-start | bytes 663560 | tf_op jit(solution)/shard_map/ppermute | solution.py:587
  9.1 0.0 copy-done
  9.1 5.0 %collective-permute-done.lo = f32[9,16,384]{2,1,0:T(8,128)S(1)} collective-permute-done((f32[9,16,384]{2,1,0:T(8,128)S(1)}, f32[9,16,384]{2,1,0:T(8,128)S(1)}, u32[]{:S(2)}, u32[]{:S(2)}) %collective-permute-start) | collective-permute-done | bytes 221216 | tf_op jit(solution)/shard_map/ppermute | solution.py:590
  14.2 0.0 collective-permute-done.1.hi
  14.4 0.0 copy-done.1
  14.4 1.2 %collective-permute-start.2 = (f32[50,4,384]{2,1,0:T(4,128)S(1)}, f32[50,4,384]{2,1,0:T(4,128)S(1)}, u32[]{:S(2)}, u32[]{:S(2)}) collective-permute-start(f32[50,4,384]{2,1,0:T(4,128)S(1)} %get-tuple-element.70), channel_id=1, source_target_pairs={{0,7},{1,0},{2,1},{3,2},{4,3},{5,4},{6,5},{7,6},{8,15},{9,8},{10,9... | collective-permute-start | bytes 921608 | tf_op jit(solution)/shard_map/ppermute | solution.py:581
  15.7 1.2 %collective-permute-start.3 = (f32[50,4,384]{2,1,0:T(4,128)S(1)}, f32[50,4,384]{2,1,0:T(4,128)S(1)}, u32[]{:S(2)}, u32[]{:S(2)}) collective-permute-start(f32[50,4,384]{2,1,0:T(4,128)S(1)} %get-tuple-element.71), channel_id=1, source_target_pairs={{0,1},{1,2},{2,3},{3,4},{4,5},{5,6},{6,7},{7,0},{8,9},{9,10},{10,1... | collective-permute-start | bytes 921608 | tf_op jit(solution)/shard_map/ppermute | solution.py:584
  16.9 4.8 %collective-permute-done.2 = f32[50,4,384]{2,1,0:T(4,128)S(1)} collective-permute-done((f32[50,4,384]{2,1,0:T(4,128)S(1)}, f32[50,4,384]{2,1,0:T(4,128)S(1)}, u32[]{:S(2)}, u32[]{:S(2)}) %collective-permute-start.2) | collective-permute-done | bytes 307232 | tf_op jit(solution)/shard_map/ppermute | solution.py:581
  21.7 0.0 collective-permute-done.3
  21.7 0.1 pad_maximum_fusion.rows
  21.8 4.6 %shard_map.28 = (f32[3,14,3,8,384]{4,3,2,1,0:T(8,128)S(1)}, f32[14,3,8,384]{3,2,1,0:T(8,128)S(1)}, f32[14,3,8,384]{3,2,1,0:T(8,128)S(1)}, f32[14,3,8,384]{3,2,1,...) custom-call(s32[2]{0:T(128)S(1)} %pad_add_fusion.idx, ...), custom_call_target="tpu_custom_call" | custom-call | flops 10000000 | bytes 9916424 | tf_op jit(solution)/shard_map/pallas_call | solution.py:563
  26.5 0.1 collective-permute-start.4
  26.6 4.9 %collective-permute-start.5 = (f32[18,8,384]{2,1,0:T(8,128)S(1)}, f32[18,8,384]{2,1,0:T(8,128)S(1)}, u32[]{:S(2)}, u32[]{:S(2)}) collective-permute-start(f32[18,8,384]{2,1,0:T(8,128)S(1)} %get-tuple-element.102), channel_id=1, source_target_pairs={{0,120},{8,0},{16,8},{24,16},{32,24},{40,32},{48,40},{56,48},{64,5... | collective-permute-start | bytes 663560 | tf_op jit(solution)/shard_map/ppermute | solution.py:587
  31.5 3.2 %collective-permute-done.4.lo = f32[18,8,384]{2,1,0:T(8,128)S(1)} collective-permute-done((f32[18,8,384]{2,1,0:T(8,128)S(1)}, f32[18,8,384]{2,1,0:T(8,128)S(1)}, u32[]{:S(2)}, u32[]{:S(2)}) %collective-permute-start.4) | collective-permute-done | bytes 221216 | tf_op jit(solution)/shard_map/ppermute | solution.py:590
  34.7 0.0 collective-permute-done.5.hi
  34.9 4.1 %collective-permute-start.7 = (f32[18,8,384]{2,1,0:T(8,128)S(1)}, f32[18,8,384]{2,1,0:T(8,128)S(1)}, u32[]{:S(2)}, u32[]{:S(2)}) collective-permute-start(f32[18,8,384]{2,1,0:T(8,128)S(1)} %get-tuple-element.58), channel_id=1, source_target_pairs={{0,1},{1,2},{2,3},{3,4},{4,5},{5,6},{6,7},{7,0},{8,9},{9,10},{10,1... | collective-permute-start | bytes 663560 | tf_op jit(solution)/shard_map/ppermute | solution.py:584
  39.0 0.4 collective-permute-start.6
  39.4 2.5 %collective-permute-done.7.before = f32[18,8,384]{2,1,0:T(8,128)S(1)} collective-permute-done((f32[18,8,384]{2,1,0:T(8,128)S(1)}, f32[18,8,384]{2,1,0:T(8,128)S(1)}, u32[]{:S(2)}, u32[]{:S(2)}) %collective-permute-start.7) | collective-permute-done | bytes 221216 | tf_op jit(solution)/shard_map/ppermute | solution.py:584
  41.9 2.8 %collective-permute-done.6.after = f32[18,8,384]{2,1,0:T(8,128)S(1)} collective-permute-done((f32[18,8,384]{2,1,0:T(8,128)S(1)}, f32[18,8,384]{2,1,0:T(8,128)S(1)}, u32[]{:S(2)}, u32[]{:S(2)}) %collective-permute-start.6) | collective-permute-done | bytes 221216 | tf_op jit(solution)/shard_map/ppermute | solution.py:581
  44.7 3.0 %shard_map.29 = (f32[3,14,3,8,256]{4,3,2,1,0:T(8,128)S(1)}, f32[14,3,8,256]{3,2,1,0:T(8,128)S(1)}, f32[14,3,8,256]{3,2,1,0:T(8,128)S(1)}, f32[14,3,8,256]{3,2,1,...) custom-call(s32[2]{0:T(128)S(1)} %pad_add_fusion.idx, ...), custom_call_target="tpu_custom_call" | custom-call | flops 10000000 | bytes 5824520 | tf_op jit(solution)/shard_map/pallas_call | solution.py:563
  47.7 0.1 broadcast_in_dim.2
  47.8 25.4 %all_to_all.5 = f32[64,3,8,128]{3,2,1,0:T(8,128)S(1)} all-to-all(f32[64,3,8,128]{3,2,1,0:T(8,128)S(1)} %broadcast_in_dim.2), channel_id=1, replica_groups=mesh['wide'=16,'y'=4,'core'=2] {'wide','y'}, dimensions={0} | all-to-all | bytes 1572864 | tf_op jit(solution)/shard_map/all_to_all | solution.py:634
  73.2 0.0 collective-permute-start.8
  73.2 2.3 %collective-permute-done.8.other = f32[16,96,128]{2,1,0:T(8,128)S(1)} collective-permute-done((f32[16,96,128]{2,1,0:T(8,128)S(1)}, f32[16,96,128]{2,1,0:T(8,128)S(1)}, u32[]{:S(2)}, u32[]{:S(2)}) %collective-permute-start.8) | collective-permute-done | bytes 786464 | tf_op jit(solution)/shard_map/ppermute | solution.py:635
  75.5 17.3 %shard_map.30 = f32[3,8,16,384]{3,2,1,0:T(8,128)} custom-call(s32[2]{0:T(128)S(1)} %pad_add_fusion.idx, f32[16,96,128]{2,1,0:T(8,128)S(1)} %bitcast.14, f32[16,96,128]{2,1,0:T(8,128)S(1)} %collective-permute-done.8.other, f32[18,8,384]{2,1,0:T(8,128)S(1)} %collective-permute-done.4.lo, f32[18,8,384]{2,1,0:T(8,128)S(1)} %collective-permute-done.5.hi, ...), custom_call_target="tpu_custom_call" | custom-call | flops 100000000 | bytes 15163400 | tf_op jit(solution)/shard_map/pallas_call | solution.py:563
  (27 shorter events, 0.5 us)
Async XLA Ops:
  0.0 9.1 %copy-start = (f32[3,8,16,384]{3,2,1,0:T(8,128)S(1)}, f32[3,8,16,384]{3,2,1,0:T(8,128)}, u32[]{:S(2)}) copy-start(f32[3,8,16,384]{3,2,1,0:T(8,128)} %load) | copy-start | bytes 1769476
  2.1 12.3 %copy-start.1 = (f32[8,16,384]{2,1,0:T(8,128)S(1)}, f32[8,16,384]{2,1,0:T(8,128)}, u32[]{:S(2)}) copy-start(f32[8,16,384]{2,1,0:T(8,128)} %dens) | copy-start | bytes 589828
  2.1 12.0 %collective-permute-start = (f32[9,16,384]{2,1,0:T(8,128)S(1)}, f32[9,16,384]{2,1,0:T(8,128)S(1)}, u32[]{:S(2)}, u32[]{:S(2)}) collective-permute-start(f32[9,16,384]{2,1,0:T(8,128)S(1)} %pad_maximum_fusion.3), channel_id=1, source_target_pairs={{0,8},{8,16},{16,24},{24,32},{32,40},{40,48},{48,56},{56,64},{64,7... | collective-permute-start | bytes 663560 | tf_op jit(solution)/shard_map/ppermute | solution.py:590
  4.2 9.9 %collective-permute-start.1 = (f32[9,16,384]{2,1,0:T(8,128)S(1)}, f32[9,16,384]{2,1,0:T(8,128)S(1)}, u32[]{:S(2)}, u32[]{:S(2)}) collective-permute-start(f32[9,16,384]{2,1,0:T(8,128)S(1)} %pad_maximum_fusion.4), channel_id=1, source_target_pairs={{0,120},{8,0},{16,8},{24,16},{32,24},{40,32},{48,40},{56,48},{64,5... | collective-permute-start | bytes 663560 | tf_op jit(solution)/shard_map/ppermute | solution.py:587
  14.4 7.3 %collective-permute-start.2 = (f32[50,4,384]{2,1,0:T(4,128)S(1)}, f32[50,4,384]{2,1,0:T(4,128)S(1)}, u32[]{:S(2)}, u32[]{:S(2)}) collective-permute-start(f32[50,4,384]{2,1,0:T(4,128)S(1)} %get-tuple-element.70), channel_id=1, source_target_pairs={{0,7},{1,0},{2,1},{3,2},{4,3},{5,4},{6,5},{7,6},{8,15},{9,8},{10,9... | collective-permute-start | bytes 921608 | tf_op jit(solution)/shard_map/ppermute | solution.py:581
  15.7 6.0 %collective-permute-start.3 = (f32[50,4,384]{2,1,0:T(4,128)S(1)}, f32[50,4,384]{2,1,0:T(4,128)S(1)}, u32[]{:S(2)}, u32[]{:S(2)}) collective-permute-start(f32[50,4,384]{2,1,0:T(4,128)S(1)} %get-tuple-element.71), channel_id=1, source_target_pairs={{0,1},{1,2},{2,3},{3,4},{4,5},{5,6},{6,7},{7,0},{8,9},{9,10},{10,1... | collective-permute-start | bytes 921608 | tf_op jit(solution)/shard_map/ppermute | solution.py:584
  26.5 8.2 %collective-permute-start.4 = (f32[18,8,384]{2,1,0:T(8,128)S(1)}, f32[18,8,384]{2,1,0:T(8,128)S(1)}, u32[]{:S(2)}, u32[]{:S(2)}) collective-permute-start(f32[18,8,384]{2,1,0:T(8,128)S(1)} %get-tuple-element.103), channel_id=1, source_target_pairs={{0,8},{8,16},{16,24},{24,32},{32,40},{40,48},{48,56},{56,64},{64,7... | collective-permute-start | bytes 663560 | tf_op jit(solution)/shard_map/ppermute | solution.py:590
  26.6 8.2 %collective-permute-start.5 = (f32[18,8,384]{2,1,0:T(8,128)S(1)}, f32[18,8,384]{2,1,0:T(8,128)S(1)}, u32[]{:S(2)}, u32[]{:S(2)}) collective-permute-start(f32[18,8,384]{2,1,0:T(8,128)S(1)} %get-tuple-element.102), channel_id=1, source_target_pairs={{0,120},{8,0},{16,8},{24,16},{32,24},{40,32},{48,40},{56,48},{64,5... | collective-permute-start | bytes 663560 | tf_op jit(solution)/shard_map/ppermute | solution.py:587
  34.9 7.0 %collective-permute-start.7 = (f32[18,8,384]{2,1,0:T(8,128)S(1)}, f32[18,8,384]{2,1,0:T(8,128)S(1)}, u32[]{:S(2)}, u32[]{:S(2)}) collective-permute-start(f32[18,8,384]{2,1,0:T(8,128)S(1)} %get-tuple-element.58), channel_id=1, source_target_pairs={{0,1},{1,2},{2,3},{3,4},{4,5},{5,6},{6,7},{7,0},{8,9},{9,10},{10,1... | collective-permute-start | bytes 663560 | tf_op jit(solution)/shard_map/ppermute | solution.py:584
  39.0 5.7 %collective-permute-start.6 = (f32[18,8,384]{2,1,0:T(8,128)S(1)}, f32[18,8,384]{2,1,0:T(8,128)S(1)}, u32[]{:S(2)}, u32[]{:S(2)}) collective-permute-start(f32[18,8,384]{2,1,0:T(8,128)S(1)} %get-tuple-element.59), channel_id=1, source_target_pairs={{0,7},{1,0},{2,1},{3,2},{4,3},{5,4},{6,5},{7,6},{8,15},{9,8},{10,9... | collective-permute-start | bytes 663560 | tf_op jit(solution)/shard_map/ppermute | solution.py:581
  73.2 2.3 %collective-permute-start.8 = (f32[16,96,128]{2,1,0:T(8,128)S(1)}, f32[16,96,128]{2,1,0:T(8,128)S(1)}, u32[]{:S(2)}, u32[]{:S(2)}) collective-permute-start(f32[16,96,128]{2,1,0:T(8,128)S(1)} %bitcast.13), channel_id=1, source_target_pairs={{0,1},{1,0},{2,3},{3,2},{4,5},{5,4},{6,7},{7,6},{8,9},{9,8},{10,11... | collective-permute-start | bytes 2359304 | tf_op jit(solution)/shard_map/ppermute | solution.py:635

commit v5 on v4

--- a/solution.py
+++ b/solution.py
@@ -36,12 +36,9 @@
 
 def times01(v, matrix):
     high = v.astype(BF16)
-    rest = v - high.astype(F32)
-    mid = rest.astype(BF16)
-    low = (rest - mid.astype(F32)).astype(BF16)
+    rest = (v - high.astype(F32)).astype(BF16)
     out = jnp.dot(high, matrix, preferred_element_type=F32)
-    out = out + jnp.dot(mid, matrix, preferred_element_type=F32)
-    return out + jnp.dot(low, matrix, preferred_element_type=F32)
+    return out + jnp.dot(rest, matrix, preferred_element_type=F32)
 
 
 def pair_sum_matrix(fine, coarse, start, factor):
@@ -96,7 +93,7 @@
         ref[(*at, k, pl.ds(start + 1, 8, stride=2), slice(None))] = part
 
 
-UNROLL = {2: 5, 4: 5, 6: 5, 9: 5}
+UNROLL = {2: 8, 4: 8, 6: 5, 9: 5}
 
 
 def planes_loop(level, lo, hi, body):

time: 93 us -> 90.8 us (0.976)
  Pallas kernels: 25 us -> 22.8 us
    pallas_call x3, Pallas kernels: 25 us -> 22.8 us  [call(): pl.pallas_call(kernel, out_shape=[jax.ShapeDtypeStruct(s, F32) for s in o...]
where the time goes in v5:
time: 90.8 us; the launch traced here: 90.7 us
  blocking collectives  25.4 us (28%)
  Pallas kernels  22.8 us (25%)
  waiting for transfers between devices  20.6 us (23%)
  starting transfers between devices  18.9 us (21%)
  local copies, waits for them, and re-layouts  2.38 us (3%)
    all_to_all x1, blocking collectives, shards(): mine = lax.all_to_all(chunks, ('wide', 'y'), 0, 0).reshape(16, 96, 128)  25.4 us
    pallas_call x3, Pallas kernels, call(): pl.pallas_call(kernel, out_shape=[jax.ShapeDtypeStruct(s, F32) for s in o...  22.8 us
    ppermute x2, starting transfers between devices, above(): return lax.ppermute(v, 'wide', cyclic(16, -steps))  9.73 us
    ppermute x2, waiting for transfers between devices, below(): return lax.ppermute(v, 'wide', cyclic(16, steps))  8.2 us
    ppermute x2, waiting for transfers between devices, next_rows(): return lax.ppermute(v, NARROW, cyclic(8, -1))  7.58 us
    ppermute x2, starting transfers between devices, previous_rows(): return lax.ppermute(v, NARROW, cyclic(8, 1))  5.36 us
    ppermute x2, waiting for transfers between devices, previous_rows(): return lax.ppermute(v, NARROW, cyclic(8, 1))  2.52 us
    ppermute x1, waiting for transfers between devices, shards(): other = lax.ppermute(mine, 'core', cyclic(2, 1))  2.28 us
  transfers between devices with their start and end apart: 9, of which 6 were waited for; matrix products, arithmetic and copies ran while one was open for 0% of the time, Pallas kernels for 0%

profile of v5, /device:TPU:1, one launch (start us, length us, event | category | flops | bytes accessed | tf_op | source)
XLA Modules:
  0.0 90.7 jit_solution(6301613632351498404)
XLA Ops:
  0.0 0.0 copy-start
  0.0 0.1 pad_add_fusion.idx
  0.1 1.0 %fusion.3 = (f32[3,16,384]{2,1,0:T(8,128)S(1)}, f32[3,16,384]{2,1,0:T(8,128)S(1)}) fusion(f32[8,16,384]{2,1,0:T(8,128)} %dens), kind=kLoop, calls=%fused_computation.48 | loop fusion | bytes 294912 | tf_op jit(solution)/shard_map/slice | solution.py:590
  1.1 1.0 %fusion = (f32[3,2,16,384]{3,2,1,0:T(8,128)S(1)}, f32[3,2,16,384]{3,2,1,0:T(8,128)S(1)}) fusion(f32[3,8,16,384]{3,2,1,0:T(8,128)} %load), kind=kLoop, calls=%fused_computation.45 | loop fusion | bytes 589824 | tf_op jit(solution)/shard_map/slice | solution.py:590
  2.1 0.0 copy-start.1
  2.1 2.1 %collective-permute-start = (f32[9,16,384]{2,1,0:T(8,128)S(1)}, f32[9,16,384]{2,1,0:T(8,128)S(1)}, u32[]{:S(2)}, u32[]{:S(2)}) collective-permute-start(f32[9,16,384]{2,1,0:T(8,128)S(1)} %pad_maximum_fusion.3), channel_id=1, source_target_pairs={{0,8},{8,16},{16,24},{24,32},{32,40},{40,48},{48,56},{56,64},{64,7... | collective-permute-start | bytes 663560 | tf_op jit(solution)/shard_map/ppermute | solution.py:587
  4.2 4.8 %collective-permute-start.1 = (f32[9,16,384]{2,1,0:T(8,128)S(1)}, f32[9,16,384]{2,1,0:T(8,128)S(1)}, u32[]{:S(2)}, u32[]{:S(2)}) collective-permute-start(f32[9,16,384]{2,1,0:T(8,128)S(1)} %pad_maximum_fusion.4), channel_id=1, source_target_pairs={{0,120},{8,0},{16,8},{24,16},{32,24},{40,32},{48,40},{56,48},{64,5... | collective-permute-start | bytes 663560 | tf_op jit(solution)/shard_map/ppermute | solution.py:584
  9.1 0.0 copy-done
  9.1 5.0 %collective-permute-done.lo = f32[9,16,384]{2,1,0:T(8,128)S(1)} collective-permute-done((f32[9,16,384]{2,1,0:T(8,128)S(1)}, f32[9,16,384]{2,1,0:T(8,128)S(1)}, u32[]{:S(2)}, u32[]{:S(2)}) %collective-permute-start) | collective-permute-done | bytes 221216 | tf_op jit(solution)/shard_map/ppermute | solution.py:587
  14.2 0.0 collective-permute-done.1.hi
  14.4 0.0 copy-done.1
  14.4 1.2 %collective-permute-start.2 = (f32[50,4,384]{2,1,0:T(4,128)S(1)}, f32[50,4,384]{2,1,0:T(4,128)S(1)}, u32[]{:S(2)}, u32[]{:S(2)}) collective-permute-start(f32[50,4,384]{2,1,0:T(4,128)S(1)} %get-tuple-element.70), channel_id=1, source_target_pairs={{0,7},{1,0},{2,1},{3,2},{4,3},{5,4},{6,5},{7,6},{8,15},{9,8},{10,9... | collective-permute-start | bytes 921608 | tf_op jit(solution)/shard_map/ppermute | solution.py:578
  15.7 1.2 %collective-permute-start.3 = (f32[50,4,384]{2,1,0:T(4,128)S(1)}, f32[50,4,384]{2,1,0:T(4,128)S(1)}, u32[]{:S(2)}, u32[]{:S(2)}) collective-permute-start(f32[50,4,384]{2,1,0:T(4,128)S(1)} %get-tuple-element.71), channel_id=1, source_target_pairs={{0,1},{1,2},{2,3},{3,4},{4,5},{5,6},{6,7},{7,0},{8,9},{9,10},{10,1... | collective-permute-start | bytes 921608 | tf_op jit(solution)/shard_map/ppermute | solution.py:581
  16.9 4.8 %collective-permute-done.2 = f32[50,4,384]{2,1,0:T(4,128)S(1)} collective-permute-done((f32[50,4,384]{2,1,0:T(4,128)S(1)}, f32[50,4,384]{2,1,0:T(4,128)S(1)}, u32[]{:S(2)}, u32[]{:S(2)}) %collective-permute-start.2) | collective-permute-done | bytes 307232 | tf_op jit(solution)/shard_map/ppermute | solution.py:578
  21.7 0.0 collective-permute-done.3
  21.7 0.1 pad_maximum_fusion.rows
  21.8 4.5 %shard_map.28 = (f32[3,14,3,8,384]{4,3,2,1,0:T(8,128)S(1)}, f32[14,3,8,384]{3,2,1,0:T(8,128)S(1)}, f32[14,3,8,384]{3,2,1,0:T(8,128)S(1)}, f32[14,3,8,384]{3,2,1,...) custom-call(s32[2]{0:T(128)S(1)} %pad_add_fusion.idx, ...), custom_call_target="tpu_custom_call" | custom-call | flops 10000000 | bytes 9916424 | tf_op jit(solution)/shard_map/pallas_call | solution.py:560
  26.4 0.1 collective-permute-start.4
  26.5 4.9 %collective-permute-start.5 = (f32[18,8,384]{2,1,0:T(8,128)S(1)}, f32[18,8,384]{2,1,0:T(8,128)S(1)}, u32[]{:S(2)}, u32[]{:S(2)}) collective-permute-start(f32[18,8,384]{2,1,0:T(8,128)S(1)} %get-tuple-element.102), channel_id=1, source_target_pairs={{0,120},{8,0},{16,8},{24,16},{32,24},{40,32},{48,40},{56,48},{64,5... | collective-permute-start | bytes 663560 | tf_op jit(solution)/shard_map/ppermute | solution.py:584
  31.4 3.2 %collective-permute-done.4.lo = f32[18,8,384]{2,1,0:T(8,128)S(1)} collective-permute-done((f32[18,8,384]{2,1,0:T(8,128)S(1)}, f32[18,8,384]{2,1,0:T(8,128)S(1)}, u32[]{:S(2)}, u32[]{:S(2)}) %collective-permute-start.4) | collective-permute-done | bytes 221216 | tf_op jit(solution)/shard_map/ppermute | solution.py:587
  34.6 0.0 collective-permute-done.5.hi
  34.8 4.2 %collective-permute-start.7 = (f32[18,8,384]{2,1,0:T(8,128)S(1)}, f32[18,8,384]{2,1,0:T(8,128)S(1)}, u32[]{:S(2)}, u32[]{:S(2)}) collective-permute-start(f32[18,8,384]{2,1,0:T(8,128)S(1)} %get-tuple-element.58), channel_id=1, source_target_pairs={{0,1},{1,2},{2,3},{3,4},{4,5},{5,6},{6,7},{7,0},{8,9},{9,10},{10,1... | collective-permute-start | bytes 663560 | tf_op jit(solution)/shard_map/ppermute | solution.py:581
  38.9 0.4 collective-permute-start.6
  39.3 2.5 %collective-permute-done.7.before = f32[18,8,384]{2,1,0:T(8,128)S(1)} collective-permute-done((f32[18,8,384]{2,1,0:T(8,128)S(1)}, f32[18,8,384]{2,1,0:T(8,128)S(1)}, u32[]{:S(2)}, u32[]{:S(2)}) %collective-permute-start.7) | collective-permute-done | bytes 221216 | tf_op jit(solution)/shard_map/ppermute | solution.py:581
  41.8 2.8 %collective-permute-done.6.after = f32[18,8,384]{2,1,0:T(8,128)S(1)} collective-permute-done((f32[18,8,384]{2,1,0:T(8,128)S(1)}, f32[18,8,384]{2,1,0:T(8,128)S(1)}, u32[]{:S(2)}, u32[]{:S(2)}) %collective-permute-start.6) | collective-permute-done | bytes 221216 | tf_op jit(solution)/shard_map/ppermute | solution.py:578
  44.6 3.0 %shard_map.29 = (f32[3,14,3,8,256]{4,3,2,1,0:T(8,128)S(1)}, f32[14,3,8,256]{3,2,1,0:T(8,128)S(1)}, f32[14,3,8,256]{3,2,1,0:T(8,128)S(1)}, f32[14,3,8,256]{3,2,1,...) custom-call(s32[2]{0:T(128)S(1)} %pad_add_fusion.idx, ...), custom_call_target="tpu_custom_call" | custom-call | flops 10000000 | bytes 5824520 | tf_op jit(solution)/shard_map/pallas_call | solution.py:560
  47.6 0.1 broadcast_in_dim.2
  47.7 25.4 %all_to_all.5 = f32[64,3,8,128]{3,2,1,0:T(8,128)S(1)} all-to-all(f32[64,3,8,128]{3,2,1,0:T(8,128)S(1)} %broadcast_in_dim.2), channel_id=1, replica_groups=mesh['wide'=16,'y'=4,'core'=2] {'wide','y'}, dimensions={0} | all-to-all | bytes 1572864 | tf_op jit(solution)/shard_map/all_to_all | solution.py:631
  73.1 0.0 collective-permute-start.8
  73.1 2.3 %collective-permute-done.8.other = f32[16,96,128]{2,1,0:T(8,128)S(1)} collective-permute-done((f32[16,96,128]{2,1,0:T(8,128)S(1)}, f32[16,96,128]{2,1,0:T(8,128)S(1)}, u32[]{:S(2)}, u32[]{:S(2)}) %collective-permute-start.8) | collective-permute-done | bytes 786464 | tf_op jit(solution)/shard_map/ppermute | solution.py:632
  75.4 15.3 %shard_map.30 = f32[3,8,16,384]{3,2,1,0:T(8,128)} custom-call(s32[2]{0:T(128)S(1)} %pad_add_fusion.idx, f32[16,96,128]{2,1,0:T(8,128)S(1)} %bitcast.14, f32[16,96,128]{2,1,0:T(8,128)S(1)} %collective-permute-done.8.other, f32[18,8,384]{2,1,0:T(8,128)S(1)} %collective-permute-done.4.lo, f32[18,8,384]{2,1,0:T(8,128)S(1)} %collective-permute-done.5.hi, ...), custom_call_target="tpu_custom_call" | custom-call | flops 100000000 | bytes 15163400 | tf_op jit(solution)/shard_map/pallas_call | solution.py:560
  (27 shorter events, 0.5 us)
Async XLA Ops:
  0.0 9.1 %copy-start = (f32[3,8,16,384]{3,2,1,0:T(8,128)S(1)}, f32[3,8,16,384]{3,2,1,0:T(8,128)}, u32[]{:S(2)}) copy-start(f32[3,8,16,384]{3,2,1,0:T(8,128)} %load) | copy-start | bytes 1769476
  2.1 12.3 %copy-start.1 = (f32[8,16,384]{2,1,0:T(8,128)S(1)}, f32[8,16,384]{2,1,0:T(8,128)}, u32[]{:S(2)}) copy-start(f32[8,16,384]{2,1,0:T(8,128)} %dens) | copy-start | bytes 589828
  2.1 12.0 %collective-permute-start = (f32[9,16,384]{2,1,0:T(8,128)S(1)}, f32[9,16,384]{2,1,0:T(8,128)S(1)}, u32[]{:S(2)}, u32[]{:S(2)}) collective-permute-start(f32[9,16,384]{2,1,0:T(8,128)S(1)} %pad_maximum_fusion.3), channel_id=1, source_target_pairs={{0,8},{8,16},{16,24},{24,32},{32,40},{40,48},{48,56},{56,64},{64,7... | collective-permute-start | bytes 663560 | tf_op jit(solution)/shard_map/ppermute | solution.py:587
  4.2 9.9 %collective-permute-start.1 = (f32[9,16,384]{2,1,0:T(8,128)S(1)}, f32[9,16,384]{2,1,0:T(8,128)S(1)}, u32[]{:S(2)}, u32[]{:S(2)}) collective-permute-start(f32[9,16,384]{2,1,0:T(8,128)S(1)} %pad_maximum_fusion.4), channel_id=1, source_target_pairs={{0,120},{8,0},{16,8},{24,16},{32,24},{40,32},{48,40},{56,48},{64,5... | collective-permute-start | bytes 663560 | tf_op jit(solution)/shard_map/ppermute | solution.py:584
  14.4 7.3 %collective-permute-start.2 = (f32[50,4,384]{2,1,0:T(4,128)S(1)}, f32[50,4,384]{2,1,0:T(4,128)S(1)}, u32[]{:S(2)}, u32[]{:S(2)}) collective-permute-start(f32[50,4,384]{2,1,0:T(4,128)S(1)} %get-tuple-element.70), channel_id=1, source_target_pairs={{0,7},{1,0},{2,1},{3,2},{4,3},{5,4},{6,5},{7,6},{8,15},{9,8},{10,9... | collective-permute-start | bytes 921608 | tf_op jit(solution)/shard_map/ppermute | solution.py:578
  15.7 6.0 %collective-permute-start.3 = (f32[50,4,384]{2,1,0:T(4,128)S(1)}, f32[50,4,384]{2,1,0:T(4,128)S(1)}, u32[]{:S(2)}, u32[]{:S(2)}) collective-permute-start(f32[50,4,384]{2,1,0:T(4,128)S(1)} %get-tuple-element.71), channel_id=1, source_target_pairs={{0,1},{1,2},{2,3},{3,4},{4,5},{5,6},{6,7},{7,0},{8,9},{9,10},{10,1... | collective-permute-start | bytes 921608 | tf_op jit(solution)/shard_map/ppermute | solution.py:581
  26.4 8.2 %collective-permute-start.4 = (f32[18,8,384]{2,1,0:T(8,128)S(1)}, f32[18,8,384]{2,1,0:T(8,128)S(1)}, u32[]{:S(2)}, u32[]{:S(2)}) collective-permute-start(f32[18,8,384]{2,1,0:T(8,128)S(1)} %get-tuple-element.103), channel_id=1, source_target_pairs={{0,8},{8,16},{16,24},{24,32},{32,40},{40,48},{48,56},{56,64},{64,7... | collective-permute-start | bytes 663560 | tf_op jit(solution)/shard_map/ppermute | solution.py:587
  26.5 8.2 %collective-permute-start.5 = (f32[18,8,384]{2,1,0:T(8,128)S(1)}, f32[18,8,384]{2,1,0:T(8,128)S(1)}, u32[]{:S(2)}, u32[]{:S(2)}) collective-permute-start(f32[18,8,384]{2,1,0:T(8,128)S(1)} %get-tuple-element.102), channel_id=1, source_target_pairs={{0,120},{8,0},{16,8},{24,16},{32,24},{40,32},{48,40},{56,48},{64,5... | collective-permute-start | bytes 663560 | tf_op jit(solution)/shard_map/ppermute | solution.py:584
  34.8 7.0 %collective-permute-start.7 = (f32[18,8,384]{2,1,0:T(8,128)S(1)}, f32[18,8,384]{2,1,0:T(8,128)S(1)}, u32[]{:S(2)}, u32[]{:S(2)}) collective-permute-start(f32[18,8,384]{2,1,0:T(8,128)S(1)} %get-tuple-element.58), channel_id=1, source_target_pairs={{0,1},{1,2},{2,3},{3,4},{4,5},{5,6},{6,7},{7,0},{8,9},{9,10},{10,1... | collective-permute-start | bytes 663560 | tf_op jit(solution)/shard_map/ppermute | solution.py:581
  38.9 5.7 %collective-permute-start.6 = (f32[18,8,384]{2,1,0:T(8,128)S(1)}, f32[18,8,384]{2,1,0:T(8,128)S(1)}, u32[]{:S(2)}, u32[]{:S(2)}) collective-permute-start(f32[18,8,384]{2,1,0:T(8,128)S(1)} %get-tuple-element.59), channel_id=1, source_target_pairs={{0,7},{1,0},{2,1},{3,2},{4,3},{5,4},{6,5},{7,6},{8,15},{9,8},{10,9... | collective-permute-start | bytes 663560 | tf_op jit(solution)/shard_map/ppermute | solution.py:578
  73.1 2.3 %collective-permute-start.8 = (f32[16,96,128]{2,1,0:T(8,128)S(1)}, f32[16,96,128]{2,1,0:T(8,128)S(1)}, u32[]{:S(2)}, u32[]{:S(2)}) collective-permute-start(f32[16,96,128]{2,1,0:T(8,128)S(1)} %bitcast.13), channel_id=1, source_target_pairs={{0,1},{1,0},{2,3},{3,2},{4,5},{5,4},{6,7},{7,6},{8,9},{9,8},{10,11... | collective-permute-start | bytes 2359304 | tf_op jit(solution)/shard_map/ppermute | solution.py:632

commit v6 on v5

--- a/solution.py
+++ b/solution.py
@@ -93,7 +93,7 @@
         ref[(*at, k, pl.ds(start + 1, 8, stride=2), slice(None))] = part
 
 
-UNROLL = {2: 8, 4: 8, 6: 5, 9: 5}
+UNROLL = {2: 16, 4: 32, 6: 12, 9: 12}
 
 
 def planes_loop(level, lo, hi, body):
@@ -136,7 +136,7 @@
         return r
 
 
-def coefficients(level, rho, lo, hi):
+def coefficients(level, rho, lo, hi, first):
     masks = level.masks()
 
     def shear(z):
@@ -175,9 +175,10 @@
         level.gy[z] = gy
         level.gz[z] = gz
         level.m[z] = m
-        level.w[0, z] = jnp.where(inside, DAMPING / (total + mn), 0.0)
-        level.w[1, z] = jnp.where(inside, DAMPING / (total + level.after(m, 1, masks)), 0.0)
-        level.w[2, z] = jnp.where(inside, DAMPING / (total + level.after(m, 2, masks)), 0.0)
+        for c, beyond in enumerate((mn, level.after(m, 1, masks), level.after(m, 2, masks))):
+            w = jnp.where(inside, DAMPING / (total + beyond), 0.0)
+            level.w[c, z] = w
+            first(z, c, w)
         return 0
 
     level.gz[lo - 1] = 0.5 * (shear(lo - 1) + shear(lo))
@@ -191,22 +192,24 @@
 
     def stress(z):
         uz, uy, ux = u[0, z], u[1, z], u[2, z]
+        left = level.before(ux, 2, masks)
+        s_ref[1] = left
         div = (uz - u[0, z - 1]) + (uy - level.before(uy, 1, masks))
-        return level.m[z] * (div + (ux - level.before(ux, 2, masks)))
-
-    s_ref[...] = stress(lo)
+        return level.m[z] * (div + (ux - left))
+
+    s_ref[0] = stress(lo)
     for c in range(3):
         f_ref[c] = level.gz[lo - 1] * (u[c, lo - 1] - u[c, lo])
 
     def plane(z, _):
-        s = s_ref[...]
+        s, left = s_ref[0], s_ref[1]
         sn = stress(z + 1)
-        s_ref[...] = sn
+        s_ref[0] = sn
         gx, gxm, gy, gz = level.gx[z], level.gxm[z], level.gy[z], level.gz[z]
         for c in range(3):
             v = u[c, z]
             fz = gz * (v - u[c, z + 1])
-            fx = gx * (v - after_x(v)) + gxm * (v - before_x(v))
+            fx = gx * (v - after_x(v)) + gxm * (v - (left if c == 2 else before_x(v)))
             fy = gy * (v - after_y(v))
             grad = s - (sn if c == 0 else level.after(s, c, masks))
             mass = MASS if level.ms is None else level.ms[z]
@@ -216,16 +219,6 @@
         return 0
 
     planes_loop(level, lo, hi, plane)
-
-
-def scaled(w, b, e, lo, hi):
-    def plane(z, _):
-        for c in range(3):
-            e[c, z] = w[c, z] * b[c, z]
-        return 0
-
-    unroll = next(k for k in (4, 5, 3, 2, 1) if (hi - lo) % k == 0)
-    lax.fori_loop(lo, hi, plane, 0, unroll=unroll)
 
 
 def smoothed(level, b, src, dst, lo, hi, s_ref, f_ref):
@@ -269,16 +262,13 @@
     for z in range(14):
         rho[z] = interleaved(nat, 3, 3, z) * (below if z < 3 else above if z > 10 else grid)
     level = Level(3, 384, True, False, gx, gxm, gy, gz, m, w, ms)
-    coefficients(level, rho, 1, 13)
-
-    def first(z, _):
-        for c in range(3):
-            v = interleaved(nat, 3, c, z)
-            b[c, z] = v
-            e1[c, z] = w[c, z] * v
-        return 0
-
-    lax.fori_loop(1, 13, first, 0, unroll=3)
+
+    def first(z, c, scale):
+        v = interleaved(nat, 3, c, z)
+        b[c, z] = v
+        e1[c, z] = scale * v
+
+    coefficients(level, rho, 1, 13, first)
     smoothed(level, b, e1, ep, 2, 12, s_ref, f_ref)
     for c in range(3):
         edge_low[c] = ep[c, 4]
@@ -356,16 +346,13 @@
     for z in range(14):
         rho[z] = interleaved(nat, 3, 3, z) * (below if z < 5 else above if z > 8 else grid)
     level = Level(3, 256, False, False, gx, gxm, gy, gz, m, w, None)
-    coefficients(level, rho, 1, 13)
-
-    def first(z, _):
-        for c in range(3):
-            v = interleaved(nat, 3, c, z)
-            b[c, z] = v
-            e1[c, z] = w[c, z] * v
-        return 0
-
-    lax.fori_loop(1, 13, first, 0, unroll=3)
+
+    def first(z, c, scale):
+        v = interleaved(nat, 3, c, z)
+        b[c, z] = v
+        e1[c, z] = scale * v
+
+    coefficients(level, rho, 1, 13, first)
     smoothed(level, b, e1, ep, 2, 12, s_ref, f_ref)
     rz[...] = jnp.zeros_like(rz)
 
@@ -443,7 +430,6 @@
         d = jnp.zeros((4, 8, 128), F32)
         for c in range(3):
             v = ea[c, z]
-            b2[c, z] = jnp.where(lane < 96, v, 0.0)
             moved = pltpu.roll(v, 32 + 32 * c, 2) if c < 3 else v
             d = jnp.where((lane >> 5) == c, moved, d)
         rho2[z] = d
@@ -452,8 +438,13 @@
     lax.fori_loop(4, 36, split, 0, unroll=4)
 
     level2 = Level(4, 128, False, True, gx2, gxm2, gy2, gz2, m2, w2, ms2)
-    coefficients(level2, rho2, 4, 36)
-    scaled(w2, b2, ea, 4, 36)
+
+    def first2(z, c, scale):
+        v = jnp.where(lane < 96, ea[c, z], 0.0)
+        b2[c, z] = v
+        ea[c, z] = scale * v
+
+    coefficients(level2, rho2, 4, 36, first2)
     smoothed(level2, b2, ea, ep2, 4, 36, s2, f2)
     rz[...] = jnp.zeros_like(rz)
 
@@ -479,8 +470,11 @@
             rho3[2:18] = v
 
     level3 = Level(2, 128, False, True, gx3, gxm3, gy3, gz3, m3, w3, ms3)
-    coefficients(level3, rho3, 2, 18)
-    scaled(w3, b3, ec, 2, 18)
+
+    def first3(z, c, scale):
+        ec[c, z] = scale * b3[c, z]
+
+    coefficients(level3, rho3, 2, 18, first3)
     for src, dst in ((ec, ed), (ed, ec), (ec, ed)):
         smoothed(level3, b3, src, dst, 2, 18, s3, f3)
 
@@ -603,7 +597,7 @@
     b0, gx0, gxm0, gy0, gz0, m0, w0, ms0, ep0, edge_low, edge_high, l1 = call(
         down0,
         [(3,) + p0, p0, p0, p0, p0, p0, (3,) + p0, p0, (3,) + p0, (3,) + c0, (3,) + c0, (9, 8, 384)],
-        [(4, 14, 3, 24, 128), p0, (3,) + p0, (3, 4) + c0, (3, 4, 3, 24, 128), c0, (3,) + c0],
+        [(4, 14, 3, 24, 128), p0, (3,) + p0, (3, 4) + c0, (3, 4, 3, 24, 128), (2,) + c0, (3,) + c0],
         [idx, load, density, rows, lo, hi],
         10**7,
         17,
@@ -621,7 +615,7 @@
     b1, gx1, gxm1, gy1, gz1, m1, w1, ep1, chunk = call(
         down1,
         [(3,) + p1, p1, p1, p1, p1, p1, (3,) + p1, (3,) + p1, (3, 8, 128)],
-        [(4, 14, 2, 24, 128), p1, (3,) + p1, (3, 4) + c1, (3, 4, 2, 24, 128), c1, (3,) + c1],
+        [(4, 14, 2, 24, 128), p1, (3,) + p1, (3, 4) + c1, (3, 4, 2, 24, 128), (2,) + c1, (3,) + c1],
         [idx, l1, lo, hi, after, before],
         10**7,
         10,
@@ -639,8 +633,8 @@
         [p2, (3,) + p2, p2, p2, p2, p2, p2, (3,) + p2, p2, (3,) + p2, (3,) + p2]
         + [p3, (3,) + p3, p3, p3, p3, p3, p3, (3,) + p3, p3, (3,) + p3, (3,) + p3]
         + [(4, 16, 2, 8, 128), (3, 6, 1, 32, 128), (3, 6, 2, 24, 128), (3, 6, 3, 32, 128)]
-        + [c3, (3,) + c3, u2, u2, c2, (3,) + c2]
-        + [(3,) + p1, (3,) + p1, c1, (3,) + c1, (3,) + p0, (3,) + p0, c0, (3,) + c0],
+        + [(2,) + c3, (3,) + c3, u2, u2, (2,) + c2, (3,) + c2]
+        + [(3,) + p1, (3,) + p1, (2,) + c1, (3,) + c1, (3,) + p0, (3,) + p0, (2,) + c0, (3,) + c0],
         [idx, mine, other, lo, hi]
         + [b1, gx1, gxm1, gy1, gz1, m1, w1, ep1]
         + [b0, gx0, gxm0, gy0, gz0, m0, w0, ms0, ep0],

time: 90.8 us -> 88 us (0.969)
  Pallas kernels: 22.8 us -> 20 us
    pallas_call x3, Pallas kernels: 22.8 us -> 20 us  [call(): pl.pallas_call(kernel, out_shape=[jax.ShapeDtypeStruct(s, F32) for s in o...]
where the time goes in v6:
time: 88 us; the launch traced here: 87.8 us
  blocking collectives  25.4 us (29%)
  waiting for transfers between devices  20.6 us (23%)
  Pallas kernels  20 us (23%)
  starting transfers between devices  18.9 us (21%)
  local copies, waits for them, and re-layouts  2.39 us (3%)
    all_to_all x1, blocking collectives, shards(): mine = lax.all_to_all(chunks, ('wide', 'y'), 0, 0).reshape(16, 96, 128)  25.4 us
    pallas_call x3, Pallas kernels, call(): pl.pallas_call(kernel, out_shape=[jax.ShapeDtypeStruct(s, F32) for s in o...  20 us
    ppermute x2, starting transfers between devices, above(): return lax.ppermute(v, 'wide', cyclic(16, -steps))  9.73 us
    ppermute x2, waiting for transfers between devices, below(): return lax.ppermute(v, 'wide', cyclic(16, steps))  8.2 us
    ppermute x2, waiting for transfers between devices, next_rows(): return lax.ppermute(v, NARROW, cyclic(8, -1))  7.58 us
    ppermute x2, starting transfers between devices, previous_rows(): return lax.ppermute(v, NARROW, cyclic(8, 1))  5.35 us
    ppermute x2, waiting for transfers between devices, previous_rows(): return lax.ppermute(v, NARROW, cyclic(8, 1))  2.52 us
    ppermute x1, waiting for transfers between devices, shards(): other = lax.ppermute(mine, 'core', cyclic(2, 1))  2.28 us
  transfers between devices with their start and end apart: 9, of which 6 were waited for; matrix products, arithmetic and copies ran while one was open for 0% of the time, Pallas kernels for 0%

profile of v6, /device:TPU:1, one launch (start us, length us, event | category | flops | bytes accessed | tf_op | source)
XLA Modules:
  0.0 87.8 jit_solution(10414843881164972038)
XLA Ops:
  0.0 0.0 copy-start
  0.0 0.1 pad_add_fusion.idx
  0.1 1.0 %fusion.3 = (f32[3,16,384]{2,1,0:T(8,128)S(1)}, f32[3,16,384]{2,1,0:T(8,128)S(1)}) fusion(f32[8,16,384]{2,1,0:T(8,128)} %dens), kind=kLoop, calls=%fused_computation.48 | loop fusion | bytes 294912 | tf_op jit(solution)/shard_map/slice | solution.py:584
  1.1 1.0 %fusion = (f32[3,2,16,384]{3,2,1,0:T(8,128)S(1)}, f32[3,2,16,384]{3,2,1,0:T(8,128)S(1)}) fusion(f32[3,8,16,384]{3,2,1,0:T(8,128)} %load), kind=kLoop, calls=%fused_computation.45 | loop fusion | bytes 589824 | tf_op jit(solution)/shard_map/slice | solution.py:584
  2.1 0.0 copy-start.1
  2.1 2.1 %collective-permute-start = (f32[9,16,384]{2,1,0:T(8,128)S(1)}, f32[9,16,384]{2,1,0:T(8,128)S(1)}, u32[]{:S(2)}, u32[]{:S(2)}) collective-permute-start(f32[9,16,384]{2,1,0:T(8,128)S(1)} %pad_maximum_fusion.3), channel_id=1, source_target_pairs={{0,8},{8,16},{16,24},{24,32},{32,40},{40,48},{48,56},{56,64},{64,7... | collective-permute-start | bytes 663560 | tf_op jit(solution)/shard_map/ppermute | solution.py:581
  4.2 4.8 %collective-permute-start.1 = (f32[9,16,384]{2,1,0:T(8,128)S(1)}, f32[9,16,384]{2,1,0:T(8,128)S(1)}, u32[]{:S(2)}, u32[]{:S(2)}) collective-permute-start(f32[9,16,384]{2,1,0:T(8,128)S(1)} %pad_maximum_fusion.4), channel_id=1, source_target_pairs={{0,120},{8,0},{16,8},{24,16},{32,24},{40,32},{48,40},{56,48},{64,5... | collective-permute-start | bytes 663560 | tf_op jit(solution)/shard_map/ppermute | solution.py:578
  9.1 0.0 copy-done
  9.1 5.0 %collective-permute-done.lo = f32[9,16,384]{2,1,0:T(8,128)S(1)} collective-permute-done((f32[9,16,384]{2,1,0:T(8,128)S(1)}, f32[9,16,384]{2,1,0:T(8,128)S(1)}, u32[]{:S(2)}, u32[]{:S(2)}) %collective-permute-start) | collective-permute-done | bytes 221216 | tf_op jit(solution)/shard_map/ppermute | solution.py:581
  14.2 0.0 collective-permute-done.1.hi
  14.4 0.0 copy-done.1
  14.4 1.2 %collective-permute-start.2 = (f32[50,4,384]{2,1,0:T(4,128)S(1)}, f32[50,4,384]{2,1,0:T(4,128)S(1)}, u32[]{:S(2)}, u32[]{:S(2)}) collective-permute-start(f32[50,4,384]{2,1,0:T(4,128)S(1)} %get-tuple-element.70), channel_id=1, source_target_pairs={{0,7},{1,0},{2,1},{3,2},{4,3},{5,4},{6,5},{7,6},{8,15},{9,8},{10,9... | collective-permute-start | bytes 921608 | tf_op jit(solution)/shard_map/ppermute | solution.py:572
  15.7 1.2 %collective-permute-start.3 = (f32[50,4,384]{2,1,0:T(4,128)S(1)}, f32[50,4,384]{2,1,0:T(4,128)S(1)}, u32[]{:S(2)}, u32[]{:S(2)}) collective-permute-start(f32[50,4,384]{2,1,0:T(4,128)S(1)} %get-tuple-element.71), channel_id=1, source_target_pairs={{0,1},{1,2},{2,3},{3,4},{4,5},{5,6},{6,7},{7,0},{8,9},{9,10},{10,1... | collective-permute-start | bytes 921608 | tf_op jit(solution)/shard_map/ppermute | solution.py:575
  16.9 4.8 %collective-permute-done.2 = f32[50,4,384]{2,1,0:T(4,128)S(1)} collective-permute-done((f32[50,4,384]{2,1,0:T(4,128)S(1)}, f32[50,4,384]{2,1,0:T(4,128)S(1)}, u32[]{:S(2)}, u32[]{:S(2)}) %collective-permute-start.2) | collective-permute-done | bytes 307232 | tf_op jit(solution)/shard_map/ppermute | solution.py:572
  21.7 0.0 collective-permute-done.3
  21.7 0.1 pad_maximum_fusion.rows
  21.8 4.1 %shard_map.28 = (f32[3,14,3,8,384]{4,3,2,1,0:T(8,128)S(1)}, f32[14,3,8,384]{3,2,1,0:T(8,128)S(1)}, f32[14,3,8,384]{3,2,1,0:T(8,128)S(1)}, f32[14,3,8,384]{3,2,1,...) custom-call(s32[2]{0:T(128)S(1)} %pad_add_fusion.idx, ...), custom_call_target="tpu_custom_call" | custom-call | flops 10000000 | bytes 9916424 | tf_op jit(solution)/shard_map/pallas_call | solution.py:554
  26.0 0.1 collective-permute-start.4
  26.1 4.9 %collective-permute-start.5 = (f32[18,8,384]{2,1,0:T(8,128)S(1)}, f32[18,8,384]{2,1,0:T(8,128)S(1)}, u32[]{:S(2)}, u32[]{:S(2)}) collective-permute-start(f32[18,8,384]{2,1,0:T(8,128)S(1)} %get-tuple-element.102), channel_id=1, source_target_pairs={{0,120},{8,0},{16,8},{24,16},{32,24},{40,32},{48,40},{56,48},{64,5... | collective-permute-start | bytes 663560 | tf_op jit(solution)/shard_map/ppermute | solution.py:578
  31.0 3.2 %collective-permute-done.4.lo = f32[18,8,384]{2,1,0:T(8,128)S(1)} collective-permute-done((f32[18,8,384]{2,1,0:T(8,128)S(1)}, f32[18,8,384]{2,1,0:T(8,128)S(1)}, u32[]{:S(2)}, u32[]{:S(2)}) %collective-permute-start.4) | collective-permute-done | bytes 221216 | tf_op jit(solution)/shard_map/ppermute | solution.py:581
  34.3 0.0 collective-permute-done.5.hi
  34.4 4.1 %collective-permute-start.7 = (f32[18,8,384]{2,1,0:T(8,128)S(1)}, f32[18,8,384]{2,1,0:T(8,128)S(1)}, u32[]{:S(2)}, u32[]{:S(2)}) collective-permute-start(f32[18,8,384]{2,1,0:T(8,128)S(1)} %get-tuple-element.58), channel_id=1, source_target_pairs={{0,1},{1,2},{2,3},{3,4},{4,5},{5,6},{6,7},{7,0},{8,9},{9,10},{10,1... | collective-permute-start | bytes 663560 | tf_op jit(solution)/shard_map/ppermute | solution.py:575
  38.6 0.4 collective-permute-start.6
  38.9 2.5 %collective-permute-done.7.before = f32[18,8,384]{2,1,0:T(8,128)S(1)} collective-permute-done((f32[18,8,384]{2,1,0:T(8,128)S(1)}, f32[18,8,384]{2,1,0:T(8,128)S(1)}, u32[]{:S(2)}, u32[]{:S(2)}) %collective-permute-start.7) | collective-permute-done | bytes 221216 | tf_op jit(solution)/shard_map/ppermute | solution.py:575
  41.4 2.8 %collective-permute-done.6.after = f32[18,8,384]{2,1,0:T(8,128)S(1)} collective-permute-done((f32[18,8,384]{2,1,0:T(8,128)S(1)}, f32[18,8,384]{2,1,0:T(8,128)S(1)}, u32[]{:S(2)}, u32[]{:S(2)}) %collective-permute-start.6) | collective-permute-done | bytes 221216 | tf_op jit(solution)/shard_map/ppermute | solution.py:572
  44.2 2.5 %shard_map.29 = (f32[3,14,3,8,256]{4,3,2,1,0:T(8,128)S(1)}, f32[14,3,8,256]{3,2,1,0:T(8,128)S(1)}, f32[14,3,8,256]{3,2,1,0:T(8,128)S(1)}, f32[14,3,8,256]{3,2,1,...) custom-call(s32[2]{0:T(128)S(1)} %pad_add_fusion.idx, ...), custom_call_target="tpu_custom_call" | custom-call | flops 10000000 | bytes 5824520 | tf_op jit(solution)/shard_map/pallas_call | solution.py:554
  46.7 0.1 broadcast_in_dim.2
  46.8 25.4 %all_to_all.5 = f32[64,3,8,128]{3,2,1,0:T(8,128)S(1)} all-to-all(f32[64,3,8,128]{3,2,1,0:T(8,128)S(1)} %broadcast_in_dim.2), channel_id=1, replica_groups=mesh['wide'=16,'y'=4,'core'=2] {'wide','y'}, dimensions={0} | all-to-all | bytes 1572864 | tf_op jit(solution)/shard_map/all_to_all | solution.py:625
  72.2 0.0 collective-permute-start.8
  72.2 2.3 %collective-permute-done.8.other = f32[16,96,128]{2,1,0:T(8,128)S(1)} collective-permute-done((f32[16,96,128]{2,1,0:T(8,128)S(1)}, f32[16,96,128]{2,1,0:T(8,128)S(1)}, u32[]{:S(2)}, u32[]{:S(2)}) %collective-permute-start.8) | collective-permute-done | bytes 786464 | tf_op jit(solution)/shard_map/ppermute | solution.py:626
  74.5 13.3 %shard_map.30 = f32[3,8,16,384]{3,2,1,0:T(8,128)} custom-call(s32[2]{0:T(128)S(1)} %pad_add_fusion.idx, f32[16,96,128]{2,1,0:T(8,128)S(1)} %bitcast.14, f32[16,96,128]{2,1,0:T(8,128)S(1)} %collective-permute-done.8.other, f32[18,8,384]{2,1,0:T(8,128)S(1)} %collective-permute-done.4.lo, f32[18,8,384]{2,1,0:T(8,128)S(1)} %collective-permute-done.5.hi, ...), custom_call_target="tpu_custom_call" | custom-call | flops 100000000 | bytes 15163400 | tf_op jit(solution)/shard_map/pallas_call | solution.py:554
  (27 shorter events, 0.5 us)
Async XLA Ops:
  0.0 9.1 %copy-start = (f32[3,8,16,384]{3,2,1,0:T(8,128)S(1)}, f32[3,8,16,384]{3,2,1,0:T(8,128)}, u32[]{:S(2)}) copy-start(f32[3,8,16,384]{3,2,1,0:T(8,128)} %load) | copy-start | bytes 1769476
  2.1 12.3 %copy-start.1 = (f32[8,16,384]{2,1,0:T(8,128)S(1)}, f32[8,16,384]{2,1,0:T(8,128)}, u32[]{:S(2)}) copy-start(f32[8,16,384]{2,1,0:T(8,128)} %dens) | copy-start | bytes 589828
  2.1 12.0 %collective-permute-start = (f32[9,16,384]{2,1,0:T(8,128)S(1)}, f32[9,16,384]{2,1,0:T(8,128)S(1)}, u32[]{:S(2)}, u32[]{:S(2)}) collective-permute-start(f32[9,16,384]{2,1,0:T(8,128)S(1)} %pad_maximum_fusion.3), channel_id=1, source_target_pairs={{0,8},{8,16},{16,24},{24,32},{32,40},{40,48},{48,56},{56,64},{64,7... | collective-permute-start | bytes 663560 | tf_op jit(solution)/shard_map/ppermute | solution.py:581
  4.2 9.9 %collective-permute-start.1 = (f32[9,16,384]{2,1,0:T(8,128)S(1)}, f32[9,16,384]{2,1,0:T(8,128)S(1)}, u32[]{:S(2)}, u32[]{:S(2)}) collective-permute-start(f32[9,16,384]{2,1,0:T(8,128)S(1)} %pad_maximum_fusion.4), channel_id=1, source_target_pairs={{0,120},{8,0},{16,8},{24,16},{32,24},{40,32},{48,40},{56,48},{64,5... | collective-permute-start | bytes 663560 | tf_op jit(solution)/shard_map/ppermute | solution.py:578
  14.4 7.3 %collective-permute-start.2 = (f32[50,4,384]{2,1,0:T(4,128)S(1)}, f32[50,4,384]{2,1,0:T(4,128)S(1)}, u32[]{:S(2)}, u32[]{:S(2)}) collective-permute-start(f32[50,4,384]{2,1,0:T(4,128)S(1)} %get-tuple-element.70), channel_id=1, source_target_pairs={{0,7},{1,0},{2,1},{3,2},{4,3},{5,4},{6,5},{7,6},{8,15},{9,8},{10,9... | collective-permute-start | bytes 921608 | tf_op jit(solution)/shard_map/ppermute | solution.py:572
  15.7 6.0 %collective-permute-start.3 = (f32[50,4,384]{2,1,0:T(4,128)S(1)}, f32[50,4,384]{2,1,0:T(4,128)S(1)}, u32[]{:S(2)}, u32[]{:S(2)}) collective-permute-start(f32[50,4,384]{2,1,0:T(4,128)S(1)} %get-tuple-element.71), channel_id=1, source_target_pairs={{0,1},{1,2},{2,3},{3,4},{4,5},{5,6},{6,7},{7,0},{8,9},{9,10},{10,1... | collective-permute-start | bytes 921608 | tf_op jit(solution)/shard_map/ppermute | solution.py:575
  26.0 8.2 %collective-permute-start.4 = (f32[18,8,384]{2,1,0:T(8,128)S(1)}, f32[18,8,384]{2,1,0:T(8,128)S(1)}, u32[]{:S(2)}, u32[]{:S(2)}) collective-permute-start(f32[18,8,384]{2,1,0:T(8,128)S(1)} %get-tuple-element.103), channel_id=1, source_target_pairs={{0,8},{8,16},{16,24},{24,32},{32,40},{40,48},{48,56},{56,64},{64,7... | collective-permute-start | bytes 663560 | tf_op jit(solution)/shard_map/ppermute | solution.py:581
  26.1 8.2 %collective-permute-start.5 = (f32[18,8,384]{2,1,0:T(8,128)S(1)}, f32[18,8,384]{2,1,0:T(8,128)S(1)}, u32[]{:S(2)}, u32[]{:S(2)}) collective-permute-start(f32[18,8,384]{2,1,0:T(8,128)S(1)} %get-tuple-element.102), channel_id=1, source_target_pairs={{0,120},{8,0},{16,8},{24,16},{32,24},{40,32},{48,40},{56,48},{64,5... | collective-permute-start | bytes 663560 | tf_op jit(solution)/shard_map/ppermute | solution.py:578
  34.4 7.0 %collective-permute-start.7 = (f32[18,8,384]{2,1,0:T(8,128)S(1)}, f32[18,8,384]{2,1,0:T(8,128)S(1)}, u32[]{:S(2)}, u32[]{:S(2)}) collective-permute-start(f32[18,8,384]{2,1,0:T(8,128)S(1)} %get-tuple-element.58), channel_id=1, source_target_pairs={{0,1},{1,2},{2,3},{3,4},{4,5},{5,6},{6,7},{7,0},{8,9},{9,10},{10,1... | collective-permute-start | bytes 663560 | tf_op jit(solution)/shard_map/ppermute | solution.py:575
  38.6 5.7 %collective-permute-start.6 = (f32[18,8,384]{2,1,0:T(8,128)S(1)}, f32[18,8,384]{2,1,0:T(8,128)S(1)}, u32[]{:S(2)}, u32[]{:S(2)}) collective-permute-start(f32[18,8,384]{2,1,0:T(8,128)S(1)} %get-tuple-element.59), channel_id=1, source_target_pairs={{0,7},{1,0},{2,1},{3,2},{4,3},{5,4},{6,5},{7,6},{8,15},{9,8},{10,9... | collective-permute-start | bytes 663560 | tf_op jit(solution)/shard_map/ppermute | solution.py:572
  72.2 2.3 %collective-permute-start.8 = (f32[16,96,128]{2,1,0:T(8,128)S(1)}, f32[16,96,128]{2,1,0:T(8,128)S(1)}, u32[]{:S(2)}, u32[]{:S(2)}) collective-permute-start(f32[16,96,128]{2,1,0:T(8,128)S(1)} %bitcast.13), channel_id=1, source_target_pairs={{0,1},{1,0},{2,3},{3,2},{4,5},{5,4},{6,7},{7,6},{8,9},{9,8},{10,11... | collective-permute-start | bytes 2359304 | tf_op jit(solution)/shard_map/ppermute | solution.py:626

commit v7 on v6

--- a/solution.py
+++ b/solution.py
@@ -37,8 +37,8 @@
 def times01(v, matrix):
     high = v.astype(BF16)
     rest = (v - high.astype(F32)).astype(BF16)
-    out = jnp.dot(high, matrix, preferred_element_type=F32)
-    return out + jnp.dot(rest, matrix, preferred_element_type=F32)
+    both = jnp.concatenate([high, rest], axis=1)
+    return jnp.dot(both, jnp.concatenate([matrix, matrix], axis=0), preferred_element_type=F32)
 
 
 def pair_sum_matrix(fine, coarse, start, factor):

time: 88 us -> 87.7 us (level)
  no operation moved by 1% of the time
where the time goes in v7:
time: 87.7 us; the launch traced here: 87.6 us
  blocking collectives  25.4 us (29%)
  waiting for transfers between devices  20.6 us (23%)
  Pallas kernels  19.7 us (22%)
  starting transfers between devices  18.9 us (22%)
  local copies, waits for them, and re-layouts  2.39 us (3%)
    all_to_all x1, blocking collectives, shards(): mine = lax.all_to_all(chunks, ('wide', 'y'), 0, 0).reshape(16, 96, 128)  25.4 us
    pallas_call x3, Pallas kernels, call(): pl.pallas_call(kernel, out_shape=[jax.ShapeDtypeStruct(s, F32) for s in o...  19.7 us
    ppermute x2, starting transfers between devices, above(): return lax.ppermute(v, 'wide', cyclic(16, -steps))  9.73 us
    ppermute x2, waiting for transfers between devices, below(): return lax.ppermute(v, 'wide', cyclic(16, steps))  8.2 us
    ppermute x2, waiting for transfers between devices, next_rows(): return lax.ppermute(v, NARROW, cyclic(8, -1))  7.58 us
    ppermute x2, starting transfers between devices, previous_rows(): return lax.ppermute(v, NARROW, cyclic(8, 1))  5.35 us
    ppermute x2, waiting for transfers between devices, previous_rows(): return lax.ppermute(v, NARROW, cyclic(8, 1))  2.52 us
    ppermute x1, waiting for transfers between devices, shards(): other = lax.ppermute(mine, 'core', cyclic(2, 1))  2.28 us
  transfers between devices with their start and end apart: 9, of which 6 were waited for; matrix products, arithmetic and copies ran while one was open for 0% of the time, Pallas kernels for 0%

profile of v7, /device:TPU:1, one launch (start us, length us, event | category | flops | bytes accessed | tf_op | source)
XLA Modules:
  0.0 87.6 jit_solution(7637927448776093887)
XLA Ops:
  0.0 0.0 copy-start
  0.0 0.1 pad_add_fusion.idx
  0.1 1.0 %fusion.3 = (f32[3,16,384]{2,1,0:T(8,128)S(1)}, f32[3,16,384]{2,1,0:T(8,128)S(1)}) fusion(f32[8,16,384]{2,1,0:T(8,128)} %dens), kind=kLoop, calls=%fused_computation.48 | loop fusion | bytes 294912 | tf_op jit(solution)/shard_map/slice | solution.py:584
  1.1 1.0 %fusion = (f32[3,2,16,384]{3,2,1,0:T(8,128)S(1)}, f32[3,2,16,384]{3,2,1,0:T(8,128)S(1)}) fusion(f32[3,8,16,384]{3,2,1,0:T(8,128)} %load), kind=kLoop, calls=%fused_computation.45 | loop fusion | bytes 589824 | tf_op jit(solution)/shard_map/slice | solution.py:584
  2.1 0.0 copy-start.1
  2.1 2.1 %collective-permute-start = (f32[9,16,384]{2,1,0:T(8,128)S(1)}, f32[9,16,384]{2,1,0:T(8,128)S(1)}, u32[]{:S(2)}, u32[]{:S(2)}) collective-permute-start(f32[9,16,384]{2,1,0:T(8,128)S(1)} %pad_maximum_fusion.3), channel_id=1, source_target_pairs={{0,8},{8,16},{16,24},{24,32},{32,40},{40,48},{48,56},{56,64},{64,7... | collective-permute-start | bytes 663560 | tf_op jit(solution)/shard_map/ppermute | solution.py:581
  4.2 4.8 %collective-permute-start.1 = (f32[9,16,384]{2,1,0:T(8,128)S(1)}, f32[9,16,384]{2,1,0:T(8,128)S(1)}, u32[]{:S(2)}, u32[]{:S(2)}) collective-permute-start(f32[9,16,384]{2,1,0:T(8,128)S(1)} %pad_maximum_fusion.4), channel_id=1, source_target_pairs={{0,120},{8,0},{16,8},{24,16},{32,24},{40,32},{48,40},{56,48},{64,5... | collective-permute-start | bytes 663560 | tf_op jit(solution)/shard_map/ppermute | solution.py:578
  9.1 0.0 copy-done
  9.1 5.0 %collective-permute-done.lo = f32[9,16,384]{2,1,0:T(8,128)S(1)} collective-permute-done((f32[9,16,384]{2,1,0:T(8,128)S(1)}, f32[9,16,384]{2,1,0:T(8,128)S(1)}, u32[]{:S(2)}, u32[]{:S(2)}) %collective-permute-start) | collective-permute-done | bytes 221216 | tf_op jit(solution)/shard_map/ppermute | solution.py:581
  14.2 0.0 collective-permute-done.1.hi
  14.4 0.0 copy-done.1
  14.4 1.2 %collective-permute-start.2 = (f32[50,4,384]{2,1,0:T(4,128)S(1)}, f32[50,4,384]{2,1,0:T(4,128)S(1)}, u32[]{:S(2)}, u32[]{:S(2)}) collective-permute-start(f32[50,4,384]{2,1,0:T(4,128)S(1)} %get-tuple-element.70), channel_id=1, source_target_pairs={{0,7},{1,0},{2,1},{3,2},{4,3},{5,4},{6,5},{7,6},{8,15},{9,8},{10,9... | collective-permute-start | bytes 921608 | tf_op jit(solution)/shard_map/ppermute | solution.py:572
  15.7 1.2 %collective-permute-start.3 = (f32[50,4,384]{2,1,0:T(4,128)S(1)}, f32[50,4,384]{2,1,0:T(4,128)S(1)}, u32[]{:S(2)}, u32[]{:S(2)}) collective-permute-start(f32[50,4,384]{2,1,0:T(4,128)S(1)} %get-tuple-element.71), channel_id=1, source_target_pairs={{0,1},{1,2},{2,3},{3,4},{4,5},{5,6},{6,7},{7,0},{8,9},{9,10},{10,1... | collective-permute-start | bytes 921608 | tf_op jit(solution)/shard_map/ppermute | solution.py:575
  16.9 4.8 %collective-permute-done.2 = f32[50,4,384]{2,1,0:T(4,128)S(1)} collective-permute-done((f32[50,4,384]{2,1,0:T(4,128)S(1)}, f32[50,4,384]{2,1,0:T(4,128)S(1)}, u32[]{:S(2)}, u32[]{:S(2)}) %collective-permute-start.2) | collective-permute-done | bytes 307232 | tf_op jit(solution)/shard_map/ppermute | solution.py:572
  21.7 0.0 collective-permute-done.3
  21.7 0.1 pad_maximum_fusion.rows
  21.8 4.1 %shard_map.28 = (f32[3,14,3,8,384]{4,3,2,1,0:T(8,128)S(1)}, f32[14,3,8,384]{3,2,1,0:T(8,128)S(1)}, f32[14,3,8,384]{3,2,1,0:T(8,128)S(1)}, f32[14,3,8,384]{3,2,1,...) custom-call(s32[2]{0:T(128)S(1)} %pad_add_fusion.idx, ...), custom_call_target="tpu_custom_call" | custom-call | flops 10000000 | bytes 9916424 | tf_op jit(solution)/shard_map/pallas_call | solution.py:554
  26.0 0.1 collective-permute-start.4
  26.1 4.9 %collective-permute-start.5 = (f32[18,8,384]{2,1,0:T(8,128)S(1)}, f32[18,8,384]{2,1,0:T(8,128)S(1)}, u32[]{:S(2)}, u32[]{:S(2)}) collective-permute-start(f32[18,8,384]{2,1,0:T(8,128)S(1)} %get-tuple-element.102), channel_id=1, source_target_pairs={{0,120},{8,0},{16,8},{24,16},{32,24},{40,32},{48,40},{56,48},{64,5... | collective-permute-start | bytes 663560 | tf_op jit(solution)/shard_map/ppermute | solution.py:578
  31.0 3.2 %collective-permute-done.4.lo = f32[18,8,384]{2,1,0:T(8,128)S(1)} collective-permute-done((f32[18,8,384]{2,1,0:T(8,128)S(1)}, f32[18,8,384]{2,1,0:T(8,128)S(1)}, u32[]{:S(2)}, u32[]{:S(2)}) %collective-permute-start.4) | collective-permute-done | bytes 221216 | tf_op jit(solution)/shard_map/ppermute | solution.py:581
  34.2 0.0 collective-permute-done.5.hi
  34.4 4.1 %collective-permute-start.7 = (f32[18,8,384]{2,1,0:T(8,128)S(1)}, f32[18,8,384]{2,1,0:T(8,128)S(1)}, u32[]{:S(2)}, u32[]{:S(2)}) collective-permute-start(f32[18,8,384]{2,1,0:T(8,128)S(1)} %get-tuple-element.58), channel_id=1, source_target_pairs={{0,1},{1,2},{2,3},{3,4},{4,5},{5,6},{6,7},{7,0},{8,9},{9,10},{10,1... | collective-permute-start | bytes 663560 | tf_op jit(solution)/shard_map/ppermute | solution.py:575
  38.5 0.4 collective-permute-start.6
  38.9 2.5 %collective-permute-done.7.before = f32[18,8,384]{2,1,0:T(8,128)S(1)} collective-permute-done((f32[18,8,384]{2,1,0:T(8,128)S(1)}, f32[18,8,384]{2,1,0:T(8,128)S(1)}, u32[]{:S(2)}, u32[]{:S(2)}) %collective-permute-start.7) | collective-permute-done | bytes 221216 | tf_op jit(solution)/shard_map/ppermute | solution.py:575
  41.4 2.8 %collective-permute-done.6.after = f32[18,8,384]{2,1,0:T(8,128)S(1)} collective-permute-done((f32[18,8,384]{2,1,0:T(8,128)S(1)}, f32[18,8,384]{2,1,0:T(8,128)S(1)}, u32[]{:S(2)}, u32[]{:S(2)}) %collective-permute-start.6) | collective-permute-done | bytes 221216 | tf_op jit(solution)/shard_map/ppermute | solution.py:572
  44.2 2.5 %shard_map.29 = (f32[3,14,3,8,256]{4,3,2,1,0:T(8,128)S(1)}, f32[14,3,8,256]{3,2,1,0:T(8,128)S(1)}, f32[14,3,8,256]{3,2,1,0:T(8,128)S(1)}, f32[14,3,8,256]{3,2,1,...) custom-call(s32[2]{0:T(128)S(1)} %pad_add_fusion.idx, ...), custom_call_target="tpu_custom_call" | custom-call | flops 10000000 | bytes 5824520 | tf_op jit(solution)/shard_map/pallas_call | solution.py:554
  46.7 0.1 broadcast_in_dim.2
  46.7 25.4 %all_to_all.5 = f32[64,3,8,128]{3,2,1,0:T(8,128)S(1)} all-to-all(f32[64,3,8,128]{3,2,1,0:T(8,128)S(1)} %broadcast_in_dim.2), channel_id=1, replica_groups=mesh['wide'=16,'y'=4,'core'=2] {'wide','y'}, dimensions={0} | all-to-all | bytes 1572864 | tf_op jit(solution)/shard_map/all_to_all | solution.py:625
  72.2 0.0 collective-permute-start.8
  72.2 2.3 %collective-permute-done.8.other = f32[16,96,128]{2,1,0:T(8,128)S(1)} collective-permute-done((f32[16,96,128]{2,1,0:T(8,128)S(1)}, f32[16,96,128]{2,1,0:T(8,128)S(1)}, u32[]{:S(2)}, u32[]{:S(2)}) %collective-permute-start.8) | collective-permute-done | bytes 786464 | tf_op jit(solution)/shard_map/ppermute | solution.py:626
  74.5 13.1 %shard_map.30 = f32[3,8,16,384]{3,2,1,0:T(8,128)} custom-call(s32[2]{0:T(128)S(1)} %pad_add_fusion.idx, f32[16,96,128]{2,1,0:T(8,128)S(1)} %bitcast.14, f32[16,96,128]{2,1,0:T(8,128)S(1)} %collective-permute-done.8.other, f32[18,8,384]{2,1,0:T(8,128)S(1)} %collective-permute-done.4.lo, f32[18,8,384]{2,1,0:T(8,128)S(1)} %collective-permute-done.5.hi, ...), custom_call_target="tpu_custom_call" | custom-call | flops 100000000 | bytes 15163400 | tf_op jit(solution)/shard_map/pallas_call | solution.py:554
  (27 shorter events, 0.5 us)
Async XLA Ops:
  0.0 9.1 %copy-start = (f32[3,8,16,384]{3,2,1,0:T(8,128)S(1)}, f32[3,8,16,384]{3,2,1,0:T(8,128)}, u32[]{:S(2)}) copy-start(f32[3,8,16,384]{3,2,1,0:T(8,128)} %load) | copy-start | bytes 1769476
  2.1 12.3 %copy-start.1 = (f32[8,16,384]{2,1,0:T(8,128)S(1)}, f32[8,16,384]{2,1,0:T(8,128)}, u32[]{:S(2)}) copy-start(f32[8,16,384]{2,1,0:T(8,128)} %dens) | copy-start | bytes 589828
  2.1 12.0 %collective-permute-start = (f32[9,16,384]{2,1,0:T(8,128)S(1)}, f32[9,16,384]{2,1,0:T(8,128)S(1)}, u32[]{:S(2)}, u32[]{:S(2)}) collective-permute-start(f32[9,16,384]{2,1,0:T(8,128)S(1)} %pad_maximum_fusion.3), channel_id=1, source_target_pairs={{0,8},{8,16},{16,24},{24,32},{32,40},{40,48},{48,56},{56,64},{64,7... | collective-permute-start | bytes 663560 | tf_op jit(solution)/shard_map/ppermute | solution.py:581
  4.2 9.9 %collective-permute-start.1 = (f32[9,16,384]{2,1,0:T(8,128)S(1)}, f32[9,16,384]{2,1,0:T(8,128)S(1)}, u32[]{:S(2)}, u32[]{:S(2)}) collective-permute-start(f32[9,16,384]{2,1,0:T(8,128)S(1)} %pad_maximum_fusion.4), channel_id=1, source_target_pairs={{0,120},{8,0},{16,8},{24,16},{32,24},{40,32},{48,40},{56,48},{64,5... | collective-permute-start | bytes 663560 | tf_op jit(solution)/shard_map/ppermute | solution.py:578
  14.4 7.3 %collective-permute-start.2 = (f32[50,4,384]{2,1,0:T(4,128)S(1)}, f32[50,4,384]{2,1,0:T(4,128)S(1)}, u32[]{:S(2)}, u32[]{:S(2)}) collective-permute-start(f32[50,4,384]{2,1,0:T(4,128)S(1)} %get-tuple-element.70), channel_id=1, source_target_pairs={{0,7},{1,0},{2,1},{3,2},{4,3},{5,4},{6,5},{7,6},{8,15},{9,8},{10,9... | collective-permute-start | bytes 921608 | tf_op jit(solution)/shard_map/ppermute | solution.py:572
  15.7 6.0 %collective-permute-start.3 = (f32[50,4,384]{2,1,0:T(4,128)S(1)}, f32[50,4,384]{2,1,0:T(4,128)S(1)}, u32[]{:S(2)}, u32[]{:S(2)}) collective-permute-start(f32[50,4,384]{2,1,0:T(4,128)S(1)} %get-tuple-element.71), channel_id=1, source_target_pairs={{0,1},{1,2},{2,3},{3,4},{4,5},{5,6},{6,7},{7,0},{8,9},{9,10},{10,1... | collective-permute-start | bytes 921608 | tf_op jit(solution)/shard_map/ppermute | solution.py:575
  26.0 8.2 %collective-permute-start.4 = (f32[18,8,384]{2,1,0:T(8,128)S(1)}, f32[18,8,384]{2,1,0:T(8,128)S(1)}, u32[]{:S(2)}, u32[]{:S(2)}) collective-permute-start(f32[18,8,384]{2,1,0:T(8,128)S(1)} %get-tuple-element.103), channel_id=1, source_target_pairs={{0,8},{8,16},{16,24},{24,32},{32,40},{40,48},{48,56},{56,64},{64,7... | collective-permute-start | bytes 663560 | tf_op jit(solution)/shard_map/ppermute | solution.py:581
  26.1 8.2 %collective-permute-start.5 = (f32[18,8,384]{2,1,0:T(8,128)S(1)}, f32[18,8,384]{2,1,0:T(8,128)S(1)}, u32[]{:S(2)}, u32[]{:S(2)}) collective-permute-start(f32[18,8,384]{2,1,0:T(8,128)S(1)} %get-tuple-element.102), channel_id=1, source_target_pairs={{0,120},{8,0},{16,8},{24,16},{32,24},{40,32},{48,40},{56,48},{64,5... | collective-permute-start | bytes 663560 | tf_op jit(solution)/shard_map/ppermute | solution.py:578
  34.4 7.0 %collective-permute-start.7 = (f32[18,8,384]{2,1,0:T(8,128)S(1)}, f32[18,8,384]{2,1,0:T(8,128)S(1)}, u32[]{:S(2)}, u32[]{:S(2)}) collective-permute-start(f32[18,8,384]{2,1,0:T(8,128)S(1)} %get-tuple-element.58), channel_id=1, source_target_pairs={{0,1},{1,2},{2,3},{3,4},{4,5},{5,6},{6,7},{7,0},{8,9},{9,10},{10,1... | collective-permute-start | bytes 663560 | tf_op jit(solution)/shard_map/ppermute | solution.py:575
  38.5 5.7 %collective-permute-start.6 = (f32[18,8,384]{2,1,0:T(8,128)S(1)}, f32[18,8,384]{2,1,0:T(8,128)S(1)}, u32[]{:S(2)}, u32[]{:S(2)}) collective-permute-start(f32[18,8,384]{2,1,0:T(8,128)S(1)} %get-tuple-element.59), channel_id=1, source_target_pairs={{0,7},{1,0},{2,1},{3,2},{4,3},{5,4},{6,5},{7,6},{8,15},{9,8},{10,9... | collective-permute-start | bytes 663560 | tf_op jit(solution)/shard_map/ppermute | solution.py:572
  72.2 2.3 %collective-permute-start.8 = (f32[16,96,128]{2,1,0:T(8,128)S(1)}, f32[16,96,128]{2,1,0:T(8,128)S(1)}, u32[]{:S(2)}, u32[]{:S(2)}) collective-permute-start(f32[16,96,128]{2,1,0:T(8,128)S(1)} %bitcast.13), channel_id=1, source_target_pairs={{0,1},{1,0},{2,3},{3,2},{4,5},{5,4},{6,7},{7,6},{8,9},{9,8},{10,11... | collective-permute-start | bytes 2359304 | tf_op jit(solution)/shard_map/ppermute | solution.py:626

commit v8 on v7

--- a/solution.py
+++ b/solution.py
@@ -435,7 +435,7 @@
         rho2[z] = d
         return 0
 
-    lax.fori_loop(4, 36, split, 0, unroll=4)
+    lax.fori_loop(4, 36, split, 0, unroll=16)
 
     level2 = Level(4, 128, False, True, gx2, gxm2, gy2, gz2, m2, w2, ms2)
 

time: 87.7 us -> 87.3 us (level)
  no operation moved by 1% of the time
where the time goes in v8:
time: 87.3 us; the launch traced here: 87.2 us
  blocking collectives  25.4 us (29%)
  waiting for transfers between devices  20.6 us (24%)
  Pallas kernels  19.3 us (22%)
  starting transfers between devices  18.9 us (22%)
  local copies, waits for them, and re-layouts  2.39 us (3%)
    all_to_all x1, blocking collectives, shards(): mine = lax.all_to_all(chunks, ('wide', 'y'), 0, 0).reshape(16, 96, 128)  25.4 us
    pallas_call x3, Pallas kernels, call(): pl.pallas_call(kernel, out_shape=[jax.ShapeDtypeStruct(s, F32) for s in o...  19.3 us
    ppermute x2, starting transfers between devices, above(): return lax.ppermute(v, 'wide', cyclic(16, -steps))  9.73 us
    ppermute x2, waiting for transfers between devices, below(): return lax.ppermute(v, 'wide', cyclic(16, steps))  8.2 us
    ppermute x2, waiting for transfers between devices, next_rows(): return lax.ppermute(v, NARROW, cyclic(8, -1))  7.58 us
    ppermute x2, starting transfers between devices, previous_rows(): return lax.ppermute(v, NARROW, cyclic(8, 1))  5.35 us
    ppermute x2, waiting for transfers between devices, previous_rows(): return lax.ppermute(v, NARROW, cyclic(8, 1))  2.52 us
    ppermute x1, waiting for transfers between devices, shards(): other = lax.ppermute(mine, 'core', cyclic(2, 1))  2.28 us
  transfers between devices with their start and end apart: 9, of which 6 were waited for; matrix products, arithmetic and copies ran while one was open for 0% of the time, Pallas kernels for 0%

profile of v8, /device:TPU:1, one launch (start us, length us, event | category | flops | bytes accessed | tf_op | source)
XLA Modules:
  0.0 87.2 jit_solution(17778714777628063571)
XLA Ops:
  0.0 0.0 copy-start
  0.0 0.1 pad_add_fusion.idx
  0.1 1.0 %fusion.3 = (f32[3,16,384]{2,1,0:T(8,128)S(1)}, f32[3,16,384]{2,1,0:T(8,128)S(1)}) fusion(f32[8,16,384]{2,1,0:T(8,128)} %dens), kind=kLoop, calls=%fused_computation.48 | loop fusion | bytes 294912 | tf_op jit(solution)/shard_map/slice | solution.py:584
  1.1 1.0 %fusion = (f32[3,2,16,384]{3,2,1,0:T(8,128)S(1)}, f32[3,2,16,384]{3,2,1,0:T(8,128)S(1)}) fusion(f32[3,8,16,384]{3,2,1,0:T(8,128)} %load), kind=kLoop, calls=%fused_computation.45 | loop fusion | bytes 589824 | tf_op jit(solution)/shard_map/slice | solution.py:584
  2.1 0.0 copy-start.1
  2.1 2.1 %collective-permute-start = (f32[9,16,384]{2,1,0:T(8,128)S(1)}, f32[9,16,384]{2,1,0:T(8,128)S(1)}, u32[]{:S(2)}, u32[]{:S(2)}) collective-permute-start(f32[9,16,384]{2,1,0:T(8,128)S(1)} %pad_maximum_fusion.3), channel_id=1, source_target_pairs={{0,8},{8,16},{16,24},{24,32},{32,40},{40,48},{48,56},{56,64},{64,7... | collective-permute-start | bytes 663560 | tf_op jit(solution)/shard_map/ppermute | solution.py:581
  4.2 4.8 %collective-permute-start.1 = (f32[9,16,384]{2,1,0:T(8,128)S(1)}, f32[9,16,384]{2,1,0:T(8,128)S(1)}, u32[]{:S(2)}, u32[]{:S(2)}) collective-permute-start(f32[9,16,384]{2,1,0:T(8,128)S(1)} %pad_maximum_fusion.4), channel_id=1, source_target_pairs={{0,120},{8,0},{16,8},{24,16},{32,24},{40,32},{48,40},{56,48},{64,5... | collective-permute-start | bytes 663560 | tf_op jit(solution)/shard_map/ppermute | solution.py:578
  9.1 0.0 copy-done
  9.1 5.0 %collective-permute-done.lo = f32[9,16,384]{2,1,0:T(8,128)S(1)} collective-permute-done((f32[9,16,384]{2,1,0:T(8,128)S(1)}, f32[9,16,384]{2,1,0:T(8,128)S(1)}, u32[]{:S(2)}, u32[]{:S(2)}) %collective-permute-start) | collective-permute-done | bytes 221216 | tf_op jit(solution)/shard_map/ppermute | solution.py:581
  14.2 0.0 collective-permute-done.1.hi
  14.4 0.0 copy-done.1
  14.4 1.2 %collective-permute-start.2 = (f32[50,4,384]{2,1,0:T(4,128)S(1)}, f32[50,4,384]{2,1,0:T(4,128)S(1)}, u32[]{:S(2)}, u32[]{:S(2)}) collective-permute-start(f32[50,4,384]{2,1,0:T(4,128)S(1)} %get-tuple-element.70), channel_id=1, source_target_pairs={{0,7},{1,0},{2,1},{3,2},{4,3},{5,4},{6,5},{7,6},{8,15},{9,8},{10,9... | collective-permute-start | bytes 921608 | tf_op jit(solution)/shard_map/ppermute | solution.py:572
  15.7 1.2 %collective-permute-start.3 = (f32[50,4,384]{2,1,0:T(4,128)S(1)}, f32[50,4,384]{2,1,0:T(4,128)S(1)}, u32[]{:S(2)}, u32[]{:S(2)}) collective-permute-start(f32[50,4,384]{2,1,0:T(4,128)S(1)} %get-tuple-element.71), channel_id=1, source_target_pairs={{0,1},{1,2},{2,3},{3,4},{4,5},{5,6},{6,7},{7,0},{8,9},{9,10},{10,1... | collective-permute-start | bytes 921608 | tf_op jit(solution)/shard_map/ppermute | solution.py:575
  16.9 4.8 %collective-permute-done.2 = f32[50,4,384]{2,1,0:T(4,128)S(1)} collective-permute-done((f32[50,4,384]{2,1,0:T(4,128)S(1)}, f32[50,4,384]{2,1,0:T(4,128)S(1)}, u32[]{:S(2)}, u32[]{:S(2)}) %collective-permute-start.2) | collective-permute-done | bytes 307232 | tf_op jit(solution)/shard_map/ppermute | solution.py:572
  21.7 0.0 collective-permute-done.3
  21.7 0.1 pad_maximum_fusion.rows
  21.8 4.1 %shard_map.28 = (f32[3,14,3,8,384]{4,3,2,1,0:T(8,128)S(1)}, f32[14,3,8,384]{3,2,1,0:T(8,128)S(1)}, f32[14,3,8,384]{3,2,1,0:T(8,128)S(1)}, f32[14,3,8,384]{3,2,1,...) custom-call(s32[2]{0:T(128)S(1)} %pad_add_fusion.idx, ...), custom_call_target="tpu_custom_call" | custom-call | flops 10000000 | bytes 9916424 | tf_op jit(solution)/shard_map/pallas_call | solution.py:554
  26.0 0.1 collective-permute-start.4
  26.1 4.9 %collective-permute-start.5 = (f32[18,8,384]{2,1,0:T(8,128)S(1)}, f32[18,8,384]{2,1,0:T(8,128)S(1)}, u32[]{:S(2)}, u32[]{:S(2)}) collective-permute-start(f32[18,8,384]{2,1,0:T(8,128)S(1)} %get-tuple-element.102), channel_id=1, source_target_pairs={{0,120},{8,0},{16,8},{24,16},{32,24},{40,32},{48,40},{56,48},{64,5... | collective-permute-start | bytes 663560 | tf_op jit(solution)/shard_map/ppermute | solution.py:578
  31.0 3.2 %collective-permute-done.4.lo = f32[18,8,384]{2,1,0:T(8,128)S(1)} collective-permute-done((f32[18,8,384]{2,1,0:T(8,128)S(1)}, f32[18,8,384]{2,1,0:T(8,128)S(1)}, u32[]{:S(2)}, u32[]{:S(2)}) %collective-permute-start.4) | collective-permute-done | bytes 221216 | tf_op jit(solution)/shard_map/ppermute | solution.py:581
  34.2 0.0 collective-permute-done.5.hi
  34.4 4.1 %collective-permute-start.7 = (f32[18,8,384]{2,1,0:T(8,128)S(1)}, f32[18,8,384]{2,1,0:T(8,128)S(1)}, u32[]{:S(2)}, u32[]{:S(2)}) collective-permute-start(f32[18,8,384]{2,1,0:T(8,128)S(1)} %get-tuple-element.58), channel_id=1, source_target_pairs={{0,1},{1,2},{2,3},{3,4},{4,5},{5,6},{6,7},{7,0},{8,9},{9,10},{10,1... | collective-permute-start | bytes 663560 | tf_op jit(solution)/shard_map/ppermute | solution.py:575
  38.5 0.4 collective-permute-start.6
  38.9 2.5 %collective-permute-done.7.before = f32[18,8,384]{2,1,0:T(8,128)S(1)} collective-permute-done((f32[18,8,384]{2,1,0:T(8,128)S(1)}, f32[18,8,384]{2,1,0:T(8,128)S(1)}, u32[]{:S(2)}, u32[]{:S(2)}) %collective-permute-start.7) | collective-permute-done | bytes 221216 | tf_op jit(solution)/shard_map/ppermute | solution.py:575
  41.4 2.8 %collective-permute-done.6.after = f32[18,8,384]{2,1,0:T(8,128)S(1)} collective-permute-done((f32[18,8,384]{2,1,0:T(8,128)S(1)}, f32[18,8,384]{2,1,0:T(8,128)S(1)}, u32[]{:S(2)}, u32[]{:S(2)}) %collective-permute-start.6) | collective-permute-done | bytes 221216 | tf_op jit(solution)/shard_map/ppermute | solution.py:572
  44.2 2.5 %shard_map.29 = (f32[3,14,3,8,256]{4,3,2,1,0:T(8,128)S(1)}, f32[14,3,8,256]{3,2,1,0:T(8,128)S(1)}, f32[14,3,8,256]{3,2,1,0:T(8,128)S(1)}, f32[14,3,8,256]{3,2,1,...) custom-call(s32[2]{0:T(128)S(1)} %pad_add_fusion.idx, ...), custom_call_target="tpu_custom_call" | custom-call | flops 10000000 | bytes 5824520 | tf_op jit(solution)/shard_map/pallas_call | solution.py:554
  46.7 0.1 broadcast_in_dim.2
  46.7 25.4 %all_to_all.5 = f32[64,3,8,128]{3,2,1,0:T(8,128)S(1)} all-to-all(f32[64,3,8,128]{3,2,1,0:T(8,128)S(1)} %broadcast_in_dim.2), channel_id=1, replica_groups=mesh['wide'=16,'y'=4,'core'=2] {'wide','y'}, dimensions={0} | all-to-all | bytes 1572864 | tf_op jit(solution)/shard_map/all_to_all | solution.py:625
  72.2 0.0 collective-permute-start.8
  72.2 2.3 %collective-permute-done.8.other = f32[16,96,128]{2,1,0:T(8,128)S(1)} collective-permute-done((f32[16,96,128]{2,1,0:T(8,128)S(1)}, f32[16,96,128]{2,1,0:T(8,128)S(1)}, u32[]{:S(2)}, u32[]{:S(2)}) %collective-permute-start.8) | collective-permute-done | bytes 786464 | tf_op jit(solution)/shard_map/ppermute | solution.py:626
  74.5 12.7 %shard_map.30 = f32[3,8,16,384]{3,2,1,0:T(8,128)} custom-call(s32[2]{0:T(128)S(1)} %pad_add_fusion.idx, f32[16,96,128]{2,1,0:T(8,128)S(1)} %bitcast.14, f32[16,96,128]{2,1,0:T(8,128)S(1)} %collective-permute-done.8.other, f32[18,8,384]{2,1,0:T(8,128)S(1)} %collective-permute-done.4.lo, f32[18,8,384]{2,1,0:T(8,128)S(1)} %collective-permute-done.5.hi, ...), custom_call_target="tpu_custom_call" | custom-call | flops 100000000 | bytes 15163400 | tf_op jit(solution)/shard_map/pallas_call | solution.py:554
  (27 shorter events, 0.5 us)
Async XLA Ops:
  0.0 9.1 %copy-start = (f32[3,8,16,384]{3,2,1,0:T(8,128)S(1)}, f32[3,8,16,384]{3,2,1,0:T(8,128)}, u32[]{:S(2)}) copy-start(f32[3,8,16,384]{3,2,1,0:T(8,128)} %load) | copy-start | bytes 1769476
  2.1 12.3 %copy-start.1 = (f32[8,16,384]{2,1,0:T(8,128)S(1)}, f32[8,16,384]{2,1,0:T(8,128)}, u32[]{:S(2)}) copy-start(f32[8,16,384]{2,1,0:T(8,128)} %dens) | copy-start | bytes 589828
  2.1 12.0 %collective-permute-start = (f32[9,16,384]{2,1,0:T(8,128)S(1)}, f32[9,16,384]{2,1,0:T(8,128)S(1)}, u32[]{:S(2)}, u32[]{:S(2)}) collective-permute-start(f32[9,16,384]{2,1,0:T(8,128)S(1)} %pad_maximum_fusion.3), channel_id=1, source_target_pairs={{0,8},{8,16},{16,24},{24,32},{32,40},{40,48},{48,56},{56,64},{64,7... | collective-permute-start | bytes 663560 | tf_op jit(solution)/shard_map/ppermute | solution.py:581
  4.2 9.9 %collective-permute-start.1 = (f32[9,16,384]{2,1,0:T(8,128)S(1)}, f32[9,16,384]{2,1,0:T(8,128)S(1)}, u32[]{:S(2)}, u32[]{:S(2)}) collective-permute-start(f32[9,16,384]{2,1,0:T(8,128)S(1)} %pad_maximum_fusion.4), channel_id=1, source_target_pairs={{0,120},{8,0},{16,8},{24,16},{32,24},{40,32},{48,40},{56,48},{64,5... | collective-permute-start | bytes 663560 | tf_op jit(solution)/shard_map/ppermute | solution.py:578
  14.4 7.3 %collective-permute-start.2 = (f32[50,4,384]{2,1,0:T(4,128)S(1)}, f32[50,4,384]{2,1,0:T(4,128)S(1)}, u32[]{:S(2)}, u32[]{:S(2)}) collective-permute-start(f32[50,4,384]{2,1,0:T(4,128)S(1)} %get-tuple-element.70), channel_id=1, source_target_pairs={{0,7},{1,0},{2,1},{3,2},{4,3},{5,4},{6,5},{7,6},{8,15},{9,8},{10,9... | collective-permute-start | bytes 921608 | tf_op jit(solution)/shard_map/ppermute | solution.py:572
  15.7 6.0 %collective-permute-start.3 = (f32[50,4,384]{2,1,0:T(4,128)S(1)}, f32[50,4,384]{2,1,0:T(4,128)S(1)}, u32[]{:S(2)}, u32[]{:S(2)}) collective-permute-start(f32[50,4,384]{2,1,0:T(4,128)S(1)} %get-tuple-element.71), channel_id=1, source_target_pairs={{0,1},{1,2},{2,3},{3,4},{4,5},{5,6},{6,7},{7,0},{8,9},{9,10},{10,1... | collective-permute-start | bytes 921608 | tf_op jit(solution)/shard_map/ppermute | solution.py:575
  26.0 8.2 %collective-permute-start.4 = (f32[18,8,384]{2,1,0:T(8,128)S(1)}, f32[18,8,384]{2,1,0:T(8,128)S(1)}, u32[]{:S(2)}, u32[]{:S(2)}) collective-permute-start(f32[18,8,384]{2,1,0:T(8,128)S(1)} %get-tuple-element.103), channel_id=1, source_target_pairs={{0,8},{8,16},{16,24},{24,32},{32,40},{40,48},{48,56},{56,64},{64,7... | collective-permute-start | bytes 663560 | tf_op jit(solution)/shard_map/ppermute | solution.py:581
  26.1 8.2 %collective-permute-start.5 = (f32[18,8,384]{2,1,0:T(8,128)S(1)}, f32[18,8,384]{2,1,0:T(8,128)S(1)}, u32[]{:S(2)}, u32[]{:S(2)}) collective-permute-start(f32[18,8,384]{2,1,0:T(8,128)S(1)} %get-tuple-element.102), channel_id=1, source_target_pairs={{0,120},{8,0},{16,8},{24,16},{32,24},{40,32},{48,40},{56,48},{64,5... | collective-permute-start | bytes 663560 | tf_op jit(solution)/shard_map/ppermute | solution.py:578
  34.4 7.0 %collective-permute-start.7 = (f32[18,8,384]{2,1,0:T(8,128)S(1)}, f32[18,8,384]{2,1,0:T(8,128)S(1)}, u32[]{:S(2)}, u32[]{:S(2)}) collective-permute-start(f32[18,8,384]{2,1,0:T(8,128)S(1)} %get-tuple-element.58), channel_id=1, source_target_pairs={{0,1},{1,2},{2,3},{3,4},{4,5},{5,6},{6,7},{7,0},{8,9},{9,10},{10,1... | collective-permute-start | bytes 663560 | tf_op jit(solution)/shard_map/ppermute | solution.py:575
  38.5 5.7 %collective-permute-start.6 = (f32[18,8,384]{2,1,0:T(8,128)S(1)}, f32[18,8,384]{2,1,0:T(8,128)S(1)}, u32[]{:S(2)}, u32[]{:S(2)}) collective-permute-start(f32[18,8,384]{2,1,0:T(8,128)S(1)} %get-tuple-element.59), channel_id=1, source_target_pairs={{0,7},{1,0},{2,1},{3,2},{4,3},{5,4},{6,5},{7,6},{8,15},{9,8},{10,9... | collective-permute-start | bytes 663560 | tf_op jit(solution)/shard_map/ppermute | solution.py:572
  72.2 2.3 %collective-permute-start.8 = (f32[16,96,128]{2,1,0:T(8,128)S(1)}, f32[16,96,128]{2,1,0:T(8,128)S(1)}, u32[]{:S(2)}, u32[]{:S(2)}) collective-permute-start(f32[16,96,128]{2,1,0:T(8,128)S(1)} %bitcast.13), channel_id=1, source_target_pairs={{0,1},{1,0},{2,3},{3,2},{4,5},{5,4},{6,7},{7,6},{8,9},{9,8},{10,11... | collective-permute-start | bytes 2359304 | tf_op jit(solution)/shard_map/ppermute | solution.py:626
